TPU v7x, 32 devices: a whole 2x2x4 slice. The times are simulated.
32 devices in a mesh: seg: 2 (over x), blk: 16 (over z, y, core).
Axes of the slice: x: 2, y: 2, z: 4, core: 2. Of those that a mesh axis runs over, the one named last changes fastest.
Arguments:
- products: bfloat16 [2, 4096, 4096], P('seg', 'blk'), may hold values from -0.09375 to 0.09375
- compat: int32 [2, 16, 16], P('seg', 'blk'), may hold values 0 or 1
- sizes: int32 [2, 16], P('seg', 'blk'), may hold values from 1 to 256, 3072 in all within a row
Outputs:
- orthonormal: bfloat16 [2, 4096, 4096], P('seg', None, 'blk')
- accumulated: float32 [2, 16, 256, 256], P('seg', 'blk')
Inputs may be any that keep to these rules, and one draw needn't show every extreme that they name: Each site's 16 sector sizes sum to 3072 and one of them is exactly 256.
All inputs are finite; a program needn't handle non-finite values. No bound on the sum of `compat` or of `sizes` on one device may be relied on, other than what follows from the above.
Results may differ from a plain program's by a relative error of at most 0.001.
Values may be sent and summed in bfloat16 or wider, within the bound.
No kernel may reach another device: no remote copies, remote signals or barrier semaphores. Data moves between devices by JAX's collectives and lax.ppermute only.
A program may use at most 64 MiB of HBM per device.

v0:
```python
import jax
import jax.numpy as jnp
from jax import lax
from jax.sharding import PartitionSpec as P

B = 256


shift_value = 0.05


def passed_along(x, axis, by):
    length = lax.axis_size(axis)
    pairs = [(i, i + by) for i in range(length) if 0 <= i + by < length]
    return lax.ppermute(x, axis, pairs)


def factor_sector(panel_in, allowed, live_cols):
    total_rows = panel_in.shape[0]
    width_cols = panel_in.shape[1]
    gate_rows = jnp.repeat(
        allowed, total_rows // allowed.shape[0], total_repeat_length=total_rows
    ).astype(jnp.bfloat16)
    masked = panel_in * gate_rows[:, None] * live_cols.astype(jnp.bfloat16)[None, :]
    gram_raw = jnp.dot(masked.T, masked, preferred_element_type=jnp.float32)
    identity = jnp.eye(width_cols, dtype=jnp.float32)
    lower_one = jnp.linalg.cholesky(gram_raw + shift_value * identity)
    half_way = jax.scipy.linalg.solve_triangular(lower_one, gram_raw, lower=True)
    gram_two = (
        jax.scipy.linalg.solve_triangular(lower_one, half_way.T, lower=True)
        + shift_value * identity
    )
    lower_two = jnp.linalg.cholesky(gram_two)
    factor_r = jnp.dot(lower_two.T, lower_one.T, precision=lax.Precision.HIGHEST)
    ortho_t = jax.scipy.linalg.solve_triangular(
        factor_r.T, masked.astype(jnp.float32).T, lower=True
    )
    return (ortho_t.T.astype(jnp.bfloat16), factor_r)


def compose(earlier, later):
    return jnp.einsum("kab,kbc->kac", later, earlier, precision=lax.Precision.HIGHEST)


def local(products, compat, sizes):
    relayed = lax.all_to_all(products, "blk", split_axis=2, concat_axis=1, tiled=True)
    sectors_here = sizes.shape[1]
    total_rows = relayed.shape[1]
    panels = relayed[0].reshape(total_rows, sectors_here, B).transpose(1, 0, 2)
    live = (jnp.arange(B, dtype=jnp.int32)[None, :] < sizes[0][:, None]).astype(jnp.int32)
    ortho, factors = jax.vmap(factor_sector)(panels, compat[0], live)
    ortho_out = ortho.transpose(1, 0, 2).reshape(1, total_rows, sectors_here * B)
    position = lax.axis_index("seg")

    def advance(step_now, prefix_now):
        incoming = passed_along(prefix_now, "seg", 1)
        updated = compose(incoming, factors)
        return jnp.where(position == step_now, updated, prefix_now)

    accumulated = lax.fori_loop(1, lax.axis_size("seg"), advance, factors)
    return (ortho_out, accumulated[None])


def solution(mesh):
    in_specs = (P("seg", "blk", None), P("seg", "blk", None), P("seg", "blk"))
    out_specs = (P("seg", None, "blk"), P("seg", "blk", None, None))
    return jax.shard_map(local, mesh=mesh, in_specs=in_specs, out_specs=out_specs, check_vma=False)
```

profile of v0, /device:TPU:14, one launch (start us, length us, event | category | flops | bytes accessed | tf_op | source)
XLA Modules:
  0.0 237.9 jit_solution(13559791561925963459)
XLA Ops:
  0.6 10.0 %copy.27 = bf16[1,256,4096]{1,0,2:T(2,128)(2,1)} copy(bf16[1,256,4096]{2,1,0:T(8,128)(2,1)} %param.8) | data formatting | bytes 4194304 | tf_op args[0]
  10.7 0.5 broadcast.428
  11.2 21.6 %reduce.16 = bf16[4096,256]{1,0:T(8,128)(2,1)S(1)} reduce(bf16[4096,1,256]{2,1,0:T(2,128)(2,1)} %bitcast.206, bf16[]{:T(256)} %broadcast.428), dimensions={1}, to_apply=%bitcast.168.reduce_sub_computation | reduce | bytes 4194306
  32.8 2.0 reshape.615
  34.9 6.6 %all-to-all-start = ((bf16[16,2,32768]{2,1,0:T(2,128)(2,1)}), bf16[16,2,32768]{2,1,0:T(2,128)(2,1)S(1)}, u32[]{:S(2)}, u32[]{:S(2)}) async-start(bf16[16,2,32768]{2,1,0:T(2,128)(2,1)} %reshape.615), calls=%async_computation | async-start | bytes 4194304 | tf_op jit(solution)/shard_map/all_to_all | solution.py:46
  42.2 0.7 fusion.48
  43.1 10.0 %select_convert_fusion = bf16[4096]{0:T(1024)(128)(2,1)S(1)} fusion(pred[4096]{0:T(1024)(128)(4,1)S(1)} %copy-done.15, pred[4096]{0:T(1024)(128)(4,1)S(1)} %copy-done.14, pred[4096]{0:T(1024)(128)(4,1)S(1)} %copy-done.13, pred[4096]{0:T(1024)(128)(4,1)S(1)} %copy-done.12, pred[4096]{0:T(1024)(128)(4,1)S(1)} %copy-done.11, pred[4096]{0:T(1024)(128)(4,1)S(1)} %copy-done.10, ...), kind=kLoop, calls=%fused_computation.88 | loop fusion | flops 65536 | bytes 69696 | tf_op jit(solution)/shard_map/vmap()/convert_element_type | solution.py:23
  53.2 35.5 %all-to-all-done = bf16[16,2,32768]{2,1,0:T(2,128)(2,1)S(1)} async-done(((bf16[16,2,32768]{2,1,0:T(2,128)(2,1)}), bf16[16,2,32768]{2,1,0:T(2,128)(2,1)S(1)}, u32[]{:S(2)}, u32[]{:S(2)}) %all-to-all-start) | async-done | bytes 2097184 | tf_op jit(solution)/shard_map/all_to_all | solution.py:46
  88.7 6.7 %reshape.616 = bf16[4096,1,256]{2,1,0:T(2,128)(2,1)} reshape(bf16[16,2,32768]{2,1,0:T(2,128)(2,1)S(1)} %all-to-all-done) | data formatting | bytes 4194304
  95.4 2.5 %copy.42 = bf16[1,256,4096]{1,2,0:T(8,128)(2,1)S(1)} copy(bf16[1,256,4096]{1,0,2:T(2,128)(2,1)} %bitcast.207) | data formatting | bytes 4194304
  98.0 0.8 fusion.3
  99.2 11.7 %custom-call.22 = f32[1,128,128]{2,1,0:T(8,128)S(1)} custom-call(f32[1,128,128]{2,1,0:T(8,128)S(1)} %cholesky.191), custom_call_target="Cholesky" | custom-call | tf_op jit(solution)/shard_map/vmap(jit(cholesky))/cholesky | solution.py:27
  110.9 9.8 %custom-call.23 = f32[1,1,128,128]{2,3,1,0:T(8,128)S(1)} custom-call(f32[1,1,128,128]{3,2,1,0:T(8,128)S(1)} %get-tuple-element.100), custom_call_target="InvertDiagBlocksLowerTriangular" | custom-call | tf_op jit(solution)/shard_map/vmap(jit(cholesky))/cholesky | solution.py:27
  121.0 0.3 fusion.12
  121.2 11.7 %custom-call.24 = f32[1,128,128]{2,1,0:T(8,128)S(1)} custom-call(f32[1,128,128]{2,1,0:T(8,128)S(1)} %fusion.12), custom_call_target="Cholesky" | custom-call | tf_op jit(solution)/shard_map/vmap(jit(cholesky))/cholesky | solution.py:27
  133.0 0.6 compare_reduce_fusion.2
  135.1 4.0 %while.12 = (s32[]{:T(128)}, f32[1,256,256]{2,1,0:T(8,128)S(1)}, s32[2,2]{1,0:T(2,128)S(1)}, f32[2,1,128,128]{3,2,1,0:T(8,128)S(1)}, s32[]{:T(128)}) while((s32[]{:T(128)}, f32[1,256,256]{2,1,0:T(8,128)S(1)}, s32[2,2]{1,0:T(2,128)S(1)}, f32[2,1,128,128]{3,2,1,0:T(8,128)S(1)}, s32[]{:T(128)}) %tuple.78), condition=%wide.while_cond.1.clone, body=%wide.while_body.1.clone.sunk | while | flops 2 | bytes 131189 | solution.py:30
  135.1 0.6 fusion.63
  135.7 1.4 bitcast_dynamic-update-slice_fusion.7
  137.1 0.6 fusion.63
  137.7 1.4 bitcast_dynamic-update-slice_fusion.7
  139.1 19.9 %custom-call.26 = f32[1,2,128,128]{2,3,1,0:T(8,128)S(1)} custom-call(f32[1,2,128,128]{3,2,1,0:T(8,128)S(1)} %bitcast.219), custom_call_target="InvertDiagBlocksLowerTriangular" | custom-call | tf_op jit(solution)/shard_map/vmap(jit(_solve_triangular))/triangular_solve | solution.py:30
  159.0 0.3 fusion.30
  159.3 0.3 fusion.9
  159.5 0.3 convolution_bitcast_fusion.3
  159.9 0.3 fusion.29
  160.2 0.4 fusion.11
  160.7 0.3 convolution_bitcast_fusion.1
  161.2 11.7 %custom-call.27 = f32[1,128,128]{2,1,0:T(8,128)S(1)} custom-call(f32[1,128,128]{2,1,0:T(8,128)S(1)} %cholesky.194), custom_call_target="Cholesky" | custom-call | tf_op jit(solution)/shard_map/vmap(jit(cholesky))/cholesky | solution.py:33
  173.0 0.6 compare_reduce_fusion.1
  173.6 9.8 %custom-call.28 = f32[1,1,128,128]{2,3,1,0:T(8,128)S(1)} custom-call(f32[1,1,128,128]{3,2,1,0:T(8,128)S(1)} %get-tuple-element.96), custom_call_target="InvertDiagBlocksLowerTriangular" | custom-call | tf_op jit(solution)/shard_map/vmap(jit(cholesky))/cholesky | solution.py:33
  183.6 0.3 fusion.13
  183.9 11.7 %custom-call.29 = f32[1,128,128]{2,1,0:T(8,128)S(1)} custom-call(f32[1,128,128]{2,1,0:T(8,128)S(1)} %fusion.13), custom_call_target="Cholesky" | custom-call | tf_op jit(solution)/shard_map/vmap(jit(cholesky))/cholesky | solution.py:33
  195.7 0.6 compare_reduce_fusion
  197.6 0.8 bitcast_select_fusion
  198.4 4.2 %while.11 = (s32[]{:T(128)}, f32[1,256,256]{1,2,0:T(8,128)S(1)}, s32[2,2]{1,0:T(2,128)S(1)}, f32[2,1,128,128]{3,2,1,0:T(8,128)S(1)}, s32[]{:T(128)}) while((s32[]{:T(128)}, f32[1,256,256]{1,2,0:T(8,128)S(1)}, s32[2,2]{1,0:T(2,128)S(1)}, f32[2,1,128,128]{3,2,1,0:T(8,128)S(1)}, s32[]{:T(128)}) %tuple.84), condition=%wide.while_cond.2, body=%wide.while_body.2.sunk | while | flops 2 | bytes 393333 | solution.py:35
  198.4 0.6 fusion.62
  199.0 1.4 constant_dynamic-slice_fusion.7
  200.5 0.6 fusion.62
  201.1 1.4 constant_dynamic-slice_fusion.7
  202.6 19.7 %custom-call.17 = f32[1,2,128,128]{2,3,1,0:T(8,128)S(1)} custom-call(f32[1,2,128,128]{3,2,1,0:T(8,128)S(1)} %bitcast.218), custom_call_target="InvertDiagBlocksLowerTriangular" | custom-call | tf_op jit(solution)/shard_map/vmap(jit(_solve_triangular))/triangular_solve | solution.py:35
  222.8 1.0 fusion.14
  223.8 2.0 fusion.1
  226.0 1.3 collective-permute-start
  227.3 1.9 fusion.2
  229.5 2.5 %copy.37 = bf16[1,4096,256]{2,1,0:T(8,128)(2,1)} copy(bf16[1,4096,256]{1,2,0:T(8,128)(2,1)S(1)} %maximum_bitcast_fusion) | data formatting | bytes 4194304
  231.9 4.5 %collective-permute-done = f32[1,256,256]{2,1,0:T(8,128)S(1)} collective-permute-done((f32[1,256,256]{2,1,0:T(8,128)S(1)}, f32[1,256,256]{2,1,0:T(8,128)S(1)}, u32[]{:S(2)}, u32[]{:S(2)}) %collective-permute-start) | collective-permute-done | bytes 262176 | tf_op jit(solution)/shard_map/while/body/eval_jaxpr/ppermute | solution.py:15
  236.4 1.1 fusion.7
  (70 shorter events, 2.5 us)
Async XLA Ops:
  34.8 7.5 %copy-start = (s32[1,1,16]{2,1,0:T(1,128)S(1)}, s32[1,1,16]{2,1,0:T(1,128)}, u32[]{:S(2)}) copy-start(s32[1,1,16]{2,1,0:T(1,128)} %param.9) | copy-start | bytes 196
  34.8 8.2 %copy-start.1 = (pred[4096]{0:T(1024)(128)(4,1)S(1)}, pred[4096]{0:T(1024)(128)(4,1)}, u32[]{:S(2)}) copy-start(pred[4096]{0:T(1024)(128)(4,1)} %constant.272) | copy-start | bytes 12292
  34.8 8.2 %copy-start.2 = (pred[4096]{0:T(1024)(128)(4,1)S(1)}, pred[4096]{0:T(1024)(128)(4,1)}, u32[]{:S(2)}) copy-start(pred[4096]{0:T(1024)(128)(4,1)} %constant.271) | copy-start | bytes 12292
  34.8 8.2 %copy-start.3 = (pred[4096]{0:T(1024)(128)(4,1)S(1)}, pred[4096]{0:T(1024)(128)(4,1)}, u32[]{:S(2)}) copy-start(pred[4096]{0:T(1024)(128)(4,1)} %constant.270) | copy-start | bytes 12292
  34.8 8.2 %copy-start.4 = (pred[4096]{0:T(1024)(128)(4,1)S(1)}, pred[4096]{0:T(1024)(128)(4,1)}, u32[]{:S(2)}) copy-start(pred[4096]{0:T(1024)(128)(4,1)} %constant.269) | copy-start | bytes 12292
  34.8 8.2 %copy-start.5 = (pred[4096]{0:T(1024)(128)(4,1)S(1)}, pred[4096]{0:T(1024)(128)(4,1)}, u32[]{:S(2)}) copy-start(pred[4096]{0:T(1024)(128)(4,1)} %constant.268) | copy-start | bytes 12292
  34.8 8.2 %copy-start.6 = (pred[4096]{0:T(1024)(128)(4,1)S(1)}, pred[4096]{0:T(1024)(128)(4,1)}, u32[]{:S(2)}) copy-start(pred[4096]{0:T(1024)(128)(4,1)} %constant.267) | copy-start | bytes 12292
  34.8 8.2 %copy-start.7 = (pred[4096]{0:T(1024)(128)(4,1)S(1)}, pred[4096]{0:T(1024)(128)(4,1)}, u32[]{:S(2)}) copy-start(pred[4096]{0:T(1024)(128)(4,1)} %constant.266) | copy-start | bytes 12292
  34.8 8.2 %copy-start.8 = (pred[4096]{0:T(1024)(128)(4,1)S(1)}, pred[4096]{0:T(1024)(128)(4,1)}, u32[]{:S(2)}) copy-start(pred[4096]{0:T(1024)(128)(4,1)} %constant.265) | copy-start | bytes 12292
  34.8 8.2 %copy-start.9 = (pred[4096]{0:T(1024)(128)(4,1)S(1)}, pred[4096]{0:T(1024)(128)(4,1)}, u32[]{:S(2)}) copy-start(pred[4096]{0:T(1024)(128)(4,1)} %constant.264) | copy-start | bytes 12292
  34.9 8.2 %copy-start.10 = (pred[4096]{0:T(1024)(128)(4,1)S(1)}, pred[4096]{0:T(1024)(128)(4,1)}, u32[]{:S(2)}) copy-start(pred[4096]{0:T(1024)(128)(4,1)} %constant.263) | copy-start | bytes 12292
  34.9 8.2 %copy-start.11 = (pred[4096]{0:T(1024)(128)(4,1)S(1)}, pred[4096]{0:T(1024)(128)(4,1)}, u32[]{:S(2)}) copy-start(pred[4096]{0:T(1024)(128)(4,1)} %constant.262) | copy-start | bytes 12292
  34.9 8.2 %copy-start.12 = (pred[4096]{0:T(1024)(128)(4,1)S(1)}, pred[4096]{0:T(1024)(128)(4,1)}, u32[]{:S(2)}) copy-start(pred[4096]{0:T(1024)(128)(4,1)} %constant.261) | copy-start | bytes 12292
  34.9 8.2 %copy-start.13 = (pred[4096]{0:T(1024)(128)(4,1)S(1)}, pred[4096]{0:T(1024)(128)(4,1)}, u32[]{:S(2)}) copy-start(pred[4096]{0:T(1024)(128)(4,1)} %constant.260) | copy-start | bytes 12292
  34.9 8.2 %copy-start.14 = (pred[4096]{0:T(1024)(128)(4,1)S(1)}, pred[4096]{0:T(1024)(128)(4,1)}, u32[]{:S(2)}) copy-start(pred[4096]{0:T(1024)(128)(4,1)} %constant.259) | copy-start | bytes 12292
  34.9 8.2 %copy-start.15 = (pred[4096]{0:T(1024)(128)(4,1)S(1)}, pred[4096]{0:T(1024)(128)(4,1)}, u32[]{:S(2)}) copy-start(pred[4096]{0:T(1024)(128)(4,1)} %constant.258) | copy-start | bytes 12292
  34.9 53.8 %all-to-all-start = ((bf16[16,2,32768]{2,1,0:T(2,128)(2,1)}), bf16[16,2,32768]{2,1,0:T(2,128)(2,1)S(1)}, u32[]{:S(2)}, u32[]{:S(2)}) async-start(bf16[16,2,32768]{2,1,0:T(2,128)(2,1)} %reshape.615), calls=%async_computation | async-start | bytes 4194304 | tf_op jit(solution)/shard_map/all_to_all | solution.py:46
  226.0 10.4 %collective-permute-start = (f32[1,256,256]{2,1,0:T(8,128)S(1)}, f32[1,256,256]{2,1,0:T(8,128)S(1)}, u32[]{:S(2)}, u32[]{:S(2)}) collective-permute-start(f32[1,256,256]{2,1,0:T(8,128)S(1)} %bitcast.217), channel_id=1, source_target_pairs={{0,16},{1,17},{2,18},{3,19},{4,20},{5,21},{6,22},{7,23},{8,24},{9,... | collective-permute-start | bytes 786440 | tf_op jit(solution)/shard_map/while/body/eval_jaxpr/ppermute | solution.py:15
where the time goes:
time: 242 us; the launch traced here: 238 us
  other arithmetic  140 us (58%)
  waiting for transfers between devices  40 us (17%)
  local copies, waits for them, and re-layouts  34 us (14%)
  matrix products  10.4 us (4%)
  starting transfers between devices  7.93 us (3%)
  between operations  4.89 us (2%)
    all_to_all x1, waiting for transfers between devices, local(): lax.all_to_all(products, 'blk', split_axis=2, concat_axis=1, tiled=True)  35.5 us
    another operation x7, other arithmetic, factor_sector(): lower_two = jnp.linalg.cholesky(gram_two)  34.6 us
    another operation x6, other arithmetic, factor_sector(): lower_one = jnp.linalg.cholesky(gram_raw + shift_value * identity)  34 us
    unnamed x38, local copies, waits for them, and re-layouts  24.3 us
    unnamed x1, other arithmetic  21.6 us
    another operation x3, other arithmetic, factor_sector(): jax.scipy.linalg.solve_triangular(lower_one, half_way.T, lower=True)  19.9 us
    another operation x2, other arithmetic, factor_sector(): jax.scipy.linalg.solve_triangular(factor_r.T, masked.astype(jnp.float32)....  19.8 us
    convert_element_type x1, other arithmetic, factor_sector(): gate_rows = jnp.repeat(allowed, total_rows // allowed.shape[0], total_rep...  10 us
  transfers between devices with their start and end apart: 2, of which 2 were waited for; matrix products, arithmetic and copies ran while one was open for 6% of the time, Pallas kernels for 0%

commit v1 on v0

v1 whole, which is shorter than its diff:
```python
import functools

import jax
import jax.numpy as jnp
from jax import lax
from jax.experimental import pallas as pl
from jax.experimental.pallas import tpu as pltpu
from jax.sharding import PartitionSpec as P

SHIFT = 0.05
HIGHEST = lax.Precision.HIGHEST
PARAMS = pltpu.CompilerParams(vmem_limit_bytes=48 << 20)
LANES = 128
SUB = 8


def wide(x, lanes):
    return jnp.concatenate([x] * (lanes // LANES), axis=1)


def split_columns(src, out, sems):
    count, _, width = out.shape
    copies = [
        pltpu.make_async_copy(src.at[0, :, pl.ds(k * width, width)], out.at[k], sems.at[k])
        for k in range(count)
    ]
    for copy in copies:
        copy.start()
    for copy in copies:
        copy.wait()


def factor_in_place(w, n, nb):
    row_at = lax.broadcasted_iota(jnp.int32, (SUB, LANES), 0)
    subs = nb // SUB
    for r0 in range(0, n, nb):
        p = [w[r0 + SUB * i : r0 + SUB * (i + 1), :] for i in range(subs)]
        for s in range(subs):
            cols = {}
            for i in range(s, subs):
                for c in range(SUB):
                    at = r0 + SUB * s + c
                    cols[i, c] = jnp.broadcast_to(p[i][:, at : at + 1], (SUB, LANES))
            pivots = jnp.ones((SUB, LANES), jnp.float32)
            for c in range(SUB):
                pivot = jnp.broadcast_to(cols[s, c][c : c + 1, :], (SUB, LANES))
                pivot = jnp.maximum(pivot, SHIFT * SHIFT)
                inverse = 1.0 / pivot
                pivots = jnp.where(row_at == c, pivot, pivots)
                row = jnp.broadcast_to(p[s][c : c + 1, :], p[s].shape)
                ahead = {
                    d: jnp.broadcast_to(cols[s, d][c : c + 1, :], (SUB, LANES)) for d in range(c + 1, SUB)
                }
                for i in range(s, subs):
                    times = cols[i, c] * inverse
                    if i == s:
                        if c == SUB - 1:
                            continue
                        times = jnp.where(row_at > c, times, 0.0)
                    p[i] = p[i] - wide(times, 2 * n) * row
                    for d in range(c + 1, SUB):
                        cols[i, d] = cols[i, d] - times * ahead[d]
            p[s] = p[s] * wide(lax.rsqrt(pivots), 2 * n)
        u = jnp.concatenate(p, axis=0)
        w[r0 : r0 + nb, :] = u
        end = r0 + nb
        if end < n:
            first = end // LANES * LANES
            last = n + -(-end // LANES) * LANES
            t = lax.dot_general(
                u[:, first:n],
                u[:, first:last],
                (((0,), (0,)), ((), ())),
                precision=HIGHEST,
                preferred_element_type=jnp.float32,
            )
            w[end:n, first:last] = w[end:n, first:last] - t[end - first :, :]


def gram_factor(nb, compat, size, panel, r_out, high_out, low_out, w):
    rows, n = panel.shape
    groups = compat.shape[1]
    each = rows // groups
    g = jnp.zeros((n, n), jnp.float32)
    for k in range(groups):
        block = panel[k * each : (k + 1) * each, :]
        part = lax.dot_general(block, block, (((0,), (0,)), ((), ())), preferred_element_type=jnp.float32)
        g = g + part * compat[0, k].astype(jnp.float32)
    i = lax.broadcasted_iota(jnp.int32, (n, n), 0)
    j = lax.broadcasted_iota(jnp.int32, (n, n), 1)
    live = jnp.logical_and(i < size[0, 0], j < size[0, 0])
    eye = (i == j).astype(jnp.float32)
    w[:, :n] = jnp.where(live, (1.0 + SHIFT) * g, 0.0) + (SHIFT * SHIFT) * eye
    w[:, n:] = eye
    factor_in_place(w, n, nb)
    r_out[...] = jnp.where(i <= j, w[:, :n], 0.0)
    inverse = jnp.where(jnp.logical_and(i >= j, live), w[:, n:], 0.0)
    high = inverse.astype(jnp.bfloat16)
    high_out[...] = high
    low_out[...] = (inverse - high.astype(jnp.float32)).astype(jnp.bfloat16)


def orthonormal_rows(compat, panel, high, low, out):
    k = pl.program_id(0)
    dims = (((1,), (1,)), ((), ()))
    block = panel[...]
    q = lax.dot_general(block, high[...], dims, preferred_element_type=jnp.float32)
    q = q + lax.dot_general(block, low[...], dims, preferred_element_type=jnp.float32)
    out[0] = (q * compat[0, k].astype(jnp.float32)).astype(jnp.bfloat16)


def chained(by, own, incoming, out):
    later = lax.axis_index("seg") >= by

    @pl.when(later)
    def _():
        out[...] = jnp.dot(own[...], incoming[...], precision=HIGHEST, preferred_element_type=jnp.float32)

    @pl.when(jnp.logical_not(later))
    def _():
        out[...] = own[...]


def local(products, compat, sizes):
    parts = lax.axis_size("blk")
    rows_here, width = products.shape[1], products.shape[2] // parts
    rows = rows_here * parts
    groups = compat.shape[2]
    f32 = functools.partial(jax.ShapeDtypeStruct, dtype=jnp.float32)
    b16 = functools.partial(jax.ShapeDtypeStruct, dtype=jnp.bfloat16)
    in_smem = pl.BlockSpec(memory_space=pltpu.SMEM)
    in_vmem = pl.BlockSpec(memory_space=pltpu.VMEM)
    blocks = pl.pallas_call(
        split_columns,
        out_shape=b16((parts, rows_here, width)),
        in_specs=[pl.BlockSpec(memory_space=pl.ANY)],
        out_specs=pl.BlockSpec(memory_space=pl.ANY),
        scratch_shapes=[pltpu.SemaphoreType.DMA((parts,))],
    )(products)
    panel = lax.all_to_all(blocks, "blk", split_axis=0, concat_axis=0, tiled=True).reshape(rows, width)
    factor, high, low = pl.pallas_call(
        functools.partial(gram_factor, 64),
        out_shape=(f32((width, width)), b16((width, width)), b16((width, width))),
        in_specs=[in_smem, in_smem, in_vmem],
        out_specs=[in_vmem] * 3,
        scratch_shapes=[pltpu.VMEM((width, 2 * width), jnp.float32)],
        compiler_params=PARAMS,
    )(compat[0], sizes, panel)
    each = rows // groups
    whole = pl.BlockSpec((width, width), lambda k: (0, 0))
    ortho = pl.pallas_call(
        orthonormal_rows,
        grid=(groups,),
        out_shape=b16((1, rows, width)),
        in_specs=[in_smem, pl.BlockSpec((each, width), lambda k: (k, 0)), whole, whole],
        out_specs=pl.BlockSpec((1, each, width), lambda k: (0, k, 0)),
        compiler_params=PARAMS,
        cost_estimate=pl.CostEstimate(
            flops=4 * rows * width * width, bytes_accessed=4 * rows * width, transcendentals=0
        ),
    )(compat[0], panel, high, low)
    sites = lax.axis_size("seg")
    accumulated, by = factor, 1
    while by < sites:
        incoming = lax.ppermute(accumulated, "seg", [(i, i + by) for i in range(sites - by)])
        accumulated = pl.pallas_call(
            functools.partial(chained, by),
            out_shape=f32((width, width)),
            in_specs=[in_vmem] * 2,
            out_specs=in_vmem,
            compiler_params=PARAMS,
        )(accumulated, incoming)
        by *= 2
    return (ortho, accumulated[None, None])


def solution(mesh):
    in_specs = (P("seg", "blk", None), P("seg", "blk", None), P("seg", "blk"))
    out_specs = (P("seg", None, "blk"), P("seg", "blk", None, None))
    return jax.shard_map(local, mesh=mesh, in_specs=in_specs, out_specs=out_specs, check_vma=False)
```

time: 242 us -> 142 us (0.59)
  other arithmetic: 140 us -> 0 us
  Pallas kernels: 0 us -> 84 us
  local copies, waits for them, and re-layouts: 34 us -> 0.01 us
  matrix products: 10.4 us -> 0 us
  waiting for transfers between devices: 40 us -> 47.5 us
  between operations: 4.89 us -> 1.31 us
    another operation x18 -> x0, other arithmetic: 108 us -> none  [the longest x7 34.6 us: factor_sector(): lower_two = jnp.linalg.cholesky(gram_two)]
    pallas_call x0 -> x4, Pallas kernels: none -> 84 us  [the longest x1 64.8 us: local(): pl.pallas_call(split_columns, out_shape=b16((parts, rows_here, width)), i...]
    unnamed x38 -> x2, local copies, waits for them, and re-layouts: 24.3 us -> 0.01 us
    unnamed x1 -> x0, other arithmetic: 21.6 us -> none
    all_to_all x1, waiting for transfers between devices: 35.5 us -> 46.6 us  [local(): lax.all_to_all(blocks, 'blk', split_axis=0, concat_axis=0, tiled=True)]
    convert_element_type x3 -> x0, other arithmetic: 10.3 us -> none  [the longest x1 10 us: factor_sector(): gate_rows = jnp.repeat(allowed, total_rows // allowed.shape[0], total_rep...]
    another operation x24 -> x0, local copies, waits for them, and re-layouts: 8.33 us -> none
    another operation x13 -> x0, matrix products: 7.77 us -> none  [the longest x3 4.99 us: factor_sector(): jax.scipy.linalg.solve_triangular(factor_r.T, masked.astype(jnp.float32)....]
  transfers between devices with their start and end apart: 2 -> 2, of which waited for: 2 -> 2; matrix products, arithmetic and copies ran while one was open for 6% -> 0% of each run, Pallas kernels for 0% -> 6%
where the time goes in v1:
time: 142 us; the launch traced here: 140 us
  Pallas kernels  84 us (59%)
  waiting for transfers between devices  47.5 us (33%)
  starting transfers between devices  7.54 us (5%)
    pallas_call x1, Pallas kernels, local(): pl.pallas_call(split_columns, out_shape=b16((parts, rows_here, width)), i...  64.8 us
    all_to_all x1, waiting for transfers between devices, local(): lax.all_to_all(blocks, 'blk', split_axis=0, concat_axis=0, tiled=True)  46.6 us
    pallas_call x1, Pallas kernels, local(): pl.pallas_call(functools.partial(gram_factor, 64), out_shape=(f32((width,...  9.87 us
    pallas_call x1, Pallas kernels, local(): pl.pallas_call(orthonormal_rows, grid=(groups,), out_shape=b16((1, rows,...  8.26 us
    all_to_all x1, starting transfers between devices, local(): lax.all_to_all(blocks, 'blk', split_axis=0, concat_axis=0, tiled=True)  6.25 us
  transfers between devices with their start and end apart: 2, of which 2 were waited for; matrix products, arithmetic and copies ran while one was open for 0% of the time, Pallas kernels for 6%

profile of v1, /device:TPU:14, one launch (start us, length us, event | category | flops | bytes accessed | tf_op | source)
XLA Modules:
  0.0 140.3 jit_solution(14854630029803588609)
XLA Ops:
  0.6 64.8 %shard_map.50 = bf16[16,256,256]{2,1,0:T(8,128)(2,1)} custom-call(bf16[1,256,4096]{2,1,0:T(8,128)(2,1)} %src.1), custom_call_target="tpu_custom_call" | custom-call | tf_op jit(solution)/shard_map/pallas_call | solution.py:133
  65.4 0.0 copy-start
  65.4 6.3 %all-to-all-start = ((bf16[16,256,256]{2,1,0:T(8,128)(2,1)}), bf16[16,256,256]{2,1,0:T(8,128)(2,1)S(1)}, u32[]{:S(2)}, u32[]{:S(2)}) async-start(bf16[16,256,256]{2,1,0:T(8,128)(2,1)} %shard_map.50), calls=%async_computation | async-start | bytes 4194304 | tf_op jit(solution)/shard_map/all_to_all | solution.py:140
  72.3 46.6 %all-to-all-done = bf16[16,256,256]{2,1,0:T(8,128)(2,1)S(1)} async-done(((bf16[16,256,256]{2,1,0:T(8,128)(2,1)}), bf16[16,256,256]{2,1,0:T(8,128)(2,1)S(1)}, u32[]{:S(2)}, u32[]{:S(2)}) %all-to-all-start) | async-done | bytes 2097184 | tf_op jit(solution)/shard_map/all_to_all | solution.py:140
  118.9 0.0 copy-done
  118.9 9.9 %shard_map.51 = (f32[256,256]{1,0:T(8,128)S(1)}, bf16[256,256]{1,0:T(8,128)(2,1)S(1)}, bf16[256,256]{1,0:T(8,128)(2,1)S(1)}) custom-call(s32[1,16]{1,0:T(1,128)S(1)} %bitcast.5, s32[1,1]{1,0:T(1,128)S(6)} %copy.5.size, bf16[4096,256]{1,0:T(8,128)(2,1)S(1)} %bitcast.3), custom_call_target="tpu_custom_call" | custom-call | tf_op jit(solution)/shard_map/pallas_call | solution.py:141
  128.8 1.3 collective-permute-start
  130.1 8.3 %shard_map.52 = bf16[1,4096,256]{2,1,0:T(8,128)(2,1)} custom-call(s32[1,16]{1,0:T(1,128)S(1)} %bitcast.6, bf16[4096,256]{1,0:T(8,128)(2,1)S(1)} %bitcast.4, bf16[256,256]{1,0:T(8,128)(2,1)S(1)} %get-tuple-element.5.high, bf16[256,256]{1,0:T(8,128)(2,1)S(1)} %get-tuple-element.6.low), custom_call_target="tpu_custom_call" | custom-call | flops 1073741824 | bytes 4194304 | tf_op jit(solution)/shard_map/pallas_call | solution.py:151
  138.4 0.8 collective-permute-done.incoming
  139.2 1.1 shard_map.53
Async XLA Ops:
  65.4 53.5 %copy-start = (s32[1,1,16]{2,1,0:T(1,128)S(1)}, s32[1,1,16]{2,1,0:T(1,128)}, u32[]{:S(2)}) copy-start(s32[1,1,16]{2,1,0:T(1,128)} %param.4) | copy-start | bytes 196
  65.4 53.5 %all-to-all-start = ((bf16[16,256,256]{2,1,0:T(8,128)(2,1)}), bf16[16,256,256]{2,1,0:T(8,128)(2,1)S(1)}, u32[]{:S(2)}, u32[]{:S(2)}) async-start(bf16[16,256,256]{2,1,0:T(8,128)(2,1)} %shard_map.50), calls=%async_computation | async-start | bytes 4194304 | tf_op jit(solution)/shard_map/all_to_all | solution.py:140
  128.8 10.4 %collective-permute-start = (f32[256,256]{1,0:T(8,128)S(1)}, f32[256,256]{1,0:T(8,128)S(1)}, u32[]{:S(2)}, u32[]{:S(2)}) collective-permute-start(f32[256,256]{1,0:T(8,128)S(1)} %get-tuple-element.7.own), channel_id=1, source_target_pairs={{0,16},{1,17},{2,18},{3,19},{4,20},{5,21},{6,22},{7,23},{8,24},{9,... | collective-permute-start | bytes 786440 | tf_op jit(solution)/shard_map/ppermute | solution.py:165

commit v2 on v1

--- a/solution.py
+++ b/solution.py
@@ -1,4 +1,5 @@
 import functools
+import math
 
 import jax
 import jax.numpy as jnp
@@ -18,16 +19,10 @@
     return jnp.concatenate([x] * (lanes // LANES), axis=1)
 
 
-def split_columns(src, out, sems):
+def split_columns(src, out):
     count, _, width = out.shape
-    copies = [
-        pltpu.make_async_copy(src.at[0, :, pl.ds(k * width, width)], out.at[k], sems.at[k])
-        for k in range(count)
-    ]
-    for copy in copies:
-        copy.start()
-    for copy in copies:
-        copy.wait()
+    for k in range(count):
+        out[k] = src[0, :, k * width : (k + 1) * width]
 
 
 def factor_in_place(w, n, nb):
@@ -101,12 +96,15 @@
 
 
 def orthonormal_rows(compat, panel, high, low, out):
-    k = pl.program_id(0)
     dims = (((1,), (1,)), ((), ()))
-    block = panel[...]
-    q = lax.dot_general(block, high[...], dims, preferred_element_type=jnp.float32)
-    q = q + lax.dot_general(block, low[...], dims, preferred_element_type=jnp.float32)
-    out[0] = (q * compat[0, k].astype(jnp.float32)).astype(jnp.bfloat16)
+    steps, groups = pl.num_programs(0), compat.shape[1]
+    at = pl.program_id(0) * (groups // steps)
+    each = panel.shape[0] * steps // groups
+    for k in range(groups // steps):
+        block = panel[k * each : (k + 1) * each, :]
+        q = lax.dot_general(block, high[...], dims, preferred_element_type=jnp.float32)
+        q = q + lax.dot_general(block, low[...], dims, preferred_element_type=jnp.float32)
+        out[0, k * each : (k + 1) * each, :] = (q * compat[0, at + k].astype(jnp.float32)).astype(jnp.bfloat16)
 
 
 def chained(by, own, incoming, out):
@@ -132,10 +130,11 @@
     in_vmem = pl.BlockSpec(memory_space=pltpu.VMEM)
     blocks = pl.pallas_call(
         split_columns,
+        grid=(2,),
         out_shape=b16((parts, rows_here, width)),
-        in_specs=[pl.BlockSpec(memory_space=pl.ANY)],
-        out_specs=pl.BlockSpec(memory_space=pl.ANY),
-        scratch_shapes=[pltpu.SemaphoreType.DMA((parts,))],
+        in_specs=[pl.BlockSpec((1, rows_here // 2, parts * width), lambda k: (0, k, 0))],
+        out_specs=pl.BlockSpec((parts, rows_here // 2, width), lambda k: (0, k, 0)),
+        compiler_params=PARAMS,
     )(products)
     panel = lax.all_to_all(blocks, "blk", split_axis=0, concat_axis=0, tiled=True).reshape(rows, width)
     factor, high, low = pl.pallas_call(
@@ -146,14 +145,14 @@
         scratch_shapes=[pltpu.VMEM((width, 2 * width), jnp.float32)],
         compiler_params=PARAMS,
     )(compat[0], sizes, panel)
-    each = rows // groups
+    steps = math.gcd(groups, 4)
     whole = pl.BlockSpec((width, width), lambda k: (0, 0))
     ortho = pl.pallas_call(
         orthonormal_rows,
-        grid=(groups,),
+        grid=(steps,),
         out_shape=b16((1, rows, width)),
-        in_specs=[in_smem, pl.BlockSpec((each, width), lambda k: (k, 0)), whole, whole],
-        out_specs=pl.BlockSpec((1, each, width), lambda k: (0, k, 0)),
+        in_specs=[in_smem, pl.BlockSpec((rows // steps, width), lambda k: (k, 0)), whole, whole],
+        out_specs=pl.BlockSpec((1, rows // steps, width), lambda k: (0, k, 0)),
         compiler_params=PARAMS,
         cost_estimate=pl.CostEstimate(
             flops=4 * rows * width * width, bytes_accessed=4 * rows * width, transcendentals=0

time: 142 us -> 79.1 us (0.56); the launches traced: 140 us -> 78.9 us
  Pallas kernels: 84 us -> 14.8 us
  waiting for transfers between devices: 47.5 us -> 52.1 us
  local copies, waits for them, and re-layouts: 0.01 us -> 2.9 us
    pallas_call x2, Pallas kernels: 73 us -> 3.89 us  [the longest x1 3.59 us: local(): pl.pallas_call(orthonormal_rows, grid=(steps,), out_shape=b16((1, rows, w...]
    ppermute x1, waiting for transfers between devices: 0.84 us -> 5.51 us  [local(): lax.ppermute(accumulated, 'seg', [(i, i + by) for i in range(sites - by)])]
    unnamed x2 -> x6, local copies, waits for them, and re-layouts: 0.01 us -> 2.9 us
  transfers between devices with their start and end apart: 2 -> 2, of which waited for: 2 -> 2; matrix products, arithmetic and copies ran while one was open for 0% -> 0% of each run, Pallas kernels for 6% -> 5%
where the time goes in v2:
time: 79.1 us; the launch traced here: 78.9 us
  waiting for transfers between devices  52.1 us (66%)
  Pallas kernels  14.8 us (19%)
  starting transfers between devices  7.66 us (10%)
  local copies, waits for them, and re-layouts  2.9 us (4%)
  between operations  1.32 us (2%)
    all_to_all x1, waiting for transfers between devices, local(): lax.all_to_all(blocks, 'blk', split_axis=0, concat_axis=0, tiled=True)  46.6 us
    pallas_call x1, Pallas kernels, local(): pl.pallas_call(functools.partial(gram_factor, 64), out_shape=(f32((width,...  9.86 us
    all_to_all x1, starting transfers between devices, local(): lax.all_to_all(blocks, 'blk', split_axis=0, concat_axis=0, tiled=True)  6.37 us
    ppermute x1, waiting for transfers between devices, local(): lax.ppermute(accumulated, 'seg', [(i, i + by) for i in range(sites - by)])  5.51 us
    pallas_call x1, Pallas kernels, local(): pl.pallas_call(orthonormal_rows, grid=(steps,), out_shape=b16((1, rows, w...  3.59 us
    unnamed x6, local copies, waits for them, and re-layouts  2.9 us
  transfers between devices with their start and end apart: 2, of which 2 were waited for; matrix products, arithmetic and copies ran while one was open for 0% of the time, Pallas kernels for 5%

profile of v2, /device:TPU:14, one launch (start us, length us, event | category | flops | bytes accessed | tf_op | source)
XLA Modules:
  0.0 78.9 jit_solution(10311284985654366194)
XLA Ops:
  0.6 0.0 copy-start.1
  0.6 1.6 %copy-done.1 = bf16[1,256,4096]{2,1,0:T(8,128)(2,1)S(1)} copy-done((bf16[1,256,4096]{2,1,0:T(8,128)(2,1)S(1)}, bf16[1,256,4096]{2,1,0:T(8,128)(2,1)}, u32[]{:S(2)}) %copy-start.1) | copy-done | bytes 2097176
  2.2 0.3 shard_map.50
  2.5 0.0 copy-start
  2.5 1.3 %copy-done = bf16[16,256,256]{2,1,0:T(8,128)(2,1)} copy-done((bf16[16,256,256]{2,1,0:T(8,128)(2,1)}, bf16[16,256,256]{2,1,0:T(8,128)(2,1)S(1)}, u32[]{:S(2)}) %copy-start) | copy-done | bytes 2097176
  3.9 0.0 copy-start.2
  3.9 6.4 %all-to-all-start = ((bf16[16,256,256]{2,1,0:T(8,128)(2,1)}), bf16[16,256,256]{2,1,0:T(8,128)(2,1)S(1)}, u32[]{:S(2)}, u32[]{:S(2)}) async-start(bf16[16,256,256]{2,1,0:T(8,128)(2,1)} %copy-done), calls=%async_computation | async-start | bytes 4194304 | tf_op jit(solution)/shard_map/all_to_all | solution.py:139
  10.9 46.6 %all-to-all-done = bf16[16,256,256]{2,1,0:T(8,128)(2,1)S(1)} async-done(((bf16[16,256,256]{2,1,0:T(8,128)(2,1)}), bf16[16,256,256]{2,1,0:T(8,128)(2,1)S(1)}, u32[]{:S(2)}, u32[]{:S(2)}) %all-to-all-start) | async-done | bytes 2097184 | tf_op jit(solution)/shard_map/all_to_all | solution.py:139
  57.5 0.0 copy-done.2
  57.5 9.9 %shard_map.51 = (f32[256,256]{1,0:T(8,128)S(1)}, bf16[256,256]{1,0:T(8,128)(2,1)S(1)}, bf16[256,256]{1,0:T(8,128)(2,1)S(1)}) custom-call(s32[1,16]{1,0:T(1,128)S(1)} %bitcast.5, s32[1,1]{1,0:T(1,128)S(6)} %copy.5.size, bf16[4096,256]{1,0:T(8,128)(2,1)S(1)} %bitcast.3), custom_call_target="tpu_custom_call" | custom-call | tf_op jit(solution)/shard_map/pallas_call | solution.py:140
  67.4 1.3 %collective-permute-start = (f32[256,256]{1,0:T(8,128)S(1)}, f32[256,256]{1,0:T(8,128)S(1)}, u32[]{:S(2)}, u32[]{:S(2)}) collective-permute-start(f32[256,256]{1,0:T(8,128)S(1)} %get-tuple-element.7.own), channel_id=1, source_target_pairs={{0,16},{1,17},{2,18},{3,19},{4,20},{5,21},{6,22},{7,23},{8,24},{9,... | collective-permute-start | bytes 786440 | tf_op jit(solution)/shard_map/ppermute | solution.py:164
  68.7 3.6 %shard_map.52 = bf16[1,4096,256]{2,1,0:T(8,128)(2,1)} custom-call(s32[1,16]{1,0:T(1,128)S(1)} %bitcast.6, bf16[4096,256]{1,0:T(8,128)(2,1)S(1)} %bitcast.4, bf16[256,256]{1,0:T(8,128)(2,1)S(1)} %get-tuple-element.5.high, bf16[256,256]{1,0:T(8,128)(2,1)S(1)} %get-tuple-element.6.low), custom_call_target="tpu_custom_call" | custom-call | flops 1073741824 | bytes 4194304 | tf_op jit(solution)/shard_map/pallas_call | solution.py:150
  72.3 5.5 %collective-permute-done.incoming = f32[256,256]{1,0:T(8,128)S(1)} collective-permute-done((f32[256,256]{1,0:T(8,128)S(1)}, f32[256,256]{1,0:T(8,128)S(1)}, u32[]{:S(2)}, u32[]{:S(2)}) %collective-permute-start) | collective-permute-done | bytes 262176 | tf_op jit(solution)/shard_map/ppermute | solution.py:164
  77.8 1.1 %shard_map.53 = f32[256,256]{1,0:T(8,128)} custom-call(f32[256,256]{1,0:T(8,128)S(1)} %get-tuple-element.7.own, f32[256,256]{1,0:T(8,128)S(1)} %collective-permute-done.incoming), custom_call_target="tpu_custom_call" | custom-call | tf_op jit(solution)/shard_map/pallas_call | solution.py:165
Async XLA Ops:
  0.6 1.6 %copy-start.1 = (bf16[1,256,4096]{2,1,0:T(8,128)(2,1)S(1)}, bf16[1,256,4096]{2,1,0:T(8,128)(2,1)}, u32[]{:S(2)}) copy-start(bf16[1,256,4096]{2,1,0:T(8,128)(2,1)} %src.1) | copy-start | bytes 6291460
  2.5 1.3 %copy-start = (bf16[16,256,256]{2,1,0:T(8,128)(2,1)}, bf16[16,256,256]{2,1,0:T(8,128)(2,1)S(1)}, u32[]{:S(2)}) copy-start(bf16[16,256,256]{2,1,0:T(8,128)(2,1)S(1)} %shard_map.50) | copy-start | bytes 6291460
  3.9 53.6 %copy-start.2 = (s32[1,1,16]{2,1,0:T(1,128)S(1)}, s32[1,1,16]{2,1,0:T(1,128)}, u32[]{:S(2)}) copy-start(s32[1,1,16]{2,1,0:T(1,128)} %param.4) | copy-start | bytes 196
  3.9 53.6 %all-to-all-start = ((bf16[16,256,256]{2,1,0:T(8,128)(2,1)}), bf16[16,256,256]{2,1,0:T(8,128)(2,1)S(1)}, u32[]{:S(2)}, u32[]{:S(2)}) async-start(bf16[16,256,256]{2,1,0:T(8,128)(2,1)} %copy-done), calls=%async_computation | async-start | bytes 4194304 | tf_op jit(solution)/shard_map/all_to_all | solution.py:139
  67.4 10.4 %collective-permute-start = (f32[256,256]{1,0:T(8,128)S(1)}, f32[256,256]{1,0:T(8,128)S(1)}, u32[]{:S(2)}, u32[]{:S(2)}) collective-permute-start(f32[256,256]{1,0:T(8,128)S(1)} %get-tuple-element.7.own), channel_id=1, source_target_pairs={{0,16},{1,17},{2,18},{3,19},{4,20},{5,21},{6,22},{7,23},{8,24},{9,... | collective-permute-start | bytes 786440 | tf_op jit(solution)/shard_map/ppermute | solution.py:164

commit v3 on v2

--- a/solution.py
+++ b/solution.py
@@ -15,8 +15,12 @@
 SUB = 8
 
 
-def wide(x, lanes):
-    return jnp.concatenate([x] * (lanes // LANES), axis=1)
+def down(x, c):
+    return jnp.broadcast_to(x[c : c + 1, :], (SUB, LANES))
+
+
+def across(x, c):
+    return jnp.broadcast_to(x[:, c : c + 1], (SUB, LANES))
 
 
 def split_columns(src, out):
@@ -25,54 +29,80 @@
         out[k] = src[0, :, k * width : (k + 1) * width]
 
 
-def factor_in_place(w, n, nb):
+def outer(u, first, last):
+    high = u.astype(jnp.bfloat16)
+    rest = u - high.astype(jnp.float32)
+    mid = rest.astype(jnp.bfloat16)
+    low = (rest - mid.astype(jnp.float32)).astype(jnp.bfloat16)
+    left = jnp.concatenate([x[:, first:last] for x in (high, high, mid, high, mid, low)], axis=0)
+    right = jnp.concatenate([high, mid, high, low, mid, high], axis=0)
+    return lax.dot_general(left, right, (((0,), (0,)), ((), ())), preferred_element_type=jnp.float32)
+
+
+def factor_in_place(w, n, step=16):
     row_at = lax.broadcasted_iota(jnp.int32, (SUB, LANES), 0)
-    subs = nb // SUB
-    for r0 in range(0, n, nb):
-        p = [w[r0 + SUB * i : r0 + SUB * (i + 1), :] for i in range(subs)]
-        for s in range(subs):
-            cols = {}
-            for i in range(s, subs):
-                for c in range(SUB):
-                    at = r0 + SUB * s + c
-                    cols[i, c] = jnp.broadcast_to(p[i][:, at : at + 1], (SUB, LANES))
-            pivots = jnp.ones((SUB, LANES), jnp.float32)
-            for c in range(SUB):
-                pivot = jnp.broadcast_to(cols[s, c][c : c + 1, :], (SUB, LANES))
-                pivot = jnp.maximum(pivot, SHIFT * SHIFT)
-                inverse = 1.0 / pivot
-                pivots = jnp.where(row_at == c, pivot, pivots)
-                row = jnp.broadcast_to(p[s][c : c + 1, :], p[s].shape)
-                ahead = {
-                    d: jnp.broadcast_to(cols[s, d][c : c + 1, :], (SUB, LANES)) for d in range(c + 1, SUB)
-                }
-                for i in range(s, subs):
-                    times = cols[i, c] * inverse
-                    if i == s:
-                        if c == SUB - 1:
-                            continue
-                        times = jnp.where(row_at > c, times, 0.0)
-                    p[i] = p[i] - wide(times, 2 * n) * row
-                    for d in range(c + 1, SUB):
-                        cols[i, d] = cols[i, d] - times * ahead[d]
-            p[s] = p[s] * wide(lax.rsqrt(pivots), 2 * n)
-        u = jnp.concatenate(p, axis=0)
-        w[r0 : r0 + nb, :] = u
-        end = r0 + nb
-        if end < n:
-            first = end // LANES * LANES
-            last = n + -(-end // LANES) * LANES
-            t = lax.dot_general(
-                u[:, first:n],
-                u[:, first:last],
-                (((0,), (0,)), ((), ())),
-                precision=HIGHEST,
-                preferred_element_type=jnp.float32,
+    lanes = 2 * n // LANES
+    p = {}
+    for r0 in range(0, n, step):
+        half, base = r0 // LANES, r0 % LANES
+        end = r0 + step
+        act = range(half, min(lanes, half + n // LANES + 1))
+        held = range(r0, min(end + step, n), SUB)
+        for r in held:
+            for t in act:
+                if (r, t) not in p:
+                    p[r, t] = w[r : r + SUB, t * LANES : (t + 1) * LANES]
+        cols = {}
+        for r in held:
+            for c in range(min(step, r - r0 + SUB)):
+                cols[r, c] = across(p[r, half], base + c)
+        pivots = {r: jnp.ones((SUB, LANES), jnp.float32) for r in range(r0, end, SUB)}
+        for c in range(step):
+            own, at = r0 + c // SUB * SUB, c % SUB
+            pivot = jnp.maximum(down(cols[own, c], at), SHIFT * SHIFT)
+            inverse = 1.0 / pivot
+            pivots[own] = jnp.where(row_at == at, pivot, pivots[own])
+            row = {t: down(p[own, t], at) for t in act}
+            ahead = {d: down(cols[r0 + d // SUB * SUB, c], d % SUB) for d in range(c + 1, step)}
+            for r in held:
+                if r < own or (r == own and at == SUB - 1):
+                    continue
+                x = cols[r, c]
+                if r == own:
+                    x = jnp.where(row_at > at, x, 0.0)
+                times = x * inverse
+                for d in range(c + 1, step):
+                    if (r, d) not in cols:
+                        continue
+                    if d == c + 1 and r == r0 + d // SUB * SUB:
+                        cols[r, d] = cols[r, d] - (x * ahead[d]) * inverse
+                    else:
+                        cols[r, d] = cols[r, d] - times * ahead[d]
+                for t in act:
+                    p[r, t] = p[r, t] - times * row[t]
+        for r in range(r0, end, SUB):
+            scale = lax.rsqrt(pivots[r])
+            for t in act:
+                p[r, t] = p[r, t] * scale
+                w[r : r + SUB, t * LANES : (t + 1) * LANES] = p[r, t]
+        below = end + step
+        if below < n:
+            first, last = end // LANES, act[-1] + 1
+            u = jnp.concatenate(
+                [
+                    jnp.concatenate([p[r, t] for t in range(first, last)], axis=1)
+                    for r in range(r0, end, SUB)
+                ],
+                axis=0,
             )
-            w[end:n, first:last] = w[end:n, first:last] - t[end - first :, :]
-
-
-def gram_factor(nb, compat, size, panel, r_out, high_out, low_out, w):
+            skip = below // LANES
+            update = outer(u, (skip - first) * LANES, n - first * LANES)
+            cut = slice(first * LANES, last * LANES)
+            w[below:n, cut] = w[below:n, cut] - update[below - skip * LANES :, :]
+        p = {at: value for at, value in p.items() if at[0] >= end}
+
+
+def gram_factor(compat, size, panel, r_out, high_out, low_out, w):
     rows, n = panel.shape
     groups = compat.shape[1]
     each = rows // groups
@@ -87,7 +117,7 @@
     eye = (i == j).astype(jnp.float32)
     w[:, :n] = jnp.where(live, (1.0 + SHIFT) * g, 0.0) + (SHIFT * SHIFT) * eye
     w[:, n:] = eye
-    factor_in_place(w, n, nb)
+    factor_in_place(w, n)
     r_out[...] = jnp.where(i <= j, w[:, :n], 0.0)
     inverse = jnp.where(jnp.logical_and(i >= j, live), w[:, n:], 0.0)
     high = inverse.astype(jnp.bfloat16)
@@ -138,7 +168,7 @@
     )(products)
     panel = lax.all_to_all(blocks, "blk", split_axis=0, concat_axis=0, tiled=True).reshape(rows, width)
     factor, high, low = pl.pallas_call(
-        functools.partial(gram_factor, 64),
+        gram_factor,
         out_shape=(f32((width, width)), b16((width, width)), b16((width, width))),
         in_specs=[in_smem, in_smem, in_vmem],
         out_specs=[in_vmem] * 3,

time: 79.1 us -> 76.2 us (0.963)
  Pallas kernels: 14.8 us -> 11.9 us
    pallas_call x1, Pallas kernels: 9.86 us -> 6.95 us  [local(): pl.pallas_call(gram_factor, out_shape=(f32((width, width)), b16((width, w...]
where the time goes in v3:
time: 76.2 us; the launch traced here: 75.9 us
  waiting for transfers between devices  52.1 us (68%)
  Pallas kernels  11.9 us (16%)
  starting transfers between devices  7.66 us (10%)
  local copies, waits for them, and re-layouts  2.9 us (4%)
  between operations  1.32 us (2%)
    all_to_all x1, waiting for transfers between devices, local(): lax.all_to_all(blocks, 'blk', split_axis=0, concat_axis=0, tiled=True)  46.6 us
    pallas_call x1, Pallas kernels, local(): pl.pallas_call(gram_factor, out_shape=(f32((width, width)), b16((width, w...  6.95 us
    all_to_all x1, starting transfers between devices, local(): lax.all_to_all(blocks, 'blk', split_axis=0, concat_axis=0, tiled=True)  6.37 us
    ppermute x1, waiting for transfers between devices, local(): lax.ppermute(accumulated, 'seg', [(i, i + by) for i in range(sites - by)])  5.51 us
    pallas_call x1, Pallas kernels, local(): pl.pallas_call(orthonormal_rows, grid=(steps,), out_shape=b16((1, rows, w...  3.59 us
    unnamed x6, local copies, waits for them, and re-layouts  2.9 us
  transfers between devices with their start and end apart: 2, of which 2 were waited for; matrix products, arithmetic and copies ran while one was open for 0% of the time, Pallas kernels for 5%

profile of v3, /device:TPU:14, one launch (start us, length us, event | category | flops | bytes accessed | tf_op | source)
XLA Modules:
  0.0 75.9 jit_solution(13796498180409118272)
XLA Ops:
  0.6 0.0 copy-start.1
  0.6 1.6 %copy-done.1 = bf16[1,256,4096]{2,1,0:T(8,128)(2,1)S(1)} copy-done((bf16[1,256,4096]{2,1,0:T(8,128)(2,1)S(1)}, bf16[1,256,4096]{2,1,0:T(8,128)(2,1)}, u32[]{:S(2)}) %copy-start.1) | copy-done | bytes 2097176
  2.2 0.3 shard_map.50
  2.5 0.0 copy-start
  2.5 1.3 %copy-done = bf16[16,256,256]{2,1,0:T(8,128)(2,1)} copy-done((bf16[16,256,256]{2,1,0:T(8,128)(2,1)}, bf16[16,256,256]{2,1,0:T(8,128)(2,1)S(1)}, u32[]{:S(2)}) %copy-start) | copy-done | bytes 2097176
  3.9 0.0 copy-start.2
  3.9 6.4 %all-to-all-start = ((bf16[16,256,256]{2,1,0:T(8,128)(2,1)}), bf16[16,256,256]{2,1,0:T(8,128)(2,1)S(1)}, u32[]{:S(2)}, u32[]{:S(2)}) async-start(bf16[16,256,256]{2,1,0:T(8,128)(2,1)} %copy-done), calls=%async_computation | async-start | bytes 4194304 | tf_op jit(solution)/shard_map/all_to_all | solution.py:169
  10.9 46.6 %all-to-all-done = bf16[16,256,256]{2,1,0:T(8,128)(2,1)S(1)} async-done(((bf16[16,256,256]{2,1,0:T(8,128)(2,1)}), bf16[16,256,256]{2,1,0:T(8,128)(2,1)S(1)}, u32[]{:S(2)}, u32[]{:S(2)}) %all-to-all-start) | async-done | bytes 2097184 | tf_op jit(solution)/shard_map/all_to_all | solution.py:169
  57.5 0.0 copy-done.2
  57.5 6.9 %shard_map.51 = (f32[256,256]{1,0:T(8,128)S(1)}, bf16[256,256]{1,0:T(8,128)(2,1)S(1)}, bf16[256,256]{1,0:T(8,128)(2,1)S(1)}) custom-call(s32[1,16]{1,0:T(1,128)S(1)} %bitcast.5, s32[1,1]{1,0:T(1,128)S(6)} %copy.5.size, bf16[4096,256]{1,0:T(8,128)(2,1)S(1)} %bitcast.3), custom_call_target="tpu_custom_call" | custom-call | tf_op jit(solution)/shard_map/pallas_call | solution.py:170
  64.5 1.3 %collective-permute-start = (f32[256,256]{1,0:T(8,128)S(1)}, f32[256,256]{1,0:T(8,128)S(1)}, u32[]{:S(2)}, u32[]{:S(2)}) collective-permute-start(f32[256,256]{1,0:T(8,128)S(1)} %get-tuple-element.7.own), channel_id=1, source_target_pairs={{0,16},{1,17},{2,18},{3,19},{4,20},{5,21},{6,22},{7,23},{8,24},{9,... | collective-permute-start | bytes 786440 | tf_op jit(solution)/shard_map/ppermute | solution.py:194
  65.8 3.6 %shard_map.52 = bf16[1,4096,256]{2,1,0:T(8,128)(2,1)} custom-call(s32[1,16]{1,0:T(1,128)S(1)} %bitcast.6, bf16[4096,256]{1,0:T(8,128)(2,1)S(1)} %bitcast.4, bf16[256,256]{1,0:T(8,128)(2,1)S(1)} %get-tuple-element.5.high, bf16[256,256]{1,0:T(8,128)(2,1)S(1)} %get-tuple-element.6.low), custom_call_target="tpu_custom_call" | custom-call | flops 1073741824 | bytes 4194304 | tf_op jit(solution)/shard_map/pallas_call | solution.py:180
  69.3 5.5 %collective-permute-done.incoming = f32[256,256]{1,0:T(8,128)S(1)} collective-permute-done((f32[256,256]{1,0:T(8,128)S(1)}, f32[256,256]{1,0:T(8,128)S(1)}, u32[]{:S(2)}, u32[]{:S(2)}) %collective-permute-start) | collective-permute-done | bytes 262176 | tf_op jit(solution)/shard_map/ppermute | solution.py:194
  74.9 1.1 %shard_map.53 = f32[256,256]{1,0:T(8,128)} custom-call(f32[256,256]{1,0:T(8,128)S(1)} %get-tuple-element.7.own, f32[256,256]{1,0:T(8,128)S(1)} %collective-permute-done.incoming), custom_call_target="tpu_custom_call" | custom-call | tf_op jit(solution)/shard_map/pallas_call | solution.py:195
Async XLA Ops:
  0.6 1.6 %copy-start.1 = (bf16[1,256,4096]{2,1,0:T(8,128)(2,1)S(1)}, bf16[1,256,4096]{2,1,0:T(8,128)(2,1)}, u32[]{:S(2)}) copy-start(bf16[1,256,4096]{2,1,0:T(8,128)(2,1)} %src.1) | copy-start | bytes 6291460
  2.5 1.3 %copy-start = (bf16[16,256,256]{2,1,0:T(8,128)(2,1)}, bf16[16,256,256]{2,1,0:T(8,128)(2,1)S(1)}, u32[]{:S(2)}) copy-start(bf16[16,256,256]{2,1,0:T(8,128)(2,1)S(1)} %shard_map.50) | copy-start | bytes 6291460
  3.9 53.6 %copy-start.2 = (s32[1,1,16]{2,1,0:T(1,128)S(1)}, s32[1,1,16]{2,1,0:T(1,128)}, u32[]{:S(2)}) copy-start(s32[1,1,16]{2,1,0:T(1,128)} %param.4) | copy-start | bytes 196
  3.9 53.6 %all-to-all-start = ((bf16[16,256,256]{2,1,0:T(8,128)(2,1)}), bf16[16,256,256]{2,1,0:T(8,128)(2,1)S(1)}, u32[]{:S(2)}, u32[]{:S(2)}) async-start(bf16[16,256,256]{2,1,0:T(8,128)(2,1)} %copy-done), calls=%async_computation | async-start | bytes 4194304 | tf_op jit(solution)/shard_map/all_to_all | solution.py:169
  64.5 10.4 %collective-permute-start = (f32[256,256]{1,0:T(8,128)S(1)}, f32[256,256]{1,0:T(8,128)S(1)}, u32[]{:S(2)}, u32[]{:S(2)}) collective-permute-start(f32[256,256]{1,0:T(8,128)S(1)} %get-tuple-element.7.own), channel_id=1, source_target_pairs={{0,16},{1,17},{2,18},{3,19},{4,20},{5,21},{6,22},{7,23},{8,24},{9,... | collective-permute-start | bytes 786440 | tf_op jit(solution)/shard_map/ppermute | solution.py:194

commit v4 on v3

--- a/solution.py
+++ b/solution.py
@@ -23,10 +23,22 @@
     return jnp.broadcast_to(x[:, c : c + 1], (SUB, LANES))
 
 
-def split_columns(src, out):
-    count, _, width = out.shape
-    for k in range(count):
-        out[k] = src[0, :, k * width : (k + 1) * width]
+def split_columns(src, out, rows, blocks, arrived, sent):
+    count, total, width = out.shape
+    parts = arrived.shape[0]
+    each = total // parts
+    cuts = [pl.ds(i * each, each) for i in range(parts)]
+    reads = [pltpu.make_async_copy(src.at[0, cut], rows.at[cut], arrived.at[i]) for i, cut in enumerate(cuts)]
+    writes = [pltpu.make_async_copy(blocks.at[:, cut], out.at[:, cut], sent.at[i]) for i, cut in enumerate(cuts)]
+    for read in reads:
+        read.start()
+    for cut, read, write in zip(cuts, reads, writes):
+        read.wait()
+        for k in range(count):
+            blocks[k, cut, :] = rows[cut, k * width : (k + 1) * width]
+        write.start()
+    for write in writes:
+        write.wait()
 
 
 def outer(u, first, last):
@@ -102,7 +114,30 @@
         p = {at: value for at, value in p.items() if at[0] >= end}
 
 
-def gram_factor(compat, size, panel, r_out, high_out, low_out, w):
+def pack(r, out):
+    n = r.shape[0]
+    q = n // 4
+    out[:q, :] = r[:q, :]
+    out[q : 2 * q, :] = r[q : 2 * q, :]
+    out[q : 2 * q, :q] = r[3 * q :, 3 * q :]
+    out[2 * q :, : 2 * q] = r[2 * q : 2 * q + q // 2, 2 * q :]
+    out[2 * q :, 2 * q :] = r[2 * q + q // 2 : 3 * q, 2 * q :]
+
+
+def unpack(packed, r):
+    n = r.shape[0]
+    q = n // 4
+    r[:q, :] = packed[:q, :]
+    r[q : 2 * q, :] = packed[q : 2 * q, :]
+    r[q : 2 * q, :q] = jnp.zeros((q, q), r.dtype)
+    r[2 * q :, : 2 * q] = jnp.zeros((2 * q, 2 * q), r.dtype)
+    r[2 * q : 2 * q + q // 2, 2 * q :] = packed[2 * q :, : 2 * q]
+    r[2 * q + q // 2 : 3 * q, 2 * q :] = packed[2 * q :, 2 * q :]
+    r[3 * q :, 2 * q : 3 * q] = jnp.zeros((q, q), r.dtype)
+    r[3 * q :, 3 * q :] = packed[q : 2 * q, :q]
+
+
+def gram_factor(compat, size, panel, r_out, packed_out, high_out, low_out, w):
     rows, n = panel.shape
     groups = compat.shape[1]
     each = rows // groups
@@ -119,6 +154,7 @@
     w[:, n:] = eye
     factor_in_place(w, n)
     r_out[...] = jnp.where(i <= j, w[:, :n], 0.0)
+    pack(r_out, packed_out)
     inverse = jnp.where(jnp.logical_and(i >= j, live), w[:, n:], 0.0)
     high = inverse.astype(jnp.bfloat16)
     high_out[...] = high
@@ -137,16 +173,23 @@
         out[0, k * each : (k + 1) * each, :] = (q * compat[0, at + k].astype(jnp.float32)).astype(jnp.bfloat16)
 
 
-def chained(by, own, incoming, out):
+def chained(by, own, incoming, out, packed_out, before):
     later = lax.axis_index("seg") >= by
 
     @pl.when(later)
     def _():
-        out[...] = jnp.dot(own[...], incoming[...], precision=HIGHEST, preferred_element_type=jnp.float32)
+        unpack(incoming, before)
+        h = own.shape[0] // 2
+        dot = functools.partial(jnp.dot, precision=HIGHEST, preferred_element_type=jnp.float32)
+        out[:h, :] = dot(own[:h, :], before[...])
+        out[h:, :h] = jnp.zeros((h, h), jnp.float32)
+        out[h:, h:] = dot(own[h:, h:], before[h:, h:])
 
     @pl.when(jnp.logical_not(later))
     def _():
         out[...] = own[...]
+
+    pack(out, packed_out)
 
 
 def local(products, compat, sizes):
@@ -158,20 +201,28 @@
     b16 = functools.partial(jax.ShapeDtypeStruct, dtype=jnp.bfloat16)
     in_smem = pl.BlockSpec(memory_space=pltpu.SMEM)
     in_vmem = pl.BlockSpec(memory_space=pltpu.VMEM)
+    in_hbm = pl.BlockSpec(memory_space=pltpu.MemorySpace.HBM)
+    pieces = 4
     blocks = pl.pallas_call(
         split_columns,
-        grid=(2,),
         out_shape=b16((parts, rows_here, width)),
-        in_specs=[pl.BlockSpec((1, rows_here // 2, parts * width), lambda k: (0, k, 0))],
-        out_specs=pl.BlockSpec((parts, rows_here // 2, width), lambda k: (0, k, 0)),
-        compiler_params=PARAMS,
+        in_specs=[in_hbm],
+        out_specs=in_hbm,
+        scratch_shapes=[
+            pltpu.VMEM((rows_here, parts * width), jnp.bfloat16),
+            pltpu.VMEM((parts, rows_here, width), jnp.bfloat16),
+            pltpu.SemaphoreType.DMA((pieces,)),
+            pltpu.SemaphoreType.DMA((pieces,)),
+        ],
+        compiler_params=pltpu.CompilerParams(vmem_limit_bytes=62 << 20),
     )(products)
     panel = lax.all_to_all(blocks, "blk", split_axis=0, concat_axis=0, tiled=True).reshape(rows, width)
-    factor, high, low = pl.pallas_call(
+    packed_rows = 5 * width // 8
+    factor, packed, high, low = pl.pallas_call(
         gram_factor,
-        out_shape=(f32((width, width)), b16((width, width)), b16((width, width))),
+        out_shape=(f32((width, width)), f32((packed_rows, width)), b16((width, width)), b16((width, width))),
         in_specs=[in_smem, in_smem, in_vmem],
-        out_specs=[in_vmem] * 3,
+        out_specs=[in_vmem] * 4,
         scratch_shapes=[pltpu.VMEM((width, 2 * width), jnp.float32)],
         compiler_params=PARAMS,
     )(compat[0], sizes, panel)
@@ -191,12 +242,13 @@
     sites = lax.axis_size("seg")
     accumulated, by = factor, 1
     while by < sites:
-        incoming = lax.ppermute(accumulated, "seg", [(i, i + by) for i in range(sites - by)])
-        accumulated = pl.pallas_call(
+        incoming = lax.ppermute(packed, "seg", [(i, (i + by) % sites) for i in range(sites)])
+        accumulated, packed = pl.pallas_call(
             functools.partial(chained, by),
-            out_shape=f32((width, width)),
+            out_shape=(f32((width, width)), f32((packed_rows, width))),
             in_specs=[in_vmem] * 2,
-            out_specs=in_vmem,
+            out_specs=[in_vmem] * 2,
+            scratch_shapes=[pltpu.VMEM((width, width), jnp.float32)],
             compiler_params=PARAMS,
         )(accumulated, incoming)
         by *= 2

time: 76.2 us -> 71.4 us (0.937)
  waiting for transfers between devices: 52.1 us -> 48.9 us
  local copies, waits for them, and re-layouts: 2.9 us -> 0.01 us
  Pallas kernels: 11.9 us -> 14.2 us
  starting transfers between devices: 7.66 us -> 6.8 us
    ppermute x1, waiting for transfers between devices: 5.51 us -> 2.3 us  [local(): lax.ppermute(packed, 'seg', [(i, (i + by) % sites) for i in range(sites)])]
    unnamed x6 -> x2, local copies, waits for them, and re-layouts: 2.9 us -> 0.01 us
    pallas_call x3, Pallas kernels: 8.34 us -> 10.6 us  [the longest x1 7.01 us: local(): pl.pallas_call(gram_factor, out_shape=(f32((width, width)), f32((packed_r...]
where the time goes in v4:
time: 71.4 us; the launch traced here: 71.2 us
  waiting for transfers between devices  48.9 us (68%)
  Pallas kernels  14.2 us (20%)
  starting transfers between devices  6.8 us (10%)
  between operations  1.3 us (2%)
    all_to_all x1, waiting for transfers between devices, local(): lax.all_to_all(blocks, 'blk', split_axis=0, concat_axis=0, tiled=True)  46.6 us
    pallas_call x1, Pallas kernels, local(): pl.pallas_call(gram_factor, out_shape=(f32((width, width)), f32((packed_r...  7.01 us
    all_to_all x1, starting transfers between devices, local(): lax.all_to_all(blocks, 'blk', split_axis=0, concat_axis=0, tiled=True)  6.25 us
    pallas_call x1, Pallas kernels, local(): pl.pallas_call(orthonormal_rows, grid=(steps,), out_shape=b16((1, rows, w...  3.56 us
    pallas_call x1, Pallas kernels, local(): pl.pallas_call(split_columns, out_shape=b16((parts, rows_here, width)), i...  2.46 us
    ppermute x1, waiting for transfers between devices, local(): lax.ppermute(packed, 'seg', [(i, (i + by) % sites) for i in range(sites)])  2.3 us
  transfers between devices with their start and end apart: 2, of which 2 were waited for; matrix products, arithmetic and copies ran while one was open for 0% of the time, Pallas kernels for 5%

profile of v4, /device:TPU:14, one launch (start us, length us, event | category | flops | bytes accessed | tf_op | source)
XLA Modules:
  0.0 71.2 jit_solution(2094689572678028442)
XLA Ops:
  0.6 2.5 %shard_map.50 = bf16[16,256,256]{2,1,0:T(8,128)(2,1)} custom-call(bf16[1,256,4096]{2,1,0:T(8,128)(2,1)} %src.1), custom_call_target="tpu_custom_call" | custom-call | tf_op jit(solution)/shard_map/pallas_call | solution.py:206
  3.1 0.0 copy-start
  3.1 6.3 %all-to-all-start = ((bf16[16,256,256]{2,1,0:T(8,128)(2,1)}), bf16[16,256,256]{2,1,0:T(8,128)(2,1)S(1)}, u32[]{:S(2)}, u32[]{:S(2)}) async-start(bf16[16,256,256]{2,1,0:T(8,128)(2,1)} %shard_map.50), calls=%async_computation | async-start | bytes 4194304 | tf_op jit(solution)/shard_map/all_to_all | solution.py:219
  10.0 46.6 %all-to-all-done = bf16[16,256,256]{2,1,0:T(8,128)(2,1)S(1)} async-done(((bf16[16,256,256]{2,1,0:T(8,128)(2,1)}), bf16[16,256,256]{2,1,0:T(8,128)(2,1)S(1)}, u32[]{:S(2)}, u32[]{:S(2)}) %all-to-all-start) | async-done | bytes 2097184 | tf_op jit(solution)/shard_map/all_to_all | solution.py:219
  56.6 0.0 copy-done
  56.6 7.0 %shard_map.51 = (f32[256,256]{1,0:T(8,128)S(1)}, f32[160,256]{1,0:T(8,128)S(1)}, bf16[256,256]{1,0:T(8,128)(2,1)S(1)}, bf16[256,256]{1,0:T(8,128)(2,1)S(1)}) custom-call(s32[1,16]{1,0:T(1,128)S(1)} %bitcast.5, s32[1,1]{1,0:T(1,128)S(6)} %copy.5.size, bf16[4096,256]{1,0:T(8,128)(2,1)S(1)} %bitcast.3), custom_call_target="tpu_custom_call" | custom-call | tf_op jit(solution)/shard_map/pallas_call | solution.py:221
  63.6 0.5 collective-permute-start
  64.2 3.6 %shard_map.52 = bf16[1,4096,256]{2,1,0:T(8,128)(2,1)} custom-call(s32[1,16]{1,0:T(1,128)S(1)} %bitcast.6, bf16[4096,256]{1,0:T(8,128)(2,1)S(1)} %bitcast.4, bf16[256,256]{1,0:T(8,128)(2,1)S(1)} %get-tuple-element.7.high, bf16[256,256]{1,0:T(8,128)(2,1)S(1)} %get-tuple-element.8.low), custom_call_target="tpu_custom_call" | custom-call | flops 1073741824 | bytes 4194304 | tf_op jit(solution)/shard_map/pallas_call | solution.py:231
  67.8 2.3 %collective-permute-done.incoming = f32[160,256]{1,0:T(8,128)S(1)} collective-permute-done((f32[160,256]{1,0:T(8,128)S(1)}, f32[160,256]{1,0:T(8,128)S(1)}, u32[]{:S(2)}, u32[]{:S(2)}) %collective-permute-start) | collective-permute-done | bytes 163872 | tf_op jit(solution)/shard_map/ppermute | solution.py:245
  70.1 1.1 %shard_map.53 = (f32[256,256]{1,0:T(8,128)}, f32[160,256]{1,0:T(8,128)}) custom-call(f32[256,256]{1,0:T(8,128)S(1)} %get-tuple-element.9.own, f32[160,256]{1,0:T(8,128)S(1)} %collective-permute-done.incoming), custom_call_target="tpu_custom_call" | custom-call | tf_op jit(solution)/shard_map/pallas_call | solution.py:246
Async XLA Ops:
  3.1 53.5 %copy-start = (s32[1,1,16]{2,1,0:T(1,128)S(1)}, s32[1,1,16]{2,1,0:T(1,128)}, u32[]{:S(2)}) copy-start(s32[1,1,16]{2,1,0:T(1,128)} %param.4) | copy-start | bytes 196
  3.1 53.5 %all-to-all-start = ((bf16[16,256,256]{2,1,0:T(8,128)(2,1)}), bf16[16,256,256]{2,1,0:T(8,128)(2,1)S(1)}, u32[]{:S(2)}, u32[]{:S(2)}) async-start(bf16[16,256,256]{2,1,0:T(8,128)(2,1)} %shard_map.50), calls=%async_computation | async-start | bytes 4194304 | tf_op jit(solution)/shard_map/all_to_all | solution.py:219
  63.6 6.4 %collective-permute-start = (f32[160,256]{1,0:T(8,128)S(1)}, f32[160,256]{1,0:T(8,128)S(1)}, u32[]{:S(2)}, u32[]{:S(2)}) collective-permute-start(f32[160,256]{1,0:T(8,128)S(1)} %get-tuple-element.10), channel_id=1, source_target_pairs={{0,16},{16,0},{1,17},{17,1},{2,18},{18,2},{3,19},{19,3},{4,20},{20... | collective-permute-start | bytes 491528 | tf_op jit(solution)/shard_map/ppermute | solution.py:245

commit v5 on v4

--- a/solution.py
+++ b/solution.py
@@ -1,5 +1,4 @@
 import functools
-import math
 
 import jax
 import jax.numpy as jnp
@@ -13,6 +12,7 @@
 PARAMS = pltpu.CompilerParams(vmem_limit_bytes=48 << 20)
 LANES = 128
 SUB = 8
+FAR, NEAR, LATE = 4, 3, 3
 
 
 def down(x, c):
@@ -23,22 +23,20 @@
     return jnp.broadcast_to(x[:, c : c + 1], (SUB, LANES))
 
 
-def split_columns(src, out, rows, blocks, arrived, sent):
-    count, total, width = out.shape
+def split_columns(src, *refs):
+    *outs, rows, arrived = refs
+    total, width = outs[0].shape
     parts = arrived.shape[0]
     each = total // parts
+    me = lax.axis_index("blk")
     cuts = [pl.ds(i * each, each) for i in range(parts)]
     reads = [pltpu.make_async_copy(src.at[0, cut], rows.at[cut], arrived.at[i]) for i, cut in enumerate(cuts)]
-    writes = [pltpu.make_async_copy(blocks.at[:, cut], out.at[:, cut], sent.at[i]) for i, cut in enumerate(cuts)]
     for read in reads:
         read.start()
-    for cut, read, write in zip(cuts, reads, writes):
+    for cut, read in zip(cuts, reads):
         read.wait()
-        for k in range(count):
-            blocks[k, cut, :] = rows[cut, k * width : (k + 1) * width]
-        write.start()
-    for write in writes:
-        write.wait()
+        for r, out in enumerate(outs):
+            out[cut, :] = rows[cut, pl.ds(pl.multiple_of((me ^ r) * width, width), width)]
 
 
 def outer(u, first, last):
@@ -137,15 +135,29 @@
     r[3 * q :, 3 * q :] = packed[q : 2 * q, :q]
 
 
-def gram_factor(compat, size, panel, r_out, packed_out, high_out, low_out, w):
-    rows, n = panel.shape
-    groups = compat.shape[1]
-    each = rows // groups
-    g = jnp.zeros((n, n), jnp.float32)
-    for k in range(groups):
-        block = panel[k * each : (k + 1) * each, :]
-        part = lax.dot_general(block, block, (((0,), (0,)), ((), ())), preferred_element_type=jnp.float32)
-        g = g + part * compat[0, k].astype(jnp.float32)
+def sender_allows(compat, r, each, rows):
+    sender = lax.axis_index("blk") ^ r
+    return compat[0, sender * each // (rows // compat.shape[1])].astype(jnp.float32)
+
+
+def gram_of(rounds, rows, compat, blocks):
+    total = None
+    for r, block in zip(rounds, blocks):
+        x = block[...]
+        part = lax.dot_general(x, x, (((0,), (0,)), ((), ())), preferred_element_type=jnp.float32)
+        part = part * sender_allows(compat, r, x.shape[0], rows)
+        total = part if total is None else total + part
+    return total
+
+
+def gram_part(rounds, rows, compat, *refs):
+    refs[-1][...] = gram_of(rounds, rows, compat, refs[:-1])
+
+
+def gram_factor(rounds, rows, compat, size, before, *refs):
+    *blocks, r_out, packed_out, high_out, low_out, w = refs
+    n = before.shape[0]
+    g = before[...] + gram_of(rounds, rows, compat, blocks)
     i = lax.broadcasted_iota(jnp.int32, (n, n), 0)
     j = lax.broadcasted_iota(jnp.int32, (n, n), 1)
     live = jnp.logical_and(i < size[0, 0], j < size[0, 0])
@@ -161,16 +173,22 @@
     low_out[...] = (inverse - high.astype(jnp.float32)).astype(jnp.bfloat16)
 
 
-def orthonormal_rows(compat, panel, high, low, out):
+def orthonormal_rows(rounds, rows, compat, high, low, *refs):
+    *blocks, out, results, sent = refs
     dims = (((1,), (1,)), ((), ()))
-    steps, groups = pl.num_programs(0), compat.shape[1]
-    at = pl.program_id(0) * (groups // steps)
-    each = panel.shape[0] * steps // groups
-    for k in range(groups // steps):
-        block = panel[k * each : (k + 1) * each, :]
-        q = lax.dot_general(block, high[...], dims, preferred_element_type=jnp.float32)
-        q = q + lax.dot_general(block, low[...], dims, preferred_element_type=jnp.float32)
-        out[0, k * each : (k + 1) * each, :] = (q * compat[0, at + k].astype(jnp.float32)).astype(jnp.bfloat16)
+    each = blocks[0].shape[0]
+    me = lax.axis_index("blk")
+    copies = []
+    for i, (r, block) in enumerate(zip(rounds, blocks)):
+        x = block[...]
+        q = lax.dot_general(x, high[...], dims, preferred_element_type=jnp.float32)
+        q = q + lax.dot_general(x, low[...], dims, preferred_element_type=jnp.float32)
+        results[i] = (q * sender_allows(compat, r, each, rows)).astype(jnp.bfloat16)
+        place = pl.ds(pl.multiple_of((me ^ r) * each, each), each)
+        copies.append(pltpu.make_async_copy(results.at[i], out.at[0, place], sent.at[i]))
+        copies[-1].start()
+    for copy in copies:
+        copy.wait()
 
 
 def chained(by, own, incoming, out, packed_out, before):
@@ -196,7 +214,6 @@
     parts = lax.axis_size("blk")
     rows_here, width = products.shape[1], products.shape[2] // parts
     rows = rows_here * parts
-    groups = compat.shape[2]
     f32 = functools.partial(jax.ShapeDtypeStruct, dtype=jnp.float32)
     b16 = functools.partial(jax.ShapeDtypeStruct, dtype=jnp.bfloat16)
     in_smem = pl.BlockSpec(memory_space=pltpu.SMEM)
@@ -205,40 +222,57 @@
     pieces = 4
     blocks = pl.pallas_call(
         split_columns,
-        out_shape=b16((parts, rows_here, width)),
+        out_shape=[b16((rows_here, width))] * parts,
         in_specs=[in_hbm],
+        out_specs=[in_vmem] * parts,
+        scratch_shapes=[
+            pltpu.VMEM((rows_here, parts * width), jnp.bfloat16),
+            pltpu.SemaphoreType.DMA((pieces,)),
+        ],
+        compiler_params=PARAMS,
+    )(products)
+    half, quarter = parts // 2, parts // 4
+    far = [r for pair in zip(range(half, half + quarter), range(half + quarter, parts)) for r in pair]
+    near = [*range(quarter, half), *range(1, quarter)]
+    got = {0: blocks[0]}
+    for order, window in ((far, FAR), (near, NEAR)):
+        for i, r in enumerate(order):
+            block = blocks[r]
+            if i >= window:
+                block, _ = lax.optimization_barrier((block, got[order[i - window]]))
+            got[r] = lax.ppermute(block, "blk", [(k, k ^ r) for k in range(parts)])
+    early, late = [0, *near, *far[: -LATE]], far[-LATE:]
+    partial = pl.pallas_call(
+        functools.partial(gram_part, early, rows),
+        out_shape=f32((width, width)),
+        in_specs=[in_smem] + [in_vmem] * len(early),
+        out_specs=in_vmem,
+        compiler_params=PARAMS,
+    )(compat[0], *[got[r] for r in early])
+    packed_rows = 5 * width // 8
+    factor, packed, high, low = pl.pallas_call(
+        functools.partial(gram_factor, late, rows),
+        out_shape=(f32((width, width)), f32((packed_rows, width)), b16((width, width)), b16((width, width))),
+        in_specs=[in_smem, in_smem] + [in_vmem] * (1 + len(late)),
+        out_specs=[in_vmem] * 4,
+        scratch_shapes=[pltpu.VMEM((width, 2 * width), jnp.float32)],
+        compiler_params=PARAMS,
+    )(compat[0], sizes, partial, *[got[r] for r in late])
+    rounds = sorted(got)
+    ortho = pl.pallas_call(
+        functools.partial(orthonormal_rows, rounds, rows),
+        out_shape=b16((1, rows, width)),
+        in_specs=[in_smem] + [in_vmem] * (2 + parts),
         out_specs=in_hbm,
         scratch_shapes=[
-            pltpu.VMEM((rows_here, parts * width), jnp.bfloat16),
             pltpu.VMEM((parts, rows_here, width), jnp.bfloat16),
-            pltpu.SemaphoreType.DMA((pieces,)),
-            pltpu.SemaphoreType.DMA((pieces,)),
+            pltpu.SemaphoreType.DMA((parts,)),
         ],
-        compiler_params=pltpu.CompilerParams(vmem_limit_bytes=62 << 20),
-    )(products)
-    panel = lax.all_to_all(blocks, "blk", split_axis=0, concat_axis=0, tiled=True).reshape(rows, width)
-    packed_rows = 5 * width // 8
-    factor, packed, high, low = pl.pallas_call(
-        gram_factor,
-        out_shape=(f32((width, width)), f32((packed_rows, width)), b16((width, width)), b16((width, width))),
-        in_specs=[in_smem, in_smem, in_vmem],
-        out_specs=[in_vmem] * 4,
-        scratch_shapes=[pltpu.VMEM((width, 2 * width), jnp.float32)],
-        compiler_params=PARAMS,
-    )(compat[0], sizes, panel)
-    steps = math.gcd(groups, 4)
-    whole = pl.BlockSpec((width, width), lambda k: (0, 0))
-    ortho = pl.pallas_call(
-        orthonormal_rows,
-        grid=(steps,),
-        out_shape=b16((1, rows, width)),
-        in_specs=[in_smem, pl.BlockSpec((rows // steps, width), lambda k: (k, 0)), whole, whole],
-        out_specs=pl.BlockSpec((1, rows // steps, width), lambda k: (0, k, 0)),
         compiler_params=PARAMS,
         cost_estimate=pl.CostEstimate(
             flops=4 * rows * width * width, bytes_accessed=4 * rows * width, transcendentals=0
         ),
-    )(compat[0], panel, high, low)
+    )(compat[0], high, low, *[got[r] for r in rounds])
     sites = lax.axis_size("seg")
     accumulated, by = factor, 1
     while by < sites:

time: 71.4 us -> 67.2 us (0.941)
  waiting for transfers between devices: 48.9 us -> 32.4 us
  starting transfers between devices: 6.8 us -> 19.6 us
  Pallas kernels: 14.2 us -> 12 us
  local copies, waits for them, and re-layouts: 0.01 us -> 1.59 us
    all_to_all x1 -> x0, waiting for transfers between devices: 46.6 us -> none  [local(): lax.all_to_all(blocks, 'blk', split_axis=0, concat_axis=0, tiled=True)]
    ppermute x0 -> x15, waiting for transfers between devices: none -> 29.5 us  [local(): got[r] = lax.ppermute(block, 'blk', [(k, k ^ r) for k in range(parts)])]
    ppermute x0 -> x15, starting transfers between devices: none -> 19.1 us  [local(): got[r] = lax.ppermute(block, 'blk', [(k, k ^ r) for k in range(parts)])]
    all_to_all x1 -> x0, starting transfers between devices: 6.25 us -> none  [local(): lax.all_to_all(blocks, 'blk', split_axis=0, concat_axis=0, tiled=True)]
    pallas_call x3 -> x4, Pallas kernels: 13 us -> 10.9 us  [the longest x1 6.55 us: local(): pl.pallas_call(functools.partial(gram_factor, late, rows), out_shape=(f32...]
    unnamed x2 -> x4, local copies, waits for them, and re-layouts: 0.01 us -> 1.59 us
  transfers between devices with their start and end apart: 2 -> 16, of which waited for: 2 -> 10; matrix products, arithmetic and copies ran while one was open for 0% -> 0% of each run, Pallas kernels for 5% -> 6%
where the time goes in v5:
time: 67.2 us; the launch traced here: 67.1 us
  waiting for transfers between devices  32.4 us (48%)
  starting transfers between devices  19.6 us (29%)
  Pallas kernels  12 us (18%)
  local copies, waits for them, and re-layouts  1.59 us (2%)
  between operations  1.35 us (2%)
    ppermute x15, waiting for transfers between devices, local(): got[r] = lax.ppermute(block, 'blk', [(k, k ^ r) for k in range(parts)])  29.5 us
    ppermute x15, starting transfers between devices, local(): got[r] = lax.ppermute(block, 'blk', [(k, k ^ r) for k in range(parts)])  19.1 us
    pallas_call x1, Pallas kernels, local(): pl.pallas_call(functools.partial(gram_factor, late, rows), out_shape=(f32...  6.55 us
    ppermute x1, waiting for transfers between devices, local(): lax.ppermute(packed, 'seg', [(i, (i + by) % sites) for i in range(sites)])  2.99 us
    pallas_call x1, Pallas kernels, local(): pl.pallas_call(functools.partial(orthonormal_rows, rounds, rows), out_sha...  2.69 us
    unnamed x4, local copies, waits for them, and re-layouts  1.59 us
  transfers between devices with their start and end apart: 16, of which 10 were waited for; matrix products, arithmetic and copies ran while one was open for 0% of the time, Pallas kernels for 6%

profile of v5, /device:TPU:14, one launch (start us, length us, event | category | flops | bytes accessed | tf_op | source)
XLA Modules:
  0.0 67.1 jit_solution(4649398803510281577)
XLA Ops:
  0.6 0.0 copy-start
  0.6 1.6 %copy-done = bf16[1,256,4096]{2,1,0:T(8,128)(2,1)S(1)} copy-done((bf16[1,256,4096]{2,1,0:T(8,128)(2,1)S(1)}, bf16[1,256,4096]{2,1,0:T(8,128)(2,1)}, u32[]{:S(2)}) %copy-start) | copy-done | bytes 2097176
  2.2 0.0 copy-start.1
  2.2 0.5 shard_map.50
  2.7 0.5 collective-permute-start
  3.2 2.6 %collective-permute-start.7 = (bf16[256,256]{1,0:T(8,128)(2,1)S(1)}, bf16[256,256]{1,0:T(8,128)(2,1)S(1)}, u32[]{:S(2)}, u32[]{:S(2)}) collective-permute-start(bf16[256,256]{1,0:T(8,128)(2,1)S(1)} %get-tuple-element.43), channel_id=1, source_target_pairs={{0,8},{1,9},{2,10},{3,11},{4,12},{5,13},{6,14},{7,15},{8,0},{9,1},... | collective-permute-start | bytes 393224 | tf_op jit(solution)/shard_map/ppermute | solution.py:243
  5.8 1.5 %collective-permute-start.2 = (bf16[256,256]{1,0:T(8,128)(2,1)S(1)}, bf16[256,256]{1,0:T(8,128)(2,1)S(1)}, u32[]{:S(2)}, u32[]{:S(2)}) collective-permute-start(bf16[256,256]{1,0:T(8,128)(2,1)S(1)} %get-tuple-element.34), channel_id=1, source_target_pairs={{0,6},{1,7},{2,4},{3,5},{4,2},{5,3},{6,0},{7,1},{8,14},{9,15},{10,... | collective-permute-start | bytes 393224 | tf_op jit(solution)/shard_map/ppermute | solution.py:243
  7.3 0.0 collective-permute-start.1
  7.3 0.6 collective-permute-start.10
  7.9 0.5 collective-permute-done.refs_1_.refs_4_
  8.5 2.3 %collective-permute-start.9 = (bf16[256,256]{1,0:T(8,128)(2,1)S(1)}, bf16[256,256]{1,0:T(8,128)(2,1)S(1)}, u32[]{:S(2)}, u32[]{:S(2)}) collective-permute-start(bf16[256,256]{1,0:T(8,128)(2,1)S(1)} %get-tuple-element.45), channel_id=1, source_target_pairs={{0,9},{1,8},{2,11},{3,10},{4,13},{5,12},{6,15},{7,14},{8,1},{9,0},... | collective-permute-start | bytes 393224 | tf_op jit(solution)/shard_map/ppermute | solution.py:243
  10.7 2.2 %collective-permute-done.7.refs_8_ = bf16[256,256]{1,0:T(8,128)(2,1)S(1)} collective-permute-done((bf16[256,256]{1,0:T(8,128)(2,1)S(1)}, bf16[256,256]{1,0:T(8,128)(2,1)S(1)}, u32[]{:S(2)}, u32[]{:S(2)}) %collective-permute-start.7) | collective-permute-done | bytes 131104 | tf_op jit(solution)/shard_map/ppermute | solution.py:243
  13.0 0.3 collective-permute-start.8
  13.3 1.3 %collective-permute-done.2.refs_3_.refs_6_ = bf16[256,256]{1,0:T(8,128)(2,1)S(1)} collective-permute-done((bf16[256,256]{1,0:T(8,128)(2,1)S(1)}, bf16[256,256]{1,0:T(8,128)(2,1)S(1)}, u32[]{:S(2)}, u32[]{:S(2)}) %collective-permute-start.2) | collective-permute-done | bytes 131104 | tf_op jit(solution)/shard_map/ppermute | solution.py:243
  14.6 0.0 collective-permute-start.3
  14.6 5.0 %collective-permute-done.1.refs_2_.refs_5_ = bf16[256,256]{1,0:T(8,128)(2,1)S(1)} collective-permute-done((bf16[256,256]{1,0:T(8,128)(2,1)S(1)}, bf16[256,256]{1,0:T(8,128)(2,1)S(1)}, u32[]{:S(2)}, u32[]{:S(2)}) %collective-permute-start.1) | collective-permute-done | bytes 131104 | tf_op jit(solution)/shard_map/ppermute | solution.py:243
  19.6 2.0 %collective-permute-start.11 = (bf16[256,256]{1,0:T(8,128)(2,1)S(1)}, bf16[256,256]{1,0:T(8,128)(2,1)S(1)}, u32[]{:S(2)}, u32[]{:S(2)}) collective-permute-start(bf16[256,256]{1,0:T(8,128)(2,1)S(1)} %get-tuple-element.48), channel_id=1, source_target_pairs={{0,10},{1,11},{2,8},{3,9},{4,14},{5,15},{6,12},{7,13},{8,2},{9,3},... | collective-permute-start | bytes 393224 | tf_op jit(solution)/shard_map/ppermute | solution.py:243
  21.6 0.0 collective-permute-done.10.refs_11_.refs_13_
  21.6 1.5 %collective-permute-start.5 = (bf16[256,256]{1,0:T(8,128)(2,1)S(1)}, bf16[256,256]{1,0:T(8,128)(2,1)S(1)}, u32[]{:S(2)}, u32[]{:S(2)}) collective-permute-start(bf16[256,256]{1,0:T(8,128)(2,1)S(1)} %get-tuple-element.40), channel_id=1, source_target_pairs={{0,2},{1,3},{2,0},{3,1},{4,6},{5,7},{6,4},{7,5},{8,10},{9,11},{10,... | collective-permute-start | bytes 393224 | tf_op jit(solution)/shard_map/ppermute | solution.py:243
  23.2 1.5 %collective-permute-done.9.refs_10_.refs_9_ = bf16[256,256]{1,0:T(8,128)(2,1)S(1)} collective-permute-done((bf16[256,256]{1,0:T(8,128)(2,1)S(1)}, bf16[256,256]{1,0:T(8,128)(2,1)S(1)}, u32[]{:S(2)}, u32[]{:S(2)}) %collective-permute-start.9) | collective-permute-done | bytes 131104 | tf_op jit(solution)/shard_map/ppermute | solution.py:243
  24.7 1.7 %collective-permute-start.4 = (bf16[256,256]{1,0:T(8,128)(2,1)S(1)}, bf16[256,256]{1,0:T(8,128)(2,1)S(1)}, u32[]{:S(2)}, u32[]{:S(2)}) collective-permute-start(bf16[256,256]{1,0:T(8,128)(2,1)S(1)} %get-tuple-element.38), channel_id=1, source_target_pairs={{0,1},{1,0},{2,3},{3,2},{4,5},{5,4},{6,7},{7,6},{8,9},{9,8},{10,11... | collective-permute-start | bytes 393224 | tf_op jit(solution)/shard_map/ppermute | solution.py:243
  26.4 8.2 %collective-permute-done.8.refs_9_.refs_12_ = bf16[256,256]{1,0:T(8,128)(2,1)S(1)} collective-permute-done((bf16[256,256]{1,0:T(8,128)(2,1)S(1)}, bf16[256,256]{1,0:T(8,128)(2,1)S(1)}, u32[]{:S(2)}, u32[]{:S(2)}) %collective-permute-start.8) | collective-permute-done | bytes 131104 | tf_op jit(solution)/shard_map/ppermute | solution.py:243
  34.6 0.0 collective-permute-start.14
  34.6 0.0 collective-permute-done.3.refs_4_.refs_7_
  34.6 2.5 %collective-permute-start.6 = (bf16[256,256]{1,0:T(8,128)(2,1)S(1)}, bf16[256,256]{1,0:T(8,128)(2,1)S(1)}, u32[]{:S(2)}, u32[]{:S(2)}) collective-permute-start(bf16[256,256]{1,0:T(8,128)(2,1)S(1)} %get-tuple-element.42), channel_id=1, source_target_pairs={{0,3},{1,2},{2,1},{3,0},{4,7},{5,6},{6,5},{7,4},{8,11},{9,10},{10,... | collective-permute-start | bytes 393224 | tf_op jit(solution)/shard_map/ppermute | solution.py:243
  37.1 0.0 collective-permute-done.11.refs_12_.refs_10_
  37.1 3.3 %collective-permute-start.13 = (bf16[256,256]{1,0:T(8,128)(2,1)S(1)}, bf16[256,256]{1,0:T(8,128)(2,1)S(1)}, u32[]{:S(2)}, u32[]{:S(2)}) collective-permute-start(bf16[256,256]{1,0:T(8,128)(2,1)S(1)} %get-tuple-element.52), channel_id=1, source_target_pairs={{0,11},{1,10},{2,9},{3,8},{4,15},{5,14},{6,13},{7,12},{8,3},{9,2},... | collective-permute-start | bytes 393224 | tf_op jit(solution)/shard_map/ppermute | solution.py:243
  40.4 0.0 collective-permute-done.5.refs_6_.refs_2_
  40.4 0.2 collective-permute-start.12
  41.3 0.0 collective-permute-done.4.refs_5_.refs_1_
  41.3 5.2 %collective-permute-done.6.refs_7_.refs_3_ = bf16[256,256]{1,0:T(8,128)(2,1)S(1)} collective-permute-done((bf16[256,256]{1,0:T(8,128)(2,1)S(1)}, bf16[256,256]{1,0:T(8,128)(2,1)S(1)}, u32[]{:S(2)}, u32[]{:S(2)}) %collective-permute-start.6) | collective-permute-done | bytes 131104 | tf_op jit(solution)/shard_map/ppermute | solution.py:243
  46.5 0.0 copy-done.1
  46.5 1.2 %shard_map.51.before = f32[256,256]{1,0:T(8,128)S(1)} custom-call(s32[1,16]{1,0:T(1,128)S(1)} %bitcast.2, bf16[256,256]{1,0:T(8,128)(2,1)S(1)} %get-tuple-element.31.refs_0_, bf16[256,256]{1,0:T(8,128)(2,1)S(1)} %collective-permute-done.refs_1_.refs_4_, bf16[256,256]{1,0:T(8,128)(2,1)S(1)} %collective-permute-done.1.refs_2_.refs_5_, ...), custom_call_target="tpu_custom_call" | custom-call | tf_op jit(solution)/shard_map/pallas_call | solution.py:245
  47.7 0.0 collective-permute-done.14.refs_2_.refs_15_
  47.8 0.2 collective-permute-done.13.refs_1_.refs_11_
  47.9 5.2 %collective-permute-done.12.refs_0_.refs_14_ = bf16[256,256]{1,0:T(8,128)(2,1)S(1)} collective-permute-done((bf16[256,256]{1,0:T(8,128)(2,1)S(1)}, bf16[256,256]{1,0:T(8,128)(2,1)S(1)}, u32[]{:S(2)}, u32[]{:S(2)}) %collective-permute-start.12) | collective-permute-done | bytes 131104 | tf_op jit(solution)/shard_map/ppermute | solution.py:243
  53.1 6.6 %shard_map.52 = (f32[256,256]{1,0:T(8,128)S(1)}, f32[160,256]{1,0:T(8,128)S(1)}, bf16[256,256]{1,0:T(8,128)(2,1)S(1)}, bf16[256,256]{1,0:T(8,128)(2,1)S(1)}) custom-call(s32[1,16]{1,0:T(1,128)S(1)} %bitcast.3, s32[1,1]{1,0:T(1,128)S(6)} %copy.5.size, f32[256,256]{1,0:T(8,128)S(1)} %shard_map.51.before, ...), custom_call_target="tpu_custom_call" | custom-call | tf_op jit(solution)/shard_map/pallas_call | solution.py:253
  59.7 0.6 collective-permute-start.15
  60.2 2.7 %shard_map.53 = bf16[1,4096,256]{2,1,0:T(8,128)(2,1)} custom-call(s32[1,16]{1,0:T(1,128)S(1)} %bitcast.4, bf16[256,256]{1,0:T(8,128)(2,1)S(1)} %get-tuple-element.55.high, bf16[256,256]{1,0:T(8,128)(2,1)S(1)} %get-tuple-element.56.low, bf16[256,256]{1,0:T(8,128)(2,1)S(1)} %get-tuple-element.31.refs_0_, ...), custom_call_target="tpu_custom_call" | custom-call | flops 1073741824 | bytes 4194304 | tf_op jit(solution)/shard_map/pallas_call | solution.py:262
  62.9 3.0 %collective-permute-done.15.incoming = f32[160,256]{1,0:T(8,128)S(1)} collective-permute-done((f32[160,256]{1,0:T(8,128)S(1)}, f32[160,256]{1,0:T(8,128)S(1)}, u32[]{:S(2)}, u32[]{:S(2)}) %collective-permute-start.15) | collective-permute-done | bytes 163872 | tf_op jit(solution)/shard_map/ppermute | solution.py:279
  65.9 1.1 %shard_map.54 = (f32[256,256]{1,0:T(8,128)}, f32[160,256]{1,0:T(8,128)}) custom-call(f32[256,256]{1,0:T(8,128)S(1)} %get-tuple-element.57.own, f32[160,256]{1,0:T(8,128)S(1)} %collective-permute-done.15.incoming), custom_call_target="tpu_custom_call" | custom-call | tf_op jit(solution)/shard_map/pallas_call | solution.py:280
Async XLA Ops:
  0.6 1.6 %copy-start = (bf16[1,256,4096]{2,1,0:T(8,128)(2,1)S(1)}, bf16[1,256,4096]{2,1,0:T(8,128)(2,1)}, u32[]{:S(2)}) copy-start(bf16[1,256,4096]{2,1,0:T(8,128)(2,1)} %src.1) | copy-start | bytes 6291460
  2.2 44.3 %copy-start.1 = (s32[1,1,16]{2,1,0:T(1,128)S(1)}, s32[1,1,16]{2,1,0:T(1,128)}, u32[]{:S(2)}) copy-start(s32[1,1,16]{2,1,0:T(1,128)} %param.4) | copy-start | bytes 196
  2.7 5.8 %collective-permute-start = (bf16[256,256]{1,0:T(8,128)(2,1)S(1)}, bf16[256,256]{1,0:T(8,128)(2,1)S(1)}, u32[]{:S(2)}, u32[]{:S(2)}) collective-permute-start(bf16[256,256]{1,0:T(8,128)(2,1)S(1)} %get-tuple-element.32), channel_id=1, source_target_pairs={{0,4},{1,5},{2,6},{3,7},{4,0},{5,1},{6,2},{7,3},{8,12},{9,13},{10,... | collective-permute-start | bytes 393224 | tf_op jit(solution)/shard_map/ppermute | solution.py:243
  3.2 9.8 %collective-permute-start.7 = (bf16[256,256]{1,0:T(8,128)(2,1)S(1)}, bf16[256,256]{1,0:T(8,128)(2,1)S(1)}, u32[]{:S(2)}, u32[]{:S(2)}) collective-permute-start(bf16[256,256]{1,0:T(8,128)(2,1)S(1)} %get-tuple-element.43), channel_id=1, source_target_pairs={{0,8},{1,9},{2,10},{3,11},{4,12},{5,13},{6,14},{7,15},{8,0},{9,1},... | collective-permute-start | bytes 393224 | tf_op jit(solution)/shard_map/ppermute | solution.py:243
  5.8 8.8 %collective-permute-start.2 = (bf16[256,256]{1,0:T(8,128)(2,1)S(1)}, bf16[256,256]{1,0:T(8,128)(2,1)S(1)}, u32[]{:S(2)}, u32[]{:S(2)}) collective-permute-start(bf16[256,256]{1,0:T(8,128)(2,1)S(1)} %get-tuple-element.34), channel_id=1, source_target_pairs={{0,6},{1,7},{2,4},{3,5},{4,2},{5,3},{6,0},{7,1},{8,14},{9,15},{10,... | collective-permute-start | bytes 393224 | tf_op jit(solution)/shard_map/ppermute | solution.py:243
  7.3 12.3 %collective-permute-start.1 = (bf16[256,256]{1,0:T(8,128)(2,1)S(1)}, bf16[256,256]{1,0:T(8,128)(2,1)S(1)}, u32[]{:S(2)}, u32[]{:S(2)}) collective-permute-start(bf16[256,256]{1,0:T(8,128)(2,1)S(1)} %get-tuple-element.33), channel_id=1, source_target_pairs={{0,5},{1,4},{2,7},{3,6},{4,1},{5,0},{6,3},{7,2},{8,13},{9,12},{10,... | collective-permute-start | bytes 393224 | tf_op jit(solution)/shard_map/ppermute | solution.py:243
  7.3 14.3 %collective-permute-start.10 = (bf16[256,256]{1,0:T(8,128)(2,1)S(1)}, bf16[256,256]{1,0:T(8,128)(2,1)S(1)}, u32[]{:S(2)}, u32[]{:S(2)}) collective-permute-start(bf16[256,256]{1,0:T(8,128)(2,1)S(1)} %get-tuple-element.46), channel_id=1, source_target_pairs={{0,13},{1,12},{2,15},{3,14},{4,9},{5,8},{6,11},{7,10},{8,5},{9,4},... | collective-permute-start | bytes 393224 | tf_op jit(solution)/shard_map/ppermute | solution.py:243
  8.5 16.2 %collective-permute-start.9 = (bf16[256,256]{1,0:T(8,128)(2,1)S(1)}, bf16[256,256]{1,0:T(8,128)(2,1)S(1)}, u32[]{:S(2)}, u32[]{:S(2)}) collective-permute-start(bf16[256,256]{1,0:T(8,128)(2,1)S(1)} %get-tuple-element.45), channel_id=1, source_target_pairs={{0,9},{1,8},{2,11},{3,10},{4,13},{5,12},{6,15},{7,14},{8,1},{9,0},... | collective-permute-start | bytes 393224 | tf_op jit(solution)/shard_map/ppermute | solution.py:243
  13.0 21.6 %collective-permute-start.8 = (bf16[256,256]{1,0:T(8,128)(2,1)S(1)}, bf16[256,256]{1,0:T(8,128)(2,1)S(1)}, u32[]{:S(2)}, u32[]{:S(2)}) collective-permute-start(bf16[256,256]{1,0:T(8,128)(2,1)S(1)} %get-tuple-element.44), channel_id=1, source_target_pairs={{0,12},{1,13},{2,14},{3,15},{4,8},{5,9},{6,10},{7,11},{8,4},{9,5},... | collective-permute-start | bytes 393224 | tf_op jit(solution)/shard_map/ppermute | solution.py:243
  14.6 20.0 %collective-permute-start.3 = (bf16[256,256]{1,0:T(8,128)(2,1)S(1)}, bf16[256,256]{1,0:T(8,128)(2,1)S(1)}, u32[]{:S(2)}, u32[]{:S(2)}) collective-permute-start(bf16[256,256]{1,0:T(8,128)(2,1)S(1)} %get-tuple-element.36), channel_id=1, source_target_pairs={{0,7},{1,6},{2,5},{3,4},{4,3},{5,2},{6,1},{7,0},{8,15},{9,14},{10,... | collective-permute-start | bytes 393224 | tf_op jit(solution)/shard_map/ppermute | solution.py:243
  19.6 17.5 %collective-permute-start.11 = (bf16[256,256]{1,0:T(8,128)(2,1)S(1)}, bf16[256,256]{1,0:T(8,128)(2,1)S(1)}, u32[]{:S(2)}, u32[]{:S(2)}) collective-permute-start(bf16[256,256]{1,0:T(8,128)(2,1)S(1)} %get-tuple-element.48), channel_id=1, source_target_pairs={{0,10},{1,11},{2,8},{3,9},{4,14},{5,15},{6,12},{7,13},{8,2},{9,3},... | collective-permute-start | bytes 393224 | tf_op jit(solution)/shard_map/ppermute | solution.py:243
  21.6 18.8 %collective-permute-start.5 = (bf16[256,256]{1,0:T(8,128)(2,1)S(1)}, bf16[256,256]{1,0:T(8,128)(2,1)S(1)}, u32[]{:S(2)}, u32[]{:S(2)}) collective-permute-start(bf16[256,256]{1,0:T(8,128)(2,1)S(1)} %get-tuple-element.40), channel_id=1, source_target_pairs={{0,2},{1,3},{2,0},{3,1},{4,6},{5,7},{6,4},{7,5},{8,10},{9,11},{10,... | collective-permute-start | bytes 393224 | tf_op jit(solution)/shard_map/ppermute | solution.py:243
  24.7 16.6 %collective-permute-start.4 = (bf16[256,256]{1,0:T(8,128)(2,1)S(1)}, bf16[256,256]{1,0:T(8,128)(2,1)S(1)}, u32[]{:S(2)}, u32[]{:S(2)}) collective-permute-start(bf16[256,256]{1,0:T(8,128)(2,1)S(1)} %get-tuple-element.38), channel_id=1, source_target_pairs={{0,1},{1,0},{2,3},{3,2},{4,5},{5,4},{6,7},{7,6},{8,9},{9,8},{10,11... | collective-permute-start | bytes 393224 | tf_op jit(solution)/shard_map/ppermute | solution.py:243
  34.6 13.1 %collective-permute-start.14 = (bf16[256,256]{1,0:T(8,128)(2,1)S(1)}, bf16[256,256]{1,0:T(8,128)(2,1)S(1)}, u32[]{:S(2)}, u32[]{:S(2)}) collective-permute-start(bf16[256,256]{1,0:T(8,128)(2,1)S(1)} %get-tuple-element.54), channel_id=1, source_target_pairs={{0,15},{1,14},{2,13},{3,12},{4,11},{5,10},{6,9},{7,8},{8,7},{9,6},... | collective-permute-start | bytes 393224 | tf_op jit(solution)/shard_map/ppermute | solution.py:243
  34.6 11.9 %collective-permute-start.6 = (bf16[256,256]{1,0:T(8,128)(2,1)S(1)}, bf16[256,256]{1,0:T(8,128)(2,1)S(1)}, u32[]{:S(2)}, u32[]{:S(2)}) collective-permute-start(bf16[256,256]{1,0:T(8,128)(2,1)S(1)} %get-tuple-element.42), channel_id=1, source_target_pairs={{0,3},{1,2},{2,1},{3,0},{4,7},{5,6},{6,5},{7,4},{8,11},{9,10},{10,... | collective-permute-start | bytes 393224 | tf_op jit(solution)/shard_map/ppermute | solution.py:243
  37.1 10.8 %collective-permute-start.13 = (bf16[256,256]{1,0:T(8,128)(2,1)S(1)}, bf16[256,256]{1,0:T(8,128)(2,1)S(1)}, u32[]{:S(2)}, u32[]{:S(2)}) collective-permute-start(bf16[256,256]{1,0:T(8,128)(2,1)S(1)} %get-tuple-element.52), channel_id=1, source_target_pairs={{0,11},{1,10},{2,9},{3,8},{4,15},{5,14},{6,13},{7,12},{8,3},{9,2},... | collective-permute-start | bytes 393224 | tf_op jit(solution)/shard_map/ppermute | solution.py:243
  40.4 12.7 %collective-permute-start.12 = (bf16[256,256]{1,0:T(8,128)(2,1)S(1)}, bf16[256,256]{1,0:T(8,128)(2,1)S(1)}, u32[]{:S(2)}, u32[]{:S(2)}) collective-permute-start(bf16[256,256]{1,0:T(8,128)(2,1)S(1)} %get-tuple-element.50), channel_id=1, source_target_pairs={{0,14},{1,15},{2,12},{3,13},{4,10},{5,11},{6,8},{7,9},{8,6},{9,7},... | collective-permute-start | bytes 393224 | tf_op jit(solution)/shard_map/ppermute | solution.py:243
  59.7 6.2 %collective-permute-start.15 = (f32[160,256]{1,0:T(8,128)S(1)}, f32[160,256]{1,0:T(8,128)S(1)}, u32[]{:S(2)}, u32[]{:S(2)}) collective-permute-start(f32[160,256]{1,0:T(8,128)S(1)} %get-tuple-element.58), channel_id=1, source_target_pairs={{0,16},{16,0},{1,17},{17,1},{2,18},{18,2},{3,19},{19,3},{4,20},{20... | collective-permute-start | bytes 491528 | tf_op jit(solution)/shard_map/ppermute | solution.py:279

commit v6 on v5

--- a/solution.py
+++ b/solution.py
@@ -12,7 +12,7 @@
 PARAMS = pltpu.CompilerParams(vmem_limit_bytes=48 << 20)
 LANES = 128
 SUB = 8
-FAR, NEAR, LATE = 4, 3, 3
+FAR, NEAR, LATE, AHEAD = 5, 3, 3, 3
 
 
 def down(x, c):
@@ -23,11 +23,12 @@
     return jnp.broadcast_to(x[:, c : c + 1], (SUB, LANES))
 
 
-def split_columns(src, *refs):
+def split_columns(wanted, src, *refs):
     *outs, rows, arrived = refs
-    total, width = outs[0].shape
+    total = rows.shape[0]
     parts = arrived.shape[0]
     each = total // parts
+    width = rows.shape[1] // lax.axis_size("blk")
     me = lax.axis_index("blk")
     cuts = [pl.ds(i * each, each) for i in range(parts)]
     reads = [pltpu.make_async_copy(src.at[0, cut], rows.at[cut], arrived.at[i]) for i, cut in enumerate(cuts)]
@@ -35,8 +36,9 @@
         read.start()
     for cut, read in zip(cuts, reads):
         read.wait()
-        for r, out in enumerate(outs):
-            out[cut, :] = rows[cut, pl.ds(pl.multiple_of((me ^ r) * width, width), width)]
+        for (r, first, count), out in zip(wanted, outs):
+            at = pl.multiple_of((me ^ r) * width + first, LANES)
+            out[cut, :] = rows[cut, pl.ds(at, count)]
 
 
 def outer(u, first, last):
@@ -140,12 +142,14 @@
     return compat[0, sender * each // (rows // compat.shape[1])].astype(jnp.float32)
 
 
-def gram_of(rounds, rows, compat, blocks):
+def product_t(x, y):
+    return lax.dot_general(x, y, (((0,), (0,)), ((), ())), preferred_element_type=jnp.float32)
+
+
+def gram_of(rounds, rows, compat, blocks, others=None):
     total = None
-    for r, block in zip(rounds, blocks):
-        x = block[...]
-        part = lax.dot_general(x, x, (((0,), (0,)), ((), ())), preferred_element_type=jnp.float32)
-        part = part * sender_allows(compat, r, x.shape[0], rows)
+    for r, block, other in zip(rounds, blocks, blocks if others is None else others):
+        part = product_t(block[...], other[...]) * sender_allows(compat, r, block.shape[0], rows)
         total = part if total is None else total + part
     return total
 
@@ -154,35 +158,83 @@
     refs[-1][...] = gram_of(rounds, rows, compat, refs[:-1])
 
 
-def gram_factor(rounds, rows, compat, size, before, *refs):
-    *blocks, r_out, packed_out, high_out, low_out, w = refs
-    n = before.shape[0]
-    g = before[...] + gram_of(rounds, rows, compat, blocks)
+def shifted(g, size, row, col):
+    i = lax.broadcasted_iota(jnp.int32, g.shape, 0) + row
+    j = lax.broadcasted_iota(jnp.int32, g.shape, 1) + col
+    live = jnp.logical_and(i < size[0, 0], j < size[0, 0])
+    return jnp.where(live, (1.0 + SHIFT) * g, 0.0) + jnp.where(i == j, SHIFT * SHIFT, 0.0)
+
+
+def factor_block(a, r_out, inverse_out, w):
+    n = a.shape[0]
     i = lax.broadcasted_iota(jnp.int32, (n, n), 0)
     j = lax.broadcasted_iota(jnp.int32, (n, n), 1)
-    live = jnp.logical_and(i < size[0, 0], j < size[0, 0])
-    eye = (i == j).astype(jnp.float32)
-    w[:, :n] = jnp.where(live, (1.0 + SHIFT) * g, 0.0) + (SHIFT * SHIFT) * eye
-    w[:, n:] = eye
+    w[:, :n] = a
+    w[:, n:] = (i == j).astype(jnp.float32)
     factor_in_place(w, n)
     r_out[...] = jnp.where(i <= j, w[:, :n], 0.0)
+    inverse_out[...] = jnp.where(i >= j, w[:, n:], 0.0)
+
+
+def leading_factor(rounds, rows, compat, size, gram, *refs):
+    *blocks, r_out, inverse_out, w = refs
+    h = r_out.shape[0]
+    g = gram[:h, :h] + gram_of(rounds, rows, compat, blocks)
+    factor_block(shifted(g, size, 0, 0), r_out, inverse_out, w)
+
+
+def trailing_factor(rounds, rows, compat, size, gram, r_lead, inverse_lead, *refs):
+    *blocks, r_out, packed_out, inverse_out, w = refs
+    first, second = blocks[: len(rounds)], blocks[len(rounds) :]
+    h = r_lead.shape[0]
+    cross = shifted(gram[:h, h:] + gram_of(rounds, rows, compat, first, second), size, 0, h)
+    own = shifted(gram[h:, h:] + gram_of(rounds, rows, compat, second), size, h, h)
+    dot = functools.partial(jnp.dot, preferred_element_type=jnp.float32)
+    right = dot(inverse_lead[...], cross, precision=HIGHEST)
+    down_t = functools.partial(
+        lax.dot_general,
+        dimension_numbers=(((0,), (0,)), ((), ())),
+        precision=HIGHEST,
+        preferred_element_type=jnp.float32,
+    )
+    right = right + dot(inverse_lead[...], cross - down_t(r_lead[...], right))
+    factor_block(own - down_t(right, right), r_out.at[h:, h:], inverse_out, w)
+    r_out[:h, :h] = r_lead[...]
+    r_out[:h, h:] = right
+    r_out[h:, :h] = jnp.zeros((h, h), jnp.float32)
     pack(r_out, packed_out)
-    inverse = jnp.where(jnp.logical_and(i >= j, live), w[:, n:], 0.0)
-    high = inverse.astype(jnp.bfloat16)
-    high_out[...] = high
-    low_out[...] = (inverse - high.astype(jnp.float32)).astype(jnp.bfloat16)
-
-
-def orthonormal_rows(rounds, rows, compat, high, low, *refs):
+
+
+def orthonormal_rows(rounds, rows, compat, size, factor, lead, trail, *refs):
     *blocks, out, results, sent = refs
     dims = (((1,), (1,)), ((), ()))
-    each = blocks[0].shape[0]
+    h = lead.shape[0]
+    below = lax.dot_general(
+        factor[:h, h:],
+        lead[...],
+        (((0,), (0,)), ((), ())),
+        precision=HIGHEST,
+        preferred_element_type=jnp.float32,
+    )
+    below = -jnp.dot(trail[...], below, precision=HIGHEST, preferred_element_type=jnp.float32)
+    inverse = jnp.concatenate(
+        [
+            jnp.concatenate([lead[...], jnp.zeros((h, h), jnp.float32)], axis=1),
+            jnp.concatenate([below, trail[...]], axis=1),
+        ],
+        axis=0,
+    )
+    inverse = jnp.where(lax.broadcasted_iota(jnp.int32, inverse.shape, 1) < size[0, 0], inverse, 0.0)
+    high = inverse.astype(jnp.bfloat16)
+    low = (inverse - high.astype(jnp.float32)).astype(jnp.bfloat16)
+    each = results.shape[1]
     me = lax.axis_index("blk")
     copies = []
-    for i, (r, block) in enumerate(zip(rounds, blocks)):
-        x = block[...]
-        q = lax.dot_general(x, high[...], dims, preferred_element_type=jnp.float32)
-        q = q + lax.dot_general(x, low[...], dims, preferred_element_type=jnp.float32)
+    views = iter(blocks)
+    for i, (r, pieces) in enumerate(rounds):
+        x = jnp.concatenate([next(views)[...] for _ in range(pieces)], axis=1)
+        q = lax.dot_general(x, high, dims, preferred_element_type=jnp.float32)
+        q = q + lax.dot_general(x, low, dims, preferred_element_type=jnp.float32)
         results[i] = (q * sender_allows(compat, r, each, rows)).astype(jnp.bfloat16)
         place = pl.ds(pl.multiple_of((me ^ r) * each, each), each)
         copies.append(pltpu.make_async_copy(results.at[i], out.at[0, place], sent.at[i]))
@@ -191,7 +243,8 @@
         copy.wait()
 
 
-def chained(by, own, incoming, out, packed_out, before):
+def chained(by, own, incoming, out, *rest):
+    *packed_out, before = rest
     later = lax.axis_index("seg") >= by
 
     @pl.when(later)
@@ -207,7 +260,8 @@
     def _():
         out[...] = own[...]
 
-    pack(out, packed_out)
+    for packed in packed_out:
+        pack(out, packed)
 
 
 def local(products, compat, sizes):
@@ -220,49 +274,66 @@
     in_vmem = pl.BlockSpec(memory_space=pltpu.VMEM)
     in_hbm = pl.BlockSpec(memory_space=pltpu.MemorySpace.HBM)
     pieces = 4
+    far, near = range(parts // 2, parts), range(1, parts // 2)
+    whole, late = far[:-LATE], far[-LATE:]
+    h = width // 2
+    first, second = [(r, 0, h) for r in late], [(r, h, h) for r in late]
+    far_sends = [(r, 0, width) for r in whole]
+    cut = len(far_sends) - AHEAD
+    far_sends = far_sends[:cut] + first + far_sends[cut:] + second
+    near_sends = [(r, 0, width) for r in near]
+    wanted = [(0, 0, width)] + far_sends + near_sends
     blocks = pl.pallas_call(
-        split_columns,
-        out_shape=[b16((rows_here, width))] * parts,
+        functools.partial(split_columns, wanted),
+        out_shape=[b16((rows_here, count)) for _, _, count in wanted],
         in_specs=[in_hbm],
-        out_specs=[in_vmem] * parts,
+        out_specs=[in_vmem] * len(wanted),
         scratch_shapes=[
             pltpu.VMEM((rows_here, parts * width), jnp.bfloat16),
             pltpu.SemaphoreType.DMA((pieces,)),
         ],
         compiler_params=PARAMS,
     )(products)
-    half, quarter = parts // 2, parts // 4
-    far = [r for pair in zip(range(half, half + quarter), range(half + quarter, parts)) for r in pair]
-    near = [*range(quarter, half), *range(1, quarter)]
-    got = {0: blocks[0]}
-    for order, window in ((far, FAR), (near, NEAR)):
-        for i, r in enumerate(order):
-            block = blocks[r]
+    blocks = dict(zip(wanted, blocks))
+    got = {wanted[0]: blocks[wanted[0]]}
+    for order, window in ((far_sends, FAR), (near_sends, NEAR)):
+        for i, key in enumerate(order):
+            block = blocks[key]
             if i >= window:
                 block, _ = lax.optimization_barrier((block, got[order[i - window]]))
-            got[r] = lax.ppermute(block, "blk", [(k, k ^ r) for k in range(parts)])
-    early, late = [0, *near, *far[: -LATE]], far[-LATE:]
-    partial = pl.pallas_call(
+            got[key] = lax.ppermute(block, "blk", [(k, k ^ key[0]) for k in range(parts)])
+    early = [0, *near, *whole]
+    gram = pl.pallas_call(
         functools.partial(gram_part, early, rows),
         out_shape=f32((width, width)),
         in_specs=[in_smem] + [in_vmem] * len(early),
         out_specs=in_vmem,
         compiler_params=PARAMS,
-    )(compat[0], *[got[r] for r in early])
+    )(compat[0], *[got[r, 0, width] for r in early])
+    firsts, seconds = [got[key] for key in first], [got[key] for key in second]
+    lead_r, lead = pl.pallas_call(
+        functools.partial(leading_factor, late, rows),
+        out_shape=(f32((h, h)), f32((h, h))),
+        in_specs=[in_smem, in_smem] + [in_vmem] * (1 + LATE),
+        out_specs=[in_vmem] * 2,
+        scratch_shapes=[pltpu.VMEM((h, 2 * h), jnp.float32)],
+        compiler_params=PARAMS,
+    )(compat[0], sizes, gram, *firsts)
     packed_rows = 5 * width // 8
-    factor, packed, high, low = pl.pallas_call(
-        functools.partial(gram_factor, late, rows),
-        out_shape=(f32((width, width)), f32((packed_rows, width)), b16((width, width)), b16((width, width))),
-        in_specs=[in_smem, in_smem] + [in_vmem] * (1 + len(late)),
-        out_specs=[in_vmem] * 4,
-        scratch_shapes=[pltpu.VMEM((width, 2 * width), jnp.float32)],
-        compiler_params=PARAMS,
-    )(compat[0], sizes, partial, *[got[r] for r in late])
-    rounds = sorted(got)
+    factor, packed, trail = pl.pallas_call(
+        functools.partial(trailing_factor, late, rows),
+        out_shape=(f32((width, width)), f32((packed_rows, width)), f32((h, h))),
+        in_specs=[in_smem, in_smem] + [in_vmem] * (3 + 2 * LATE),
+        out_specs=[in_vmem] * 3,
+        scratch_shapes=[pltpu.VMEM((h, 2 * h), jnp.float32)],
+        compiler_params=PARAMS,
+    )(compat[0], sizes, gram, lead_r, lead, *firsts, *seconds)
+    rounds = [(r, 1) for r in early] + [(r, 2) for r in late]
+    views = [got[r, 0, width] for r in early] + [x for pair in zip(firsts, seconds) for x in pair]
     ortho = pl.pallas_call(
         functools.partial(orthonormal_rows, rounds, rows),
         out_shape=b16((1, rows, width)),
-        in_specs=[in_smem] + [in_vmem] * (2 + parts),
+        in_specs=[in_smem, in_smem] + [in_vmem] * (3 + len(views)),
         out_specs=in_hbm,
         scratch_shapes=[
             pltpu.VMEM((parts, rows_here, width), jnp.bfloat16),
@@ -272,19 +343,21 @@
         cost_estimate=pl.CostEstimate(
             flops=4 * rows * width * width, bytes_accessed=4 * rows * width, transcendentals=0
         ),
-    )(compat[0], high, low, *[got[r] for r in rounds])
+    )(compat[0], sizes, factor, lead, trail, *views)
     sites = lax.axis_size("seg")
     accumulated, by = factor, 1
     while by < sites:
         incoming = lax.ppermute(packed, "seg", [(i, (i + by) % sites) for i in range(sites)])
-        accumulated, packed = pl.pallas_call(
+        shapes = [f32((width, width)), f32((packed_rows, width))][: 1 if by * 2 >= sites else 2]
+        accumulated, *packed = pl.pallas_call(
             functools.partial(chained, by),
-            out_shape=(f32((width, width)), f32((packed_rows, width))),
+            out_shape=shapes,
             in_specs=[in_vmem] * 2,
-            out_specs=[in_vmem] * 2,
+            out_specs=[in_vmem] * len(shapes),
             scratch_shapes=[pltpu.VMEM((width, width), jnp.float32)],
             compiler_params=PARAMS,
         )(accumulated, incoming)
+        packed = packed[0] if packed else None
         by *= 2
     return (ortho, accumulated[None, None])
 

time: 67.2 us -> 65.5 us (0.975); the launches traced: 67.1 us -> 64.3 us
  waiting for transfers between devices: 32.4 us -> 22.2 us
  starting transfers between devices: 19.6 us -> 25.3 us
  Pallas kernels: 12 us -> 13.8 us
    ppermute x15 -> x18, waiting for transfers between devices: 29.5 us -> 19.6 us  [local(): lax.ppermute(block, 'blk', [(k, k ^ key[0]) for k in range(parts)])]
    ppermute x15 -> x18, starting transfers between devices: 19.1 us -> 24.8 us  [local(): lax.ppermute(block, 'blk', [(k, k ^ key[0]) for k in range(parts)])]
    pallas_call x3 -> x4, Pallas kernels: 8.15 us -> 9.42 us  [the longest x1 4.4 us: local(): pl.pallas_call(functools.partial(trailing_factor, late, rows), out_shape=...]
  transfers between devices with their start and end apart: 16 -> 19, of which waited for: 10 -> 7; matrix products, arithmetic and copies ran while one was open for 0% -> 0% of each run, Pallas kernels for 6% -> 12%
where the time goes in v6:
time: 65.5 us; the launch traced here: 64.3 us
  starting transfers between devices  25.3 us (39%)
  waiting for transfers between devices  22.2 us (34%)
  Pallas kernels  13.8 us (21%)
  local copies, waits for them, and re-layouts  1.59 us (2%)
  between operations  1.37 us (2%)
    ppermute x18, starting transfers between devices, local(): lax.ppermute(block, 'blk', [(k, k ^ key[0]) for k in range(parts)])  24.8 us
    ppermute x18, waiting for transfers between devices, local(): lax.ppermute(block, 'blk', [(k, k ^ key[0]) for k in range(parts)])  19.6 us
    pallas_call x1, Pallas kernels, local(): pl.pallas_call(functools.partial(trailing_factor, late, rows), out_shape=...  4.4 us
    pallas_call x1, Pallas kernels, local(): pl.pallas_call(functools.partial(leading_factor, late, rows), out_shape=(...  3.42 us
    pallas_call x1, Pallas kernels, local(): pl.pallas_call(functools.partial(orthonormal_rows, rounds, rows), out_sha...  3.17 us
    ppermute x1, waiting for transfers between devices, local(): lax.ppermute(packed, 'seg', [(i, (i + by) % sites) for i in range(sites)])  2.59 us
    unnamed x4, local copies, waits for them, and re-layouts  1.59 us
  transfers between devices with their start and end apart: 19, of which 7 were waited for; matrix products, arithmetic and copies ran while one was open for 0% of the time, Pallas kernels for 12%

profile of v6, /device:TPU:14, one launch (start us, length us, event | category | flops | bytes accessed | tf_op | source)
XLA Modules:
  0.0 64.3 jit_solution(12076918375226058188)
XLA Ops:
  0.6 0.0 copy-start
  0.6 1.6 %copy-done = bf16[1,256,4096]{2,1,0:T(8,128)(2,1)S(1)} copy-done((bf16[1,256,4096]{2,1,0:T(8,128)(2,1)S(1)}, bf16[1,256,4096]{2,1,0:T(8,128)(2,1)}, u32[]{:S(2)}) %copy-start) | copy-done | bytes 2097176
  2.2 0.0 copy-start.1
  2.2 0.5 shard_map.50
  2.7 0.1 collective-permute-start
  2.8 2.7 %collective-permute-start.7 = (bf16[256,256]{1,0:T(8,128)(2,1)S(1)}, bf16[256,256]{1,0:T(8,128)(2,1)S(1)}, u32[]{:S(2)}, u32[]{:S(2)}) collective-permute-start(bf16[256,256]{1,0:T(8,128)(2,1)S(1)} %get-tuple-element.48), channel_id=1, source_target_pairs={{0,8},{1,9},{2,10},{3,11},{4,12},{5,13},{6,14},{7,15},{8,0},{9,1},... | collective-permute-start | bytes 393224 | tf_op jit(solution)/shard_map/ppermute | solution.py:304
  5.5 0.5 collective-permute-start.1
  6.0 1.0 %collective-permute-start.2 = (bf16[256,256]{1,0:T(8,128)(2,1)S(1)}, bf16[256,256]{1,0:T(8,128)(2,1)S(1)}, u32[]{:S(2)}, u32[]{:S(2)}) collective-permute-start(bf16[256,256]{1,0:T(8,128)(2,1)S(1)} %get-tuple-element.39), channel_id=1, source_target_pairs={{0,3},{1,2},{2,1},{3,0},{4,7},{5,6},{6,5},{7,4},{8,11},{9,10},{10,... | collective-permute-start | bytes 393224 | tf_op jit(solution)/shard_map/ppermute | solution.py:304
  7.0 0.0 collective-permute-start.11
  7.0 0.0 collective-permute-done.refs_1_
  7.0 2.5 %collective-permute-start.8 = (bf16[256,256]{1,0:T(8,128)(2,1)S(1)}, bf16[256,256]{1,0:T(8,128)(2,1)S(1)}, u32[]{:S(2)}, u32[]{:S(2)}) collective-permute-start(bf16[256,256]{1,0:T(8,128)(2,1)S(1)} %get-tuple-element.49), channel_id=1, source_target_pairs={{0,9},{1,8},{2,11},{3,10},{4,13},{5,12},{6,15},{7,14},{8,1},{9,0},... | collective-permute-start | bytes 393224 | tf_op jit(solution)/shard_map/ppermute | solution.py:304
  9.5 6.3 %collective-permute-done.7.refs_8_ = bf16[256,256]{1,0:T(8,128)(2,1)S(1)} collective-permute-done((bf16[256,256]{1,0:T(8,128)(2,1)S(1)}, bf16[256,256]{1,0:T(8,128)(2,1)S(1)}, u32[]{:S(2)}, u32[]{:S(2)}) %collective-permute-start.7) | collective-permute-done | bytes 131104 | tf_op jit(solution)/shard_map/ppermute | solution.py:304
  15.8 1.8 %collective-permute-start.3 = (bf16[256,256]{1,0:T(8,128)(2,1)S(1)}, bf16[256,256]{1,0:T(8,128)(2,1)S(1)}, u32[]{:S(2)}, u32[]{:S(2)}) collective-permute-start(bf16[256,256]{1,0:T(8,128)(2,1)S(1)} %get-tuple-element.41), channel_id=1, source_target_pairs={{0,4},{1,5},{2,6},{3,7},{4,0},{5,1},{6,2},{7,3},{8,12},{9,13},{10,... | collective-permute-start | bytes 393224 | tf_op jit(solution)/shard_map/ppermute | solution.py:304
  17.6 0.0 collective-permute-done.11.refs_0_.refs_13_
  17.6 2.1 %collective-permute-start.13 = (bf16[256,128]{1,0:T(8,128)(2,1)S(1)}, bf16[256,128]{1,0:T(8,128)(2,1)S(1)}, u32[]{:S(2)}, u32[]{:S(2)}) collective-permute-start(bf16[256,128]{1,0:T(8,128)(2,1)S(1)} %get-tuple-element.57), channel_id=1, source_target_pairs={{0,14},{1,15},{2,12},{3,13},{4,10},{5,11},{6,8},{7,9},{8,6},{9,7},... | collective-permute-start | bytes 196616 | tf_op jit(solution)/shard_map/ppermute | solution.py:304
  19.7 0.0 collective-permute-done.1.refs_2_
  19.7 1.4 %collective-permute-start.9 = (bf16[256,256]{1,0:T(8,128)(2,1)S(1)}, bf16[256,256]{1,0:T(8,128)(2,1)S(1)}, u32[]{:S(2)}, u32[]{:S(2)}) collective-permute-start(bf16[256,256]{1,0:T(8,128)(2,1)S(1)} %get-tuple-element.51), channel_id=1, source_target_pairs={{0,10},{1,11},{2,8},{3,9},{4,14},{5,15},{6,12},{7,13},{8,2},{9,3},... | collective-permute-start | bytes 393224 | tf_op jit(solution)/shard_map/ppermute | solution.py:304
  21.1 0.0 collective-permute-done.2.refs_3_
  21.1 0.9 %collective-permute-start.14 = (bf16[256,128]{1,0:T(8,128)(2,1)S(1)}, bf16[256,128]{1,0:T(8,128)(2,1)S(1)}, u32[]{:S(2)}, u32[]{:S(2)}) collective-permute-start(bf16[256,128]{1,0:T(8,128)(2,1)S(1)} %get-tuple-element.58), channel_id=1, source_target_pairs={{0,15},{1,14},{2,13},{3,12},{4,11},{5,10},{6,9},{7,8},{8,7},{9,6},... | collective-permute-start | bytes 196616 | tf_op jit(solution)/shard_map/ppermute | solution.py:304
  22.0 6.8 %collective-permute-done.13.refs_1_.refs_15_ = bf16[256,128]{1,0:T(8,128)(2,1)S(1)} collective-permute-done((bf16[256,128]{1,0:T(8,128)(2,1)S(1)}, bf16[256,128]{1,0:T(8,128)(2,1)S(1)}, u32[]{:S(2)}, u32[]{:S(2)}) %collective-permute-start.13) | collective-permute-done | bytes 65568 | tf_op jit(solution)/shard_map/ppermute | solution.py:304
  28.8 4.7 %collective-permute-start.12 = (bf16[256,256]{1,0:T(8,128)(2,1)S(1)}, bf16[256,256]{1,0:T(8,128)(2,1)S(1)}, u32[]{:S(2)}, u32[]{:S(2)}) collective-permute-start(bf16[256,256]{1,0:T(8,128)(2,1)S(1)} %get-tuple-element.56), channel_id=1, source_target_pairs={{0,12},{1,13},{2,14},{3,15},{4,8},{5,9},{6,10},{7,11},{8,4},{9,5},... | collective-permute-start | bytes 393224 | tf_op jit(solution)/shard_map/ppermute | solution.py:304
  33.5 0.0 collective-permute-done.8.refs_9_
  33.5 0.0 collective-permute-start.4
  33.5 0.0 collective-permute-done.3.refs_4_
  33.5 0.1 collective-permute-start.5
  33.6 1.6 %collective-permute-done.14.refs_2_.refs_17_ = bf16[256,128]{1,0:T(8,128)(2,1)S(1)} collective-permute-done((bf16[256,128]{1,0:T(8,128)(2,1)S(1)}, bf16[256,128]{1,0:T(8,128)(2,1)S(1)}, u32[]{:S(2)}, u32[]{:S(2)}) %collective-permute-start.14) | collective-permute-done | bytes 65568 | tf_op jit(solution)/shard_map/ppermute | solution.py:304
  35.2 0.0 collective-permute-start.10
  35.2 0.0 collective-permute-done.9.refs_10_
  35.2 3.7 %collective-permute-start.6 = (bf16[256,256]{1,0:T(8,128)(2,1)S(1)}, bf16[256,256]{1,0:T(8,128)(2,1)S(1)}, u32[]{:S(2)}, u32[]{:S(2)}) collective-permute-start(bf16[256,256]{1,0:T(8,128)(2,1)S(1)} %get-tuple-element.47), channel_id=1, source_target_pairs={{0,7},{1,6},{2,5},{3,4},{4,3},{5,2},{6,1},{7,0},{8,15},{9,14},{10,... | collective-permute-start | bytes 393224 | tf_op jit(solution)/shard_map/ppermute | solution.py:304
  38.9 0.0 collective-permute-done.12.refs_12_
  38.9 0.2 collective-permute-start.15
  39.1 0.0 collective-permute-done.4.refs_5_
  39.1 2.6 %collective-permute-start.16 = (bf16[256,128]{1,0:T(8,128)(2,1)S(1)}, bf16[256,128]{1,0:T(8,128)(2,1)S(1)}, u32[]{:S(2)}, u32[]{:S(2)}) collective-permute-start(bf16[256,128]{1,0:T(8,128)(2,1)S(1)} %get-tuple-element.64), channel_id=1, source_target_pairs={{0,14},{1,15},{2,12},{3,13},{4,10},{5,11},{6,8},{7,9},{8,6},{9,7},... | collective-permute-start | bytes 196616 | tf_op jit(solution)/shard_map/ppermute | solution.py:304
  41.7 0.0 collective-permute-done.5.refs_6_
  41.7 0.5 collective-permute-start.17
  42.8 0.0 collective-permute-done.10.refs_11_
  42.9 1.8 %collective-permute-done.6.refs_7_ = bf16[256,256]{1,0:T(8,128)(2,1)S(1)} collective-permute-done((bf16[256,256]{1,0:T(8,128)(2,1)S(1)}, bf16[256,256]{1,0:T(8,128)(2,1)S(1)}, u32[]{:S(2)}, u32[]{:S(2)}) %collective-permute-start.6) | collective-permute-done | bytes 131104 | tf_op jit(solution)/shard_map/ppermute | solution.py:304
  44.6 0.0 copy-done.1
  44.6 1.2 %shard_map.51.gram = f32[256,256]{1,0:T(8,128)S(1)} custom-call(s32[1,16]{1,0:T(1,128)S(1)} %bitcast.2, bf16[256,256]{1,0:T(8,128)(2,1)S(1)} %get-tuple-element.36.refs_0_, bf16[256,256]{1,0:T(8,128)(2,1)S(1)} %collective-permute-done.refs_1_, bf16[256,256]{1,0:T(8,128)(2,1)S(1)} %collective-permute-done.1.refs_2_, ...), custom_call_target="tpu_custom_call" | custom-call | tf_op jit(solution)/shard_map/pallas_call | solution.py:306
  45.8 3.4 %shard_map.52 = (f32[128,128]{1,0:T(8,128)S(1)}, f32[128,128]{1,0:T(8,128)S(1)}) custom-call(s32[1,16]{1,0:T(1,128)S(1)} %bitcast.3, s32[1,1]{1,0:T(1,128)S(6)} %copy.5.size, f32[256,256]{1,0:T(8,128)S(1)} %shard_map.51.gram, bf16[256,128]{1,0:T(8,128)(2,1)S(1)} %collective-permute-done.11.refs_0_.refs_13_, ...), custom_call_target="tpu_custom_call" | custom-call | tf_op jit(solution)/shard_map/pallas_call | solution.py:314
  49.3 0.0 collective-permute-done.15.refs_3_.refs_14_
  49.3 2.6 %collective-permute-done.16.refs_4_.refs_16_ = bf16[256,128]{1,0:T(8,128)(2,1)S(1)} collective-permute-done((bf16[256,128]{1,0:T(8,128)(2,1)S(1)}, bf16[256,128]{1,0:T(8,128)(2,1)S(1)}, u32[]{:S(2)}, u32[]{:S(2)}) %collective-permute-start.16) | collective-permute-done | bytes 65568 | tf_op jit(solution)/shard_map/ppermute | solution.py:304
  51.9 0.7 %collective-permute-done.17.refs_5_.refs_18_ = bf16[256,128]{1,0:T(8,128)(2,1)S(1)} collective-permute-done((bf16[256,128]{1,0:T(8,128)(2,1)S(1)}, bf16[256,128]{1,0:T(8,128)(2,1)S(1)}, u32[]{:S(2)}, u32[]{:S(2)}) %collective-permute-start.17) | collective-permute-done | bytes 65568 | tf_op jit(solution)/shard_map/ppermute | solution.py:304
  52.5 4.4 %shard_map.53 = (f32[256,256]{1,0:T(8,128)S(1)}, f32[160,256]{1,0:T(8,128)S(1)}, f32[128,128]{1,0:T(8,128)S(1)}) custom-call(s32[1,16]{1,0:T(1,128)S(1)} %bitcast.4, s32[1,1]{1,0:T(1,128)S(6)} %copy.5.size, f32[256,256]{1,0:T(8,128)S(1)} %shard_map.51.gram, f32[128,128]{1,0:T(8,128)S(1)} %get-tuple-element.59.r_lead, ...), custom_call_target="tpu_custom_call" | custom-call | tf_op jit(solution)/shard_map/pallas_call | solution.py:323
  56.9 0.6 collective-permute-start.18
  57.5 3.2 %shard_map.54 = bf16[1,4096,256]{2,1,0:T(8,128)(2,1)} custom-call(s32[1,16]{1,0:T(1,128)S(1)} %bitcast.5, s32[1,1]{1,0:T(1,128)S(6)} %copy.5.size, f32[256,256]{1,0:T(8,128)S(1)} %get-tuple-element.67.factor.own, f32[128,128]{1,0:T(8,128)S(1)} %get-tuple-element.60.inverse_lead.lead, f32[128,128]{1,0:T(8,128)S(1)} %get-tuple-element.68.trail, ...), custom_call_target="tpu_custom_call" | custom-call | flops 1073741824 | bytes 4194304 | tf_op jit(solution)/shard_map/pallas_call | solution.py:333
  60.6 2.6 %collective-permute-done.18.incoming = f32[160,256]{1,0:T(8,128)S(1)} collective-permute-done((f32[160,256]{1,0:T(8,128)S(1)}, f32[160,256]{1,0:T(8,128)S(1)}, u32[]{:S(2)}, u32[]{:S(2)}) %collective-permute-start.18) | collective-permute-done | bytes 163872 | tf_op jit(solution)/shard_map/ppermute | solution.py:350
  63.2 1.1 %shard_map.55 = f32[256,256]{1,0:T(8,128)} custom-call(f32[256,256]{1,0:T(8,128)S(1)} %get-tuple-element.67.factor.own, f32[160,256]{1,0:T(8,128)S(1)} %collective-permute-done.18.incoming), custom_call_target="tpu_custom_call" | custom-call | tf_op jit(solution)/shard_map/pallas_call | solution.py:352
Async XLA Ops:
  0.6 1.6 %copy-start = (bf16[1,256,4096]{2,1,0:T(8,128)(2,1)S(1)}, bf16[1,256,4096]{2,1,0:T(8,128)(2,1)}, u32[]{:S(2)}) copy-start(bf16[1,256,4096]{2,1,0:T(8,128)(2,1)} %src.1) | copy-start | bytes 6291460
  2.2 42.4 %copy-start.1 = (s32[1,1,16]{2,1,0:T(1,128)S(1)}, s32[1,1,16]{2,1,0:T(1,128)}, u32[]{:S(2)}) copy-start(s32[1,1,16]{2,1,0:T(1,128)} %param.4) | copy-start | bytes 196
  2.7 4.3 %collective-permute-start = (bf16[256,256]{1,0:T(8,128)(2,1)S(1)}, bf16[256,256]{1,0:T(8,128)(2,1)S(1)}, u32[]{:S(2)}, u32[]{:S(2)}) collective-permute-start(bf16[256,256]{1,0:T(8,128)(2,1)S(1)} %get-tuple-element.37), channel_id=1, source_target_pairs={{0,1},{1,0},{2,3},{3,2},{4,5},{5,4},{6,7},{7,6},{8,9},{9,8},{10,11... | collective-permute-start | bytes 393224 | tf_op jit(solution)/shard_map/ppermute | solution.py:304
  2.8 13.0 %collective-permute-start.7 = (bf16[256,256]{1,0:T(8,128)(2,1)S(1)}, bf16[256,256]{1,0:T(8,128)(2,1)S(1)}, u32[]{:S(2)}, u32[]{:S(2)}) collective-permute-start(bf16[256,256]{1,0:T(8,128)(2,1)S(1)} %get-tuple-element.48), channel_id=1, source_target_pairs={{0,8},{1,9},{2,10},{3,11},{4,12},{5,13},{6,14},{7,15},{8,0},{9,1},... | collective-permute-start | bytes 393224 | tf_op jit(solution)/shard_map/ppermute | solution.py:304
  5.5 14.2 %collective-permute-start.1 = (bf16[256,256]{1,0:T(8,128)(2,1)S(1)}, bf16[256,256]{1,0:T(8,128)(2,1)S(1)}, u32[]{:S(2)}, u32[]{:S(2)}) collective-permute-start(bf16[256,256]{1,0:T(8,128)(2,1)S(1)} %get-tuple-element.38), channel_id=1, source_target_pairs={{0,2},{1,3},{2,0},{3,1},{4,6},{5,7},{6,4},{7,5},{8,10},{9,11},{10,... | collective-permute-start | bytes 393224 | tf_op jit(solution)/shard_map/ppermute | solution.py:304
  6.0 15.1 %collective-permute-start.2 = (bf16[256,256]{1,0:T(8,128)(2,1)S(1)}, bf16[256,256]{1,0:T(8,128)(2,1)S(1)}, u32[]{:S(2)}, u32[]{:S(2)}) collective-permute-start(bf16[256,256]{1,0:T(8,128)(2,1)S(1)} %get-tuple-element.39), channel_id=1, source_target_pairs={{0,3},{1,2},{2,1},{3,0},{4,7},{5,6},{6,5},{7,4},{8,11},{9,10},{10,... | collective-permute-start | bytes 393224 | tf_op jit(solution)/shard_map/ppermute | solution.py:304
  7.0 10.6 %collective-permute-start.11 = (bf16[256,128]{1,0:T(8,128)(2,1)S(1)}, bf16[256,128]{1,0:T(8,128)(2,1)S(1)}, u32[]{:S(2)}, u32[]{:S(2)}) collective-permute-start(bf16[256,128]{1,0:T(8,128)(2,1)S(1)} %get-tuple-element.55), channel_id=1, source_target_pairs={{0,13},{1,12},{2,15},{3,14},{4,9},{5,8},{6,11},{7,10},{8,5},{9,4},... | collective-permute-start | bytes 196616 | tf_op jit(solution)/shard_map/ppermute | solution.py:304
  7.0 26.5 %collective-permute-start.8 = (bf16[256,256]{1,0:T(8,128)(2,1)S(1)}, bf16[256,256]{1,0:T(8,128)(2,1)S(1)}, u32[]{:S(2)}, u32[]{:S(2)}) collective-permute-start(bf16[256,256]{1,0:T(8,128)(2,1)S(1)} %get-tuple-element.49), channel_id=1, source_target_pairs={{0,9},{1,8},{2,11},{3,10},{4,13},{5,12},{6,15},{7,14},{8,1},{9,0},... | collective-permute-start | bytes 393224 | tf_op jit(solution)/shard_map/ppermute | solution.py:304
  15.8 17.7 %collective-permute-start.3 = (bf16[256,256]{1,0:T(8,128)(2,1)S(1)}, bf16[256,256]{1,0:T(8,128)(2,1)S(1)}, u32[]{:S(2)}, u32[]{:S(2)}) collective-permute-start(bf16[256,256]{1,0:T(8,128)(2,1)S(1)} %get-tuple-element.41), channel_id=1, source_target_pairs={{0,4},{1,5},{2,6},{3,7},{4,0},{5,1},{6,2},{7,3},{8,12},{9,13},{10,... | collective-permute-start | bytes 393224 | tf_op jit(solution)/shard_map/ppermute | solution.py:304
  17.6 11.2 %collective-permute-start.13 = (bf16[256,128]{1,0:T(8,128)(2,1)S(1)}, bf16[256,128]{1,0:T(8,128)(2,1)S(1)}, u32[]{:S(2)}, u32[]{:S(2)}) collective-permute-start(bf16[256,128]{1,0:T(8,128)(2,1)S(1)} %get-tuple-element.57), channel_id=1, source_target_pairs={{0,14},{1,15},{2,12},{3,13},{4,10},{5,11},{6,8},{7,9},{8,6},{9,7},... | collective-permute-start | bytes 196616 | tf_op jit(solution)/shard_map/ppermute | solution.py:304
  19.7 15.5 %collective-permute-start.9 = (bf16[256,256]{1,0:T(8,128)(2,1)S(1)}, bf16[256,256]{1,0:T(8,128)(2,1)S(1)}, u32[]{:S(2)}, u32[]{:S(2)}) collective-permute-start(bf16[256,256]{1,0:T(8,128)(2,1)S(1)} %get-tuple-element.51), channel_id=1, source_target_pairs={{0,10},{1,11},{2,8},{3,9},{4,14},{5,15},{6,12},{7,13},{8,2},{9,3},... | collective-permute-start | bytes 393224 | tf_op jit(solution)/shard_map/ppermute | solution.py:304
  21.1 14.1 %collective-permute-start.14 = (bf16[256,128]{1,0:T(8,128)(2,1)S(1)}, bf16[256,128]{1,0:T(8,128)(2,1)S(1)}, u32[]{:S(2)}, u32[]{:S(2)}) collective-permute-start(bf16[256,128]{1,0:T(8,128)(2,1)S(1)} %get-tuple-element.58), channel_id=1, source_target_pairs={{0,15},{1,14},{2,13},{3,12},{4,11},{5,10},{6,9},{7,8},{8,7},{9,6},... | collective-permute-start | bytes 196616 | tf_op jit(solution)/shard_map/ppermute | solution.py:304
  28.8 10.1 %collective-permute-start.12 = (bf16[256,256]{1,0:T(8,128)(2,1)S(1)}, bf16[256,256]{1,0:T(8,128)(2,1)S(1)}, u32[]{:S(2)}, u32[]{:S(2)}) collective-permute-start(bf16[256,256]{1,0:T(8,128)(2,1)S(1)} %get-tuple-element.56), channel_id=1, source_target_pairs={{0,12},{1,13},{2,14},{3,15},{4,8},{5,9},{6,10},{7,11},{8,4},{9,5},... | collective-permute-start | bytes 393224 | tf_op jit(solution)/shard_map/ppermute | solution.py:304
  33.5 5.5 %collective-permute-start.4 = (bf16[256,256]{1,0:T(8,128)(2,1)S(1)}, bf16[256,256]{1,0:T(8,128)(2,1)S(1)}, u32[]{:S(2)}, u32[]{:S(2)}) collective-permute-start(bf16[256,256]{1,0:T(8,128)(2,1)S(1)} %get-tuple-element.43), channel_id=1, source_target_pairs={{0,5},{1,4},{2,7},{3,6},{4,1},{5,0},{6,3},{7,2},{8,13},{9,12},{10,... | collective-permute-start | bytes 393224 | tf_op jit(solution)/shard_map/ppermute | solution.py:304
  33.5 8.1 %collective-permute-start.5 = (bf16[256,256]{1,0:T(8,128)(2,1)S(1)}, bf16[256,256]{1,0:T(8,128)(2,1)S(1)}, u32[]{:S(2)}, u32[]{:S(2)}) collective-permute-start(bf16[256,256]{1,0:T(8,128)(2,1)S(1)} %get-tuple-element.45), channel_id=1, source_target_pairs={{0,6},{1,7},{2,4},{3,5},{4,2},{5,3},{6,0},{7,1},{8,14},{9,15},{10,... | collective-permute-start | bytes 393224 | tf_op jit(solution)/shard_map/ppermute | solution.py:304
  35.2 7.7 %collective-permute-start.10 = (bf16[256,256]{1,0:T(8,128)(2,1)S(1)}, bf16[256,256]{1,0:T(8,128)(2,1)S(1)}, u32[]{:S(2)}, u32[]{:S(2)}) collective-permute-start(bf16[256,256]{1,0:T(8,128)(2,1)S(1)} %get-tuple-element.53), channel_id=1, source_target_pairs={{0,11},{1,10},{2,9},{3,8},{4,15},{5,14},{6,13},{7,12},{8,3},{9,2},... | collective-permute-start | bytes 393224 | tf_op jit(solution)/shard_map/ppermute | solution.py:304
  35.2 9.4 %collective-permute-start.6 = (bf16[256,256]{1,0:T(8,128)(2,1)S(1)}, bf16[256,256]{1,0:T(8,128)(2,1)S(1)}, u32[]{:S(2)}, u32[]{:S(2)}) collective-permute-start(bf16[256,256]{1,0:T(8,128)(2,1)S(1)} %get-tuple-element.47), channel_id=1, source_target_pairs={{0,7},{1,6},{2,5},{3,4},{4,3},{5,2},{6,1},{7,0},{8,15},{9,14},{10,... | collective-permute-start | bytes 393224 | tf_op jit(solution)/shard_map/ppermute | solution.py:304
  38.9 10.4 %collective-permute-start.15 = (bf16[256,128]{1,0:T(8,128)(2,1)S(1)}, bf16[256,128]{1,0:T(8,128)(2,1)S(1)}, u32[]{:S(2)}, u32[]{:S(2)}) collective-permute-start(bf16[256,128]{1,0:T(8,128)(2,1)S(1)} %get-tuple-element.62), channel_id=1, source_target_pairs={{0,13},{1,12},{2,15},{3,14},{4,9},{5,8},{6,11},{7,10},{8,5},{9,4},... | collective-permute-start | bytes 196616 | tf_op jit(solution)/shard_map/ppermute | solution.py:304
  39.1 12.8 %collective-permute-start.16 = (bf16[256,128]{1,0:T(8,128)(2,1)S(1)}, bf16[256,128]{1,0:T(8,128)(2,1)S(1)}, u32[]{:S(2)}, u32[]{:S(2)}) collective-permute-start(bf16[256,128]{1,0:T(8,128)(2,1)S(1)} %get-tuple-element.64), channel_id=1, source_target_pairs={{0,14},{1,15},{2,12},{3,13},{4,10},{5,11},{6,8},{7,9},{8,6},{9,7},... | collective-permute-start | bytes 196616 | tf_op jit(solution)/shard_map/ppermute | solution.py:304
  41.7 10.8 %collective-permute-start.17 = (bf16[256,128]{1,0:T(8,128)(2,1)S(1)}, bf16[256,128]{1,0:T(8,128)(2,1)S(1)}, u32[]{:S(2)}, u32[]{:S(2)}) collective-permute-start(bf16[256,128]{1,0:T(8,128)(2,1)S(1)} %get-tuple-element.66), channel_id=1, source_target_pairs={{0,15},{1,14},{2,13},{3,12},{4,11},{5,10},{6,9},{7,8},{8,7},{9,6},... | collective-permute-start | bytes 196616 | tf_op jit(solution)/shard_map/ppermute | solution.py:304
  56.9 6.3 %collective-permute-start.18 = (f32[160,256]{1,0:T(8,128)S(1)}, f32[160,256]{1,0:T(8,128)S(1)}, u32[]{:S(2)}, u32[]{:S(2)}) collective-permute-start(f32[160,256]{1,0:T(8,128)S(1)} %get-tuple-element.69), channel_id=1, source_target_pairs={{0,16},{16,0},{1,17},{17,1},{2,18},{18,2},{3,19},{19,3},{4,20},{20... | collective-permute-start | bytes 491528 | tf_op jit(solution)/shard_map/ppermute | solution.py:350

commit v7 on v6

--- a/solution.py
+++ b/solution.py
@@ -114,29 +114,6 @@
         p = {at: value for at, value in p.items() if at[0] >= end}
 
 
-def pack(r, out):
-    n = r.shape[0]
-    q = n // 4
-    out[:q, :] = r[:q, :]
-    out[q : 2 * q, :] = r[q : 2 * q, :]
-    out[q : 2 * q, :q] = r[3 * q :, 3 * q :]
-    out[2 * q :, : 2 * q] = r[2 * q : 2 * q + q // 2, 2 * q :]
-    out[2 * q :, 2 * q :] = r[2 * q + q // 2 : 3 * q, 2 * q :]
-
-
-def unpack(packed, r):
-    n = r.shape[0]
-    q = n // 4
-    r[:q, :] = packed[:q, :]
-    r[q : 2 * q, :] = packed[q : 2 * q, :]
-    r[q : 2 * q, :q] = jnp.zeros((q, q), r.dtype)
-    r[2 * q :, : 2 * q] = jnp.zeros((2 * q, 2 * q), r.dtype)
-    r[2 * q : 2 * q + q // 2, 2 * q :] = packed[2 * q :, : 2 * q]
-    r[2 * q + q // 2 : 3 * q, 2 * q :] = packed[2 * q :, 2 * q :]
-    r[3 * q :, 2 * q : 3 * q] = jnp.zeros((q, q), r.dtype)
-    r[3 * q :, 3 * q :] = packed[q : 2 * q, :q]
-
-
 def sender_allows(compat, r, each, rows):
     sender = lax.axis_index("blk") ^ r
     return compat[0, sender * each // (rows // compat.shape[1])].astype(jnp.float32)
@@ -184,7 +161,7 @@
 
 
 def trailing_factor(rounds, rows, compat, size, gram, r_lead, inverse_lead, *refs):
-    *blocks, r_out, packed_out, inverse_out, w = refs
+    *blocks, r_out, rest_out, inverse_out, w = refs
     first, second = blocks[: len(rounds)], blocks[len(rounds) :]
     h = r_lead.shape[0]
     cross = shifted(gram[:h, h:] + gram_of(rounds, rows, compat, first, second), size, 0, h)
@@ -198,11 +175,12 @@
         preferred_element_type=jnp.float32,
     )
     right = right + dot(inverse_lead[...], cross - down_t(r_lead[...], right))
-    factor_block(own - down_t(right, right), r_out.at[h:, h:], inverse_out, w)
+    factor_block(own - down_t(right, right), rest_out.at[:, h:], inverse_out, w)
+    rest_out[:, :h] = right
     r_out[:h, :h] = r_lead[...]
     r_out[:h, h:] = right
     r_out[h:, :h] = jnp.zeros((h, h), jnp.float32)
-    pack(r_out, packed_out)
+    r_out[h:, h:] = rest_out[:, h:]
 
 
 def orthonormal_rows(rounds, rows, compat, size, factor, lead, trail, *refs):
@@ -243,25 +221,29 @@
         copy.wait()
 
 
-def chained(by, own, incoming, out, *rest):
-    *packed_out, before = rest
+def chained(by, own, lead, rest, out, *parts_out):
     later = lax.axis_index("seg") >= by
+    h = lead.shape[0]
 
     @pl.when(later)
     def _():
-        unpack(incoming, before)
-        h = own.shape[0] // 2
         dot = functools.partial(jnp.dot, precision=HIGHEST, preferred_element_type=jnp.float32)
-        out[:h, :] = dot(own[:h, :], before[...])
+        top = dot(own[:h, :h], jnp.concatenate([lead[...], rest[:, :h]], axis=1))
+        right = dot(own[:, h:], rest[:, h:])
+        out[:h, :h] = top[:, :h]
+        out[:h, h:] = top[:, h:] + right[:h, :]
         out[h:, :h] = jnp.zeros((h, h), jnp.float32)
-        out[h:, h:] = dot(own[h:, h:], before[h:, h:])
+        out[h:, h:] = right[h:, :]
 
     @pl.when(jnp.logical_not(later))
     def _():
         out[...] = own[...]
 
-    for packed in packed_out:
-        pack(out, packed)
+    if parts_out:
+        lead_out, rest_out = parts_out
+        lead_out[...] = out[:h, :h]
+        rest_out[:, :h] = out[:h, h:]
+        rest_out[:, h:] = out[h:, h:]
 
 
 def local(products, compat, sizes):
@@ -319,10 +301,15 @@
         scratch_shapes=[pltpu.VMEM((h, 2 * h), jnp.float32)],
         compiler_params=PARAMS,
     )(compat[0], sizes, gram, *firsts)
-    packed_rows = 5 * width // 8
-    factor, packed, trail = pl.pallas_call(
+    sites = lax.axis_size("seg")
+
+    def onward(x, by):
+        return lax.ppermute(x, "seg", [(i, (i + by) % sites) for i in range(sites)])
+
+    lead_in = onward(lead_r, 1)
+    factor, rest, trail = pl.pallas_call(
         functools.partial(trailing_factor, late, rows),
-        out_shape=(f32((width, width)), f32((packed_rows, width)), f32((h, h))),
+        out_shape=(f32((width, width)), f32((h, width)), f32((h, h))),
         in_specs=[in_smem, in_smem] + [in_vmem] * (3 + 2 * LATE),
         out_specs=[in_vmem] * 3,
         scratch_shapes=[pltpu.VMEM((h, 2 * h), jnp.float32)],
@@ -344,21 +331,21 @@
             flops=4 * rows * width * width, bytes_accessed=4 * rows * width, transcendentals=0
         ),
     )(compat[0], sizes, factor, lead, trail, *views)
-    sites = lax.axis_size("seg")
     accumulated, by = factor, 1
     while by < sites:
-        incoming = lax.ppermute(packed, "seg", [(i, (i + by) % sites) for i in range(sites)])
-        shapes = [f32((width, width)), f32((packed_rows, width))][: 1 if by * 2 >= sites else 2]
-        accumulated, *packed = pl.pallas_call(
+        rest, lead_in = lax.optimization_barrier((rest, lead_in))
+        rest_in = onward(rest, by)
+        shapes = [f32((width, width)), f32((h, h)), f32((h, width))][: 1 if by * 2 >= sites else 3]
+        accumulated, *others = pl.pallas_call(
             functools.partial(chained, by),
             out_shape=shapes,
-            in_specs=[in_vmem] * 2,
+            in_specs=[in_vmem] * 3,
             out_specs=[in_vmem] * len(shapes),
-            scratch_shapes=[pltpu.VMEM((width, width), jnp.float32)],
             compiler_params=PARAMS,
-        )(accumulated, incoming)
-        packed = packed[0] if packed else None
+        )(accumulated, lead_in, rest_in)
         by *= 2
+        if others:
+            lead_in, rest = onward(others[0], by), others[1]
     return (ortho, accumulated[None, None])
 
 

time: 65.5 us -> 64.7 us (0.988)
  starting transfers between devices: 25.3 us -> 24.2 us
  waiting for transfers between devices: 22.2 us -> 23.1 us
    ppermute x18, starting transfers between devices: 24.8 us -> 23 us  [local(): lax.ppermute(block, 'blk', [(k, k ^ key[0]) for k in range(parts)])]
    ppermute x18, waiting for transfers between devices: 19.6 us -> 21 us  [local(): lax.ppermute(block, 'blk', [(k, k ^ key[0]) for k in range(parts)])]
    ppermute x1 -> x2, waiting for transfers between devices: 2.59 us -> 2.05 us  [onward(): return lax.ppermute(x, 'seg', [(i, (i + by) % sites) for i in range(sites)])]
  transfers between devices with their start and end apart: 19 -> 20, of which waited for: 7 -> 8; matrix products, arithmetic and copies ran while one was open for 0% -> 0% of each run, Pallas kernels for 12% -> 19%
where the time goes in v7:
time: 64.7 us; the launch traced here: 63.9 us
  starting transfers between devices  24.2 us (37%)
  waiting for transfers between devices  23.1 us (36%)
  Pallas kernels  13.7 us (21%)
  local copies, waits for them, and re-layouts  1.59 us (2%)
  between operations  1.37 us (2%)
    ppermute x18, starting transfers between devices, local(): lax.ppermute(block, 'blk', [(k, k ^ key[0]) for k in range(parts)])  23 us
    ppermute x18, waiting for transfers between devices, local(): lax.ppermute(block, 'blk', [(k, k ^ key[0]) for k in range(parts)])  21 us
    pallas_call x1, Pallas kernels, local(): pl.pallas_call(functools.partial(trailing_factor, late, rows), out_shape=...  4.33 us
    pallas_call x1, Pallas kernels, local(): pl.pallas_call(functools.partial(leading_factor, late, rows), out_shape=(...  3.43 us
    pallas_call x1, Pallas kernels, local(): pl.pallas_call(functools.partial(orthonormal_rows, rounds, rows), out_sha...  3.17 us
    ppermute x2, waiting for transfers between devices, onward(): return lax.ppermute(x, 'seg', [(i, (i + by) % sites) for i in range(sites)])  2.05 us
    unnamed x4, local copies, waits for them, and re-layouts  1.59 us
  transfers between devices with their start and end apart: 20, of which 8 were waited for; matrix products, arithmetic and copies ran while one was open for 0% of the time, Pallas kernels for 19%

profile of v7, /device:TPU:14, one launch (start us, length us, event | category | flops | bytes accessed | tf_op | source)
XLA Modules:
  0.0 63.9 jit_solution(7730534677857270521)
XLA Ops:
  0.6 1.6 %copy-done = bf16[1,256,4096]{2,1,0:T(8,128)(2,1)S(1)} copy-done((bf16[1,256,4096]{2,1,0:T(8,128)(2,1)S(1)}, bf16[1,256,4096]{2,1,0:T(8,128)(2,1)}, u32[]{:S(2)}) %copy-start) | copy-done | bytes 2097176
  2.2 0.5 shard_map.50
  2.7 0.1 collective-permute-start
  2.8 2.7 %collective-permute-start.7 = (bf16[256,256]{1,0:T(8,128)(2,1)S(1)}, bf16[256,256]{1,0:T(8,128)(2,1)S(1)}, u32[]{:S(2)}, u32[]{:S(2)}) collective-permute-start(bf16[256,256]{1,0:T(8,128)(2,1)S(1)} %get-tuple-element.50), channel_id=1, source_target_pairs={{0,8},{1,9},{2,10},{3,11},{4,12},{5,13},{6,14},{7,15},{8,0},{9,1},... | collective-permute-start | bytes 393224 | tf_op jit(solution)/shard_map/ppermute | solution.py:286
  5.5 0.5 collective-permute-start.1
  6.0 1.0 %collective-permute-start.2 = (bf16[256,256]{1,0:T(8,128)(2,1)S(1)}, bf16[256,256]{1,0:T(8,128)(2,1)S(1)}, u32[]{:S(2)}, u32[]{:S(2)}) collective-permute-start(bf16[256,256]{1,0:T(8,128)(2,1)S(1)} %get-tuple-element.41), channel_id=1, source_target_pairs={{0,3},{1,2},{2,1},{3,0},{4,7},{5,6},{6,5},{7,4},{8,11},{9,10},{10,... | collective-permute-start | bytes 393224 | tf_op jit(solution)/shard_map/ppermute | solution.py:286
  7.0 0.0 collective-permute-start.11
  7.0 0.0 collective-permute-done.refs_1_
  7.0 2.5 %collective-permute-start.8 = (bf16[256,256]{1,0:T(8,128)(2,1)S(1)}, bf16[256,256]{1,0:T(8,128)(2,1)S(1)}, u32[]{:S(2)}, u32[]{:S(2)}) collective-permute-start(bf16[256,256]{1,0:T(8,128)(2,1)S(1)} %get-tuple-element.51), channel_id=1, source_target_pairs={{0,9},{1,8},{2,11},{3,10},{4,13},{5,12},{6,15},{7,14},{8,1},{9,0},... | collective-permute-start | bytes 393224 | tf_op jit(solution)/shard_map/ppermute | solution.py:286
  9.5 6.3 %collective-permute-done.7.refs_8_ = bf16[256,256]{1,0:T(8,128)(2,1)S(1)} collective-permute-done((bf16[256,256]{1,0:T(8,128)(2,1)S(1)}, bf16[256,256]{1,0:T(8,128)(2,1)S(1)}, u32[]{:S(2)}, u32[]{:S(2)}) %collective-permute-start.7) | collective-permute-done | bytes 131104 | tf_op jit(solution)/shard_map/ppermute | solution.py:286
  15.8 1.8 %collective-permute-start.3 = (bf16[256,256]{1,0:T(8,128)(2,1)S(1)}, bf16[256,256]{1,0:T(8,128)(2,1)S(1)}, u32[]{:S(2)}, u32[]{:S(2)}) collective-permute-start(bf16[256,256]{1,0:T(8,128)(2,1)S(1)} %get-tuple-element.43), channel_id=1, source_target_pairs={{0,4},{1,5},{2,6},{3,7},{4,0},{5,1},{6,2},{7,3},{8,12},{9,13},{10,... | collective-permute-start | bytes 393224 | tf_op jit(solution)/shard_map/ppermute | solution.py:286
  17.6 0.0 collective-permute-done.11.refs_0_.refs_13_
  17.6 1.6 %collective-permute-start.9 = (bf16[256,256]{1,0:T(8,128)(2,1)S(1)}, bf16[256,256]{1,0:T(8,128)(2,1)S(1)}, u32[]{:S(2)}, u32[]{:S(2)}) collective-permute-start(bf16[256,256]{1,0:T(8,128)(2,1)S(1)} %get-tuple-element.53), channel_id=1, source_target_pairs={{0,10},{1,11},{2,8},{3,9},{4,14},{5,15},{6,12},{7,13},{8,2},{9,3},... | collective-permute-start | bytes 393224 | tf_op jit(solution)/shard_map/ppermute | solution.py:286
  19.1 0.0 collective-permute-done.1.refs_2_
  19.1 1.1 %collective-permute-start.13 = (bf16[256,128]{1,0:T(8,128)(2,1)S(1)}, bf16[256,128]{1,0:T(8,128)(2,1)S(1)}, u32[]{:S(2)}, u32[]{:S(2)}) collective-permute-start(bf16[256,128]{1,0:T(8,128)(2,1)S(1)} %get-tuple-element.59), channel_id=1, source_target_pairs={{0,14},{1,15},{2,12},{3,13},{4,10},{5,11},{6,8},{7,9},{8,6},{9,7},... | collective-permute-start | bytes 196616 | tf_op jit(solution)/shard_map/ppermute | solution.py:286
  20.2 0.0 collective-permute-done.2.refs_3_
  20.2 0.9 %collective-permute-start.14 = (bf16[256,128]{1,0:T(8,128)(2,1)S(1)}, bf16[256,128]{1,0:T(8,128)(2,1)S(1)}, u32[]{:S(2)}, u32[]{:S(2)}) collective-permute-start(bf16[256,128]{1,0:T(8,128)(2,1)S(1)} %get-tuple-element.60), channel_id=1, source_target_pairs={{0,15},{1,14},{2,13},{3,12},{4,11},{5,10},{6,9},{7,8},{8,7},{9,6},... | collective-permute-start | bytes 196616 | tf_op jit(solution)/shard_map/ppermute | solution.py:286
  21.1 0.0 collective-permute-done.8.refs_9_
  21.1 1.1 %collective-permute-start.12 = (bf16[256,256]{1,0:T(8,128)(2,1)S(1)}, bf16[256,256]{1,0:T(8,128)(2,1)S(1)}, u32[]{:S(2)}, u32[]{:S(2)}) collective-permute-start(bf16[256,256]{1,0:T(8,128)(2,1)S(1)} %get-tuple-element.58), channel_id=1, source_target_pairs={{0,12},{1,13},{2,14},{3,15},{4,8},{5,9},{6,10},{7,11},{8,4},{9,5},... | collective-permute-start | bytes 393224 | tf_op jit(solution)/shard_map/ppermute | solution.py:286
  22.2 1.7 %collective-permute-done.3.refs_4_ = bf16[256,256]{1,0:T(8,128)(2,1)S(1)} collective-permute-done((bf16[256,256]{1,0:T(8,128)(2,1)S(1)}, bf16[256,256]{1,0:T(8,128)(2,1)S(1)}, u32[]{:S(2)}, u32[]{:S(2)}) %collective-permute-start.3) | collective-permute-done | bytes 131104 | tf_op jit(solution)/shard_map/ppermute | solution.py:286
  23.9 2.2 %collective-permute-start.4 = (bf16[256,256]{1,0:T(8,128)(2,1)S(1)}, bf16[256,256]{1,0:T(8,128)(2,1)S(1)}, u32[]{:S(2)}, u32[]{:S(2)}) collective-permute-start(bf16[256,256]{1,0:T(8,128)(2,1)S(1)} %get-tuple-element.45), channel_id=1, source_target_pairs={{0,5},{1,4},{2,7},{3,6},{4,1},{5,0},{6,3},{7,2},{8,13},{9,12},{10,... | collective-permute-start | bytes 393224 | tf_op jit(solution)/shard_map/ppermute | solution.py:286
  26.1 8.2 %collective-permute-done.13.refs_1_.refs_15_ = bf16[256,128]{1,0:T(8,128)(2,1)S(1)} collective-permute-done((bf16[256,128]{1,0:T(8,128)(2,1)S(1)}, bf16[256,128]{1,0:T(8,128)(2,1)S(1)}, u32[]{:S(2)}, u32[]{:S(2)}) %collective-permute-start.13) | collective-permute-done | bytes 65568 | tf_op jit(solution)/shard_map/ppermute | solution.py:286
  34.3 0.0 collective-permute-start.5
  34.3 0.1 collective-permute-done.14.refs_2_.refs_17_
  34.4 1.6 %collective-permute-start.10 = (bf16[256,256]{1,0:T(8,128)(2,1)S(1)}, bf16[256,256]{1,0:T(8,128)(2,1)S(1)}, u32[]{:S(2)}, u32[]{:S(2)}) collective-permute-start(bf16[256,256]{1,0:T(8,128)(2,1)S(1)} %get-tuple-element.55), channel_id=1, source_target_pairs={{0,11},{1,10},{2,9},{3,8},{4,15},{5,14},{6,13},{7,12},{8,3},{9,2},... | collective-permute-start | bytes 393224 | tf_op jit(solution)/shard_map/ppermute | solution.py:286
  35.9 0.0 collective-permute-done.9.refs_10_
  36.0 2.5 %collective-permute-start.6 = (bf16[256,256]{1,0:T(8,128)(2,1)S(1)}, bf16[256,256]{1,0:T(8,128)(2,1)S(1)}, u32[]{:S(2)}, u32[]{:S(2)}) collective-permute-start(bf16[256,256]{1,0:T(8,128)(2,1)S(1)} %get-tuple-element.49), channel_id=1, source_target_pairs={{0,7},{1,6},{2,5},{3,4},{4,3},{5,2},{6,1},{7,0},{8,15},{9,14},{10,... | collective-permute-start | bytes 393224 | tf_op jit(solution)/shard_map/ppermute | solution.py:286
  39.1 0.0 collective-permute-done.12.refs_12_
  39.1 0.9 %collective-permute-start.15 = (bf16[256,128]{1,0:T(8,128)(2,1)S(1)}, bf16[256,128]{1,0:T(8,128)(2,1)S(1)}, u32[]{:S(2)}, u32[]{:S(2)}) collective-permute-start(bf16[256,128]{1,0:T(8,128)(2,1)S(1)} %get-tuple-element.64), channel_id=1, source_target_pairs={{0,13},{1,12},{2,15},{3,14},{4,9},{5,8},{6,11},{7,10},{8,5},{9,4},... | collective-permute-start | bytes 196616 | tf_op jit(solution)/shard_map/ppermute | solution.py:286
  39.9 0.0 collective-permute-done.4.refs_5_
  39.9 2.1 %collective-permute-start.16 = (bf16[256,128]{1,0:T(8,128)(2,1)S(1)}, bf16[256,128]{1,0:T(8,128)(2,1)S(1)}, u32[]{:S(2)}, u32[]{:S(2)}) collective-permute-start(bf16[256,128]{1,0:T(8,128)(2,1)S(1)} %get-tuple-element.66), channel_id=1, source_target_pairs={{0,14},{1,15},{2,12},{3,13},{4,10},{5,11},{6,8},{7,9},{8,6},{9,7},... | collective-permute-start | bytes 196616 | tf_op jit(solution)/shard_map/ppermute | solution.py:286
  42.0 0.0 collective-permute-done.5.refs_6_
  42.0 0.7 %collective-permute-start.17 = (bf16[256,128]{1,0:T(8,128)(2,1)S(1)}, bf16[256,128]{1,0:T(8,128)(2,1)S(1)}, u32[]{:S(2)}, u32[]{:S(2)}) collective-permute-start(bf16[256,128]{1,0:T(8,128)(2,1)S(1)} %get-tuple-element.68), channel_id=1, source_target_pairs={{0,15},{1,14},{2,13},{3,12},{4,11},{5,10},{6,9},{7,8},{8,7},{9,6},... | collective-permute-start | bytes 196616 | tf_op jit(solution)/shard_map/ppermute | solution.py:286
  42.7 0.0 collective-permute-done.10.refs_11_
  42.7 2.8 %collective-permute-done.6.refs_7_ = bf16[256,256]{1,0:T(8,128)(2,1)S(1)} collective-permute-done((bf16[256,256]{1,0:T(8,128)(2,1)S(1)}, bf16[256,256]{1,0:T(8,128)(2,1)S(1)}, u32[]{:S(2)}, u32[]{:S(2)}) %collective-permute-start.6) | collective-permute-done | bytes 131104 | tf_op jit(solution)/shard_map/ppermute | solution.py:286
  45.5 0.0 copy-done.1
  45.5 1.2 %shard_map.51.gram = f32[256,256]{1,0:T(8,128)S(1)} custom-call(s32[1,16]{1,0:T(1,128)S(1)} %bitcast.2, bf16[256,256]{1,0:T(8,128)(2,1)S(1)} %get-tuple-element.38.refs_0_, bf16[256,256]{1,0:T(8,128)(2,1)S(1)} %collective-permute-done.refs_1_, bf16[256,256]{1,0:T(8,128)(2,1)S(1)} %collective-permute-done.1.refs_2_, ...), custom_call_target="tpu_custom_call" | custom-call | tf_op jit(solution)/shard_map/pallas_call | solution.py:288
  46.7 3.4 %shard_map.52 = (f32[128,128]{1,0:T(8,128)S(1)}, f32[128,128]{1,0:T(8,128)S(1)}) custom-call(s32[1,16]{1,0:T(1,128)S(1)} %bitcast.3, s32[1,1]{1,0:T(1,128)S(6)} %copy.5.size, f32[256,256]{1,0:T(8,128)S(1)} %shard_map.51.gram, bf16[256,128]{1,0:T(8,128)(2,1)S(1)} %collective-permute-done.11.refs_0_.refs_13_, ...), custom_call_target="tpu_custom_call" | custom-call | tf_op jit(solution)/shard_map/pallas_call | solution.py:296
  50.1 0.6 collective-permute-start.18
  50.7 0.0 collective-permute-done.15.refs_3_.refs_14_
  50.7 1.6 %collective-permute-done.16.refs_4_.refs_16_ = bf16[256,128]{1,0:T(8,128)(2,1)S(1)} collective-permute-done((bf16[256,128]{1,0:T(8,128)(2,1)S(1)}, bf16[256,128]{1,0:T(8,128)(2,1)S(1)}, u32[]{:S(2)}, u32[]{:S(2)}) %collective-permute-start.16) | collective-permute-done | bytes 65568 | tf_op jit(solution)/shard_map/ppermute | solution.py:286
  52.3 0.3 collective-permute-done.17.refs_5_.refs_18_
  52.7 4.3 %shard_map.53 = (f32[256,256]{1,0:T(8,128)S(1)}, f32[128,256]{1,0:T(8,128)S(1)}, f32[128,128]{1,0:T(8,128)S(1)}) custom-call(s32[1,16]{1,0:T(1,128)S(1)} %bitcast.4, s32[1,1]{1,0:T(1,128)S(6)} %copy.5.size, f32[256,256]{1,0:T(8,128)S(1)} %shard_map.51.gram, f32[128,128]{1,0:T(8,128)S(1)} %get-tuple-element.61.r_lead, ...), custom_call_target="tpu_custom_call" | custom-call | tf_op jit(solution)/shard_map/pallas_call | solution.py:310
  57.0 0.0 collective-permute-done.18.lead
  57.0 0.6 collective-permute-start.19
  57.6 3.2 %shard_map.54 = bf16[1,4096,256]{2,1,0:T(8,128)(2,1)} custom-call(s32[1,16]{1,0:T(1,128)S(1)} %bitcast.5, s32[1,1]{1,0:T(1,128)S(6)} %copy.5.size, f32[256,256]{1,0:T(8,128)S(1)} %get-tuple-element.69.factor.own, f32[128,128]{1,0:T(8,128)S(1)} %get-tuple-element.62.inverse_lead.lead, f32[128,128]{1,0:T(8,128)S(1)} %get-tuple-element.70.trail, ...), custom_call_target="tpu_custom_call" | custom-call | flops 1073741824 | bytes 4194304 | tf_op jit(solution)/shard_map/pallas_call | solution.py:320
  60.8 2.1 %collective-permute-done.19.rest = f32[128,256]{1,0:T(8,128)S(1)} collective-permute-done((f32[128,256]{1,0:T(8,128)S(1)}, f32[128,256]{1,0:T(8,128)S(1)}, u32[]{:S(2)}, u32[]{:S(2)}) %collective-permute-start.19) | collective-permute-done | bytes 131104 | tf_op jit(solution)/shard_map/ppermute | solution.py:307
  62.8 1.1 %shard_map.55 = f32[256,256]{1,0:T(8,128)} custom-call(f32[256,256]{1,0:T(8,128)S(1)} %get-tuple-element.69.factor.own, f32[128,128]{1,0:T(8,128)S(1)} %collective-permute-done.18.lead, f32[128,256]{1,0:T(8,128)S(1)} %collective-permute-done.19.rest), custom_call_target="tpu_custom_call" | custom-call | tf_op jit(solution)/shard_map/pallas_call | solution.py:339
  (2 shorter events, 0.0 us)
Async XLA Ops:
  0.6 1.6 %copy-start = (bf16[1,256,4096]{2,1,0:T(8,128)(2,1)S(1)}, bf16[1,256,4096]{2,1,0:T(8,128)(2,1)}, u32[]{:S(2)}) copy-start(bf16[1,256,4096]{2,1,0:T(8,128)(2,1)} %src.1) | copy-start | bytes 6291460
  2.2 43.2 %copy-start.1 = (s32[1,1,16]{2,1,0:T(1,128)S(1)}, s32[1,1,16]{2,1,0:T(1,128)}, u32[]{:S(2)}) copy-start(s32[1,1,16]{2,1,0:T(1,128)} %param.4) | copy-start | bytes 196
  2.7 4.3 %collective-permute-start = (bf16[256,256]{1,0:T(8,128)(2,1)S(1)}, bf16[256,256]{1,0:T(8,128)(2,1)S(1)}, u32[]{:S(2)}, u32[]{:S(2)}) collective-permute-start(bf16[256,256]{1,0:T(8,128)(2,1)S(1)} %get-tuple-element.39), channel_id=1, source_target_pairs={{0,1},{1,0},{2,3},{3,2},{4,5},{5,4},{6,7},{7,6},{8,9},{9,8},{10,11... | collective-permute-start | bytes 393224 | tf_op jit(solution)/shard_map/ppermute | solution.py:286
  2.8 13.0 %collective-permute-start.7 = (bf16[256,256]{1,0:T(8,128)(2,1)S(1)}, bf16[256,256]{1,0:T(8,128)(2,1)S(1)}, u32[]{:S(2)}, u32[]{:S(2)}) collective-permute-start(bf16[256,256]{1,0:T(8,128)(2,1)S(1)} %get-tuple-element.50), channel_id=1, source_target_pairs={{0,8},{1,9},{2,10},{3,11},{4,12},{5,13},{6,14},{7,15},{8,0},{9,1},... | collective-permute-start | bytes 393224 | tf_op jit(solution)/shard_map/ppermute | solution.py:286
  5.5 13.7 %collective-permute-start.1 = (bf16[256,256]{1,0:T(8,128)(2,1)S(1)}, bf16[256,256]{1,0:T(8,128)(2,1)S(1)}, u32[]{:S(2)}, u32[]{:S(2)}) collective-permute-start(bf16[256,256]{1,0:T(8,128)(2,1)S(1)} %get-tuple-element.40), channel_id=1, source_target_pairs={{0,2},{1,3},{2,0},{3,1},{4,6},{5,7},{6,4},{7,5},{8,10},{9,11},{10,... | collective-permute-start | bytes 393224 | tf_op jit(solution)/shard_map/ppermute | solution.py:286
  6.0 14.2 %collective-permute-start.2 = (bf16[256,256]{1,0:T(8,128)(2,1)S(1)}, bf16[256,256]{1,0:T(8,128)(2,1)S(1)}, u32[]{:S(2)}, u32[]{:S(2)}) collective-permute-start(bf16[256,256]{1,0:T(8,128)(2,1)S(1)} %get-tuple-element.41), channel_id=1, source_target_pairs={{0,3},{1,2},{2,1},{3,0},{4,7},{5,6},{6,5},{7,4},{8,11},{9,10},{10,... | collective-permute-start | bytes 393224 | tf_op jit(solution)/shard_map/ppermute | solution.py:286
  7.0 10.6 %collective-permute-start.11 = (bf16[256,128]{1,0:T(8,128)(2,1)S(1)}, bf16[256,128]{1,0:T(8,128)(2,1)S(1)}, u32[]{:S(2)}, u32[]{:S(2)}) collective-permute-start(bf16[256,128]{1,0:T(8,128)(2,1)S(1)} %get-tuple-element.57), channel_id=1, source_target_pairs={{0,13},{1,12},{2,15},{3,14},{4,9},{5,8},{6,11},{7,10},{8,5},{9,4},... | collective-permute-start | bytes 196616 | tf_op jit(solution)/shard_map/ppermute | solution.py:286
  7.0 14.1 %collective-permute-start.8 = (bf16[256,256]{1,0:T(8,128)(2,1)S(1)}, bf16[256,256]{1,0:T(8,128)(2,1)S(1)}, u32[]{:S(2)}, u32[]{:S(2)}) collective-permute-start(bf16[256,256]{1,0:T(8,128)(2,1)S(1)} %get-tuple-element.51), channel_id=1, source_target_pairs={{0,9},{1,8},{2,11},{3,10},{4,13},{5,12},{6,15},{7,14},{8,1},{9,0},... | collective-permute-start | bytes 393224 | tf_op jit(solution)/shard_map/ppermute | solution.py:286
  15.8 8.1 %collective-permute-start.3 = (bf16[256,256]{1,0:T(8,128)(2,1)S(1)}, bf16[256,256]{1,0:T(8,128)(2,1)S(1)}, u32[]{:S(2)}, u32[]{:S(2)}) collective-permute-start(bf16[256,256]{1,0:T(8,128)(2,1)S(1)} %get-tuple-element.43), channel_id=1, source_target_pairs={{0,4},{1,5},{2,6},{3,7},{4,0},{5,1},{6,2},{7,3},{8,12},{9,13},{10,... | collective-permute-start | bytes 393224 | tf_op jit(solution)/shard_map/ppermute | solution.py:286
  17.6 18.4 %collective-permute-start.9 = (bf16[256,256]{1,0:T(8,128)(2,1)S(1)}, bf16[256,256]{1,0:T(8,128)(2,1)S(1)}, u32[]{:S(2)}, u32[]{:S(2)}) collective-permute-start(bf16[256,256]{1,0:T(8,128)(2,1)S(1)} %get-tuple-element.53), channel_id=1, source_target_pairs={{0,10},{1,11},{2,8},{3,9},{4,14},{5,15},{6,12},{7,13},{8,2},{9,3},... | collective-permute-start | bytes 393224 | tf_op jit(solution)/shard_map/ppermute | solution.py:286
  19.1 15.1 %collective-permute-start.13 = (bf16[256,128]{1,0:T(8,128)(2,1)S(1)}, bf16[256,128]{1,0:T(8,128)(2,1)S(1)}, u32[]{:S(2)}, u32[]{:S(2)}) collective-permute-start(bf16[256,128]{1,0:T(8,128)(2,1)S(1)} %get-tuple-element.59), channel_id=1, source_target_pairs={{0,14},{1,15},{2,12},{3,13},{4,10},{5,11},{6,8},{7,9},{8,6},{9,7},... | collective-permute-start | bytes 196616 | tf_op jit(solution)/shard_map/ppermute | solution.py:286
  20.2 14.2 %collective-permute-start.14 = (bf16[256,128]{1,0:T(8,128)(2,1)S(1)}, bf16[256,128]{1,0:T(8,128)(2,1)S(1)}, u32[]{:S(2)}, u32[]{:S(2)}) collective-permute-start(bf16[256,128]{1,0:T(8,128)(2,1)S(1)} %get-tuple-element.60), channel_id=1, source_target_pairs={{0,15},{1,14},{2,13},{3,12},{4,11},{5,10},{6,9},{7,8},{8,7},{9,6},... | collective-permute-start | bytes 196616 | tf_op jit(solution)/shard_map/ppermute | solution.py:286
  21.1 17.9 %collective-permute-start.12 = (bf16[256,256]{1,0:T(8,128)(2,1)S(1)}, bf16[256,256]{1,0:T(8,128)(2,1)S(1)}, u32[]{:S(2)}, u32[]{:S(2)}) collective-permute-start(bf16[256,256]{1,0:T(8,128)(2,1)S(1)} %get-tuple-element.58), channel_id=1, source_target_pairs={{0,12},{1,13},{2,14},{3,15},{4,8},{5,9},{6,10},{7,11},{8,4},{9,5},... | collective-permute-start | bytes 393224 | tf_op jit(solution)/shard_map/ppermute | solution.py:286
  23.9 16.0 %collective-permute-start.4 = (bf16[256,256]{1,0:T(8,128)(2,1)S(1)}, bf16[256,256]{1,0:T(8,128)(2,1)S(1)}, u32[]{:S(2)}, u32[]{:S(2)}) collective-permute-start(bf16[256,256]{1,0:T(8,128)(2,1)S(1)} %get-tuple-element.45), channel_id=1, source_target_pairs={{0,5},{1,4},{2,7},{3,6},{4,1},{5,0},{6,3},{7,2},{8,13},{9,12},{10,... | collective-permute-start | bytes 393224 | tf_op jit(solution)/shard_map/ppermute | solution.py:286
  34.3 7.8 %collective-permute-start.5 = (bf16[256,256]{1,0:T(8,128)(2,1)S(1)}, bf16[256,256]{1,0:T(8,128)(2,1)S(1)}, u32[]{:S(2)}, u32[]{:S(2)}) collective-permute-start(bf16[256,256]{1,0:T(8,128)(2,1)S(1)} %get-tuple-element.47), channel_id=1, source_target_pairs={{0,6},{1,7},{2,4},{3,5},{4,2},{5,3},{6,0},{7,1},{8,14},{9,15},{10,... | collective-permute-start | bytes 393224 | tf_op jit(solution)/shard_map/ppermute | solution.py:286
  34.4 8.3 %collective-permute-start.10 = (bf16[256,256]{1,0:T(8,128)(2,1)S(1)}, bf16[256,256]{1,0:T(8,128)(2,1)S(1)}, u32[]{:S(2)}, u32[]{:S(2)}) collective-permute-start(bf16[256,256]{1,0:T(8,128)(2,1)S(1)} %get-tuple-element.55), channel_id=1, source_target_pairs={{0,11},{1,10},{2,9},{3,8},{4,15},{5,14},{6,13},{7,12},{8,3},{9,2},... | collective-permute-start | bytes 393224 | tf_op jit(solution)/shard_map/ppermute | solution.py:286
  36.0 9.5 %collective-permute-start.6 = (bf16[256,256]{1,0:T(8,128)(2,1)S(1)}, bf16[256,256]{1,0:T(8,128)(2,1)S(1)}, u32[]{:S(2)}, u32[]{:S(2)}) collective-permute-start(bf16[256,256]{1,0:T(8,128)(2,1)S(1)} %get-tuple-element.49), channel_id=1, source_target_pairs={{0,7},{1,6},{2,5},{3,4},{4,3},{5,2},{6,1},{7,0},{8,15},{9,14},{10,... | collective-permute-start | bytes 393224 | tf_op jit(solution)/shard_map/ppermute | solution.py:286
  39.1 11.6 %collective-permute-start.15 = (bf16[256,128]{1,0:T(8,128)(2,1)S(1)}, bf16[256,128]{1,0:T(8,128)(2,1)S(1)}, u32[]{:S(2)}, u32[]{:S(2)}) collective-permute-start(bf16[256,128]{1,0:T(8,128)(2,1)S(1)} %get-tuple-element.64), channel_id=1, source_target_pairs={{0,13},{1,12},{2,15},{3,14},{4,9},{5,8},{6,11},{7,10},{8,5},{9,4},... | collective-permute-start | bytes 196616 | tf_op jit(solution)/shard_map/ppermute | solution.py:286
  39.9 12.4 %collective-permute-start.16 = (bf16[256,128]{1,0:T(8,128)(2,1)S(1)}, bf16[256,128]{1,0:T(8,128)(2,1)S(1)}, u32[]{:S(2)}, u32[]{:S(2)}) collective-permute-start(bf16[256,128]{1,0:T(8,128)(2,1)S(1)} %get-tuple-element.66), channel_id=1, source_target_pairs={{0,14},{1,15},{2,12},{3,13},{4,10},{5,11},{6,8},{7,9},{8,6},{9,7},... | collective-permute-start | bytes 196616 | tf_op jit(solution)/shard_map/ppermute | solution.py:286
  42.0 10.6 %collective-permute-start.17 = (bf16[256,128]{1,0:T(8,128)(2,1)S(1)}, bf16[256,128]{1,0:T(8,128)(2,1)S(1)}, u32[]{:S(2)}, u32[]{:S(2)}) collective-permute-start(bf16[256,128]{1,0:T(8,128)(2,1)S(1)} %get-tuple-element.68), channel_id=1, source_target_pairs={{0,15},{1,14},{2,13},{3,12},{4,11},{5,10},{6,9},{7,8},{8,7},{9,6},... | collective-permute-start | bytes 196616 | tf_op jit(solution)/shard_map/ppermute | solution.py:286
  50.1 6.9 %collective-permute-start.18 = (f32[128,128]{1,0:T(8,128)S(1)}, f32[128,128]{1,0:T(8,128)S(1)}, u32[]{:S(2)}, u32[]{:S(2)}) collective-permute-start(f32[128,128]{1,0:T(8,128)S(1)} %get-tuple-element.61.r_lead), channel_id=1, source_target_pairs={{0,16},{16,0},{1,17},{17,1},{2,18},{18,2},{3,19},{19,3},{4,20},{20... | collective-permute-start | bytes 196616 | tf_op jit(solution)/shard_map/ppermute | solution.py:307
  57.0 5.8 %collective-permute-start.19 = (f32[128,256]{1,0:T(8,128)S(1)}, f32[128,256]{1,0:T(8,128)S(1)}, u32[]{:S(2)}, u32[]{:S(2)}) collective-permute-start(f32[128,256]{1,0:T(8,128)S(1)} %get-tuple-element.73), channel_id=1, source_target_pairs={{0,16},{16,0},{1,17},{17,1},{2,18},{18,2},{3,19},{19,3},{4,20},{20... | collective-permute-start | bytes 393224 | tf_op jit(solution)/shard_map/ppermute | solution.py:307

commit v8 on v7

--- a/solution.py
+++ b/solution.py
@@ -160,6 +160,14 @@
     factor_block(shifted(g, size, 0, 0), r_out, inverse_out, w)
 
 
+def thrice(x, y):
+    x_high, y_high = x.astype(jnp.bfloat16), y.astype(jnp.bfloat16)
+    x_low = (x - x_high.astype(jnp.float32)).astype(jnp.bfloat16)
+    y_low = (y - y_high.astype(jnp.float32)).astype(jnp.bfloat16)
+    left = jnp.concatenate([x_high, x_high, x_low], axis=1)
+    return jnp.dot(left, jnp.concatenate([y_high, y_low, y_high], axis=0), preferred_element_type=jnp.float32)
+
+
 def trailing_factor(rounds, rows, compat, size, gram, r_lead, inverse_lead, *refs):
     *blocks, r_out, rest_out, inverse_out, w = refs
     first, second = blocks[: len(rounds)], blocks[len(rounds) :]
@@ -167,7 +175,7 @@
     cross = shifted(gram[:h, h:] + gram_of(rounds, rows, compat, first, second), size, 0, h)
     own = shifted(gram[h:, h:] + gram_of(rounds, rows, compat, second), size, h, h)
     dot = functools.partial(jnp.dot, preferred_element_type=jnp.float32)
-    right = dot(inverse_lead[...], cross, precision=HIGHEST)
+    right = thrice(inverse_lead[...], cross)
     down_t = functools.partial(
         lax.dot_general,
         dimension_numbers=(((0,), (0,)), ((), ())),
@@ -227,9 +235,8 @@
 
     @pl.when(later)
     def _():
-        dot = functools.partial(jnp.dot, precision=HIGHEST, preferred_element_type=jnp.float32)
-        top = dot(own[:h, :h], jnp.concatenate([lead[...], rest[:, :h]], axis=1))
-        right = dot(own[:, h:], rest[:, h:])
+        top = thrice(own[:h, :h], jnp.concatenate([lead[...], rest[:, :h]], axis=1))
+        right = thrice(own[:, h:], rest[:, h:])
         out[:h, :h] = top[:, :h]
         out[:h, h:] = top[:, h:] + right[:h, :]
         out[h:, :h] = jnp.zeros((h, h), jnp.float32)
@@ -290,6 +297,7 @@
         out_shape=f32((width, width)),
         in_specs=[in_smem] + [in_vmem] * len(early),
         out_specs=in_vmem,
+        cost_estimate=pl.CostEstimate(flops=2 * rows * width * width, bytes_accessed=2 * rows * width, transcendentals=0),
         compiler_params=PARAMS,
     )(compat[0], *[got[r, 0, width] for r in early])
     firsts, seconds = [got[key] for key in first], [got[key] for key in second]

time: 64.7 us -> 64.6 us (level)
  no operation moved by 1% of the time
where the time goes in v8:
time: 64.6 us; the launch traced here: 63.7 us
  starting transfers between devices  24.2 us (37%)
  waiting for transfers between devices  23.1 us (36%)
  Pallas kernels  13.5 us (21%)
  local copies, waits for them, and re-layouts  1.59 us (2%)
  between operations  1.37 us (2%)
    ppermute x18, starting transfers between devices, local(): lax.ppermute(block, 'blk', [(k, k ^ key[0]) for k in range(parts)])  23 us
    ppermute x18, waiting for transfers between devices, local(): lax.ppermute(block, 'blk', [(k, k ^ key[0]) for k in range(parts)])  21 us
    pallas_call x1, Pallas kernels, local(): pl.pallas_call(functools.partial(trailing_factor, late, rows), out_shape=...  4.25 us
    pallas_call x1, Pallas kernels, local(): pl.pallas_call(functools.partial(leading_factor, late, rows), out_shape=(...  3.43 us
    pallas_call x1, Pallas kernels, local(): pl.pallas_call(functools.partial(orthonormal_rows, rounds, rows), out_sha...  3.18 us
    ppermute x2, waiting for transfers between devices, onward(): return lax.ppermute(x, 'seg', [(i, (i + by) % sites) for i in range(sites)])  2.05 us
    unnamed x4, local copies, waits for them, and re-layouts  1.59 us
  transfers between devices with their start and end apart: 20, of which 8 were waited for; matrix products, arithmetic and copies ran while one was open for 0% of the time, Pallas kernels for 19%

profile of v8, /device:TPU:14, one launch (start us, length us, event | category | flops | bytes accessed | tf_op | source)
XLA Modules:
  0.0 63.7 jit_solution(16941723982579884475)
XLA Ops:
  0.6 0.0 copy-start
  0.6 1.6 %copy-done = bf16[1,256,4096]{2,1,0:T(8,128)(2,1)S(1)} copy-done((bf16[1,256,4096]{2,1,0:T(8,128)(2,1)S(1)}, bf16[1,256,4096]{2,1,0:T(8,128)(2,1)}, u32[]{:S(2)}) %copy-start) | copy-done | bytes 2097176
  2.2 0.5 shard_map.50
  2.7 0.1 collective-permute-start
  2.8 2.7 %collective-permute-start.7 = (bf16[256,256]{1,0:T(8,128)(2,1)S(1)}, bf16[256,256]{1,0:T(8,128)(2,1)S(1)}, u32[]{:S(2)}, u32[]{:S(2)}) collective-permute-start(bf16[256,256]{1,0:T(8,128)(2,1)S(1)} %get-tuple-element.50), channel_id=1, source_target_pairs={{0,8},{1,9},{2,10},{3,11},{4,12},{5,13},{6,14},{7,15},{8,0},{9,1},... | collective-permute-start | bytes 393224 | tf_op jit(solution)/shard_map/ppermute | solution.py:293
  5.5 0.5 collective-permute-start.1
  6.0 1.0 %collective-permute-start.2 = (bf16[256,256]{1,0:T(8,128)(2,1)S(1)}, bf16[256,256]{1,0:T(8,128)(2,1)S(1)}, u32[]{:S(2)}, u32[]{:S(2)}) collective-permute-start(bf16[256,256]{1,0:T(8,128)(2,1)S(1)} %get-tuple-element.41), channel_id=1, source_target_pairs={{0,3},{1,2},{2,1},{3,0},{4,7},{5,6},{6,5},{7,4},{8,11},{9,10},{10,... | collective-permute-start | bytes 393224 | tf_op jit(solution)/shard_map/ppermute | solution.py:293
  7.0 0.0 collective-permute-start.11
  7.0 0.0 collective-permute-done.refs_1_
  7.0 2.5 %collective-permute-start.8 = (bf16[256,256]{1,0:T(8,128)(2,1)S(1)}, bf16[256,256]{1,0:T(8,128)(2,1)S(1)}, u32[]{:S(2)}, u32[]{:S(2)}) collective-permute-start(bf16[256,256]{1,0:T(8,128)(2,1)S(1)} %get-tuple-element.51), channel_id=1, source_target_pairs={{0,9},{1,8},{2,11},{3,10},{4,13},{5,12},{6,15},{7,14},{8,1},{9,0},... | collective-permute-start | bytes 393224 | tf_op jit(solution)/shard_map/ppermute | solution.py:293
  9.5 6.3 %collective-permute-done.7.refs_8_ = bf16[256,256]{1,0:T(8,128)(2,1)S(1)} collective-permute-done((bf16[256,256]{1,0:T(8,128)(2,1)S(1)}, bf16[256,256]{1,0:T(8,128)(2,1)S(1)}, u32[]{:S(2)}, u32[]{:S(2)}) %collective-permute-start.7) | collective-permute-done | bytes 131104 | tf_op jit(solution)/shard_map/ppermute | solution.py:293
  15.8 1.8 %collective-permute-start.3 = (bf16[256,256]{1,0:T(8,128)(2,1)S(1)}, bf16[256,256]{1,0:T(8,128)(2,1)S(1)}, u32[]{:S(2)}, u32[]{:S(2)}) collective-permute-start(bf16[256,256]{1,0:T(8,128)(2,1)S(1)} %get-tuple-element.43), channel_id=1, source_target_pairs={{0,4},{1,5},{2,6},{3,7},{4,0},{5,1},{6,2},{7,3},{8,12},{9,13},{10,... | collective-permute-start | bytes 393224 | tf_op jit(solution)/shard_map/ppermute | solution.py:293
  17.6 0.0 collective-permute-done.11.refs_0_.refs_13_
  17.6 1.6 %collective-permute-start.9 = (bf16[256,256]{1,0:T(8,128)(2,1)S(1)}, bf16[256,256]{1,0:T(8,128)(2,1)S(1)}, u32[]{:S(2)}, u32[]{:S(2)}) collective-permute-start(bf16[256,256]{1,0:T(8,128)(2,1)S(1)} %get-tuple-element.53), channel_id=1, source_target_pairs={{0,10},{1,11},{2,8},{3,9},{4,14},{5,15},{6,12},{7,13},{8,2},{9,3},... | collective-permute-start | bytes 393224 | tf_op jit(solution)/shard_map/ppermute | solution.py:293
  19.1 0.0 collective-permute-done.1.refs_2_
  19.1 1.1 %collective-permute-start.13 = (bf16[256,128]{1,0:T(8,128)(2,1)S(1)}, bf16[256,128]{1,0:T(8,128)(2,1)S(1)}, u32[]{:S(2)}, u32[]{:S(2)}) collective-permute-start(bf16[256,128]{1,0:T(8,128)(2,1)S(1)} %get-tuple-element.59), channel_id=1, source_target_pairs={{0,14},{1,15},{2,12},{3,13},{4,10},{5,11},{6,8},{7,9},{8,6},{9,7},... | collective-permute-start | bytes 196616 | tf_op jit(solution)/shard_map/ppermute | solution.py:293
  20.2 0.0 collective-permute-done.2.refs_3_
  20.2 0.9 %collective-permute-start.14 = (bf16[256,128]{1,0:T(8,128)(2,1)S(1)}, bf16[256,128]{1,0:T(8,128)(2,1)S(1)}, u32[]{:S(2)}, u32[]{:S(2)}) collective-permute-start(bf16[256,128]{1,0:T(8,128)(2,1)S(1)} %get-tuple-element.60), channel_id=1, source_target_pairs={{0,15},{1,14},{2,13},{3,12},{4,11},{5,10},{6,9},{7,8},{8,7},{9,6},... | collective-permute-start | bytes 196616 | tf_op jit(solution)/shard_map/ppermute | solution.py:293
  21.1 0.0 collective-permute-done.8.refs_9_
  21.1 1.1 %collective-permute-start.12 = (bf16[256,256]{1,0:T(8,128)(2,1)S(1)}, bf16[256,256]{1,0:T(8,128)(2,1)S(1)}, u32[]{:S(2)}, u32[]{:S(2)}) collective-permute-start(bf16[256,256]{1,0:T(8,128)(2,1)S(1)} %get-tuple-element.58), channel_id=1, source_target_pairs={{0,12},{1,13},{2,14},{3,15},{4,8},{5,9},{6,10},{7,11},{8,4},{9,5},... | collective-permute-start | bytes 393224 | tf_op jit(solution)/shard_map/ppermute | solution.py:293
  22.2 1.7 %collective-permute-done.3.refs_4_ = bf16[256,256]{1,0:T(8,128)(2,1)S(1)} collective-permute-done((bf16[256,256]{1,0:T(8,128)(2,1)S(1)}, bf16[256,256]{1,0:T(8,128)(2,1)S(1)}, u32[]{:S(2)}, u32[]{:S(2)}) %collective-permute-start.3) | collective-permute-done | bytes 131104 | tf_op jit(solution)/shard_map/ppermute | solution.py:293
  23.9 2.2 %collective-permute-start.4 = (bf16[256,256]{1,0:T(8,128)(2,1)S(1)}, bf16[256,256]{1,0:T(8,128)(2,1)S(1)}, u32[]{:S(2)}, u32[]{:S(2)}) collective-permute-start(bf16[256,256]{1,0:T(8,128)(2,1)S(1)} %get-tuple-element.45), channel_id=1, source_target_pairs={{0,5},{1,4},{2,7},{3,6},{4,1},{5,0},{6,3},{7,2},{8,13},{9,12},{10,... | collective-permute-start | bytes 393224 | tf_op jit(solution)/shard_map/ppermute | solution.py:293
  26.1 8.2 %collective-permute-done.13.refs_1_.refs_15_ = bf16[256,128]{1,0:T(8,128)(2,1)S(1)} collective-permute-done((bf16[256,128]{1,0:T(8,128)(2,1)S(1)}, bf16[256,128]{1,0:T(8,128)(2,1)S(1)}, u32[]{:S(2)}, u32[]{:S(2)}) %collective-permute-start.13) | collective-permute-done | bytes 65568 | tf_op jit(solution)/shard_map/ppermute | solution.py:293
  34.3 0.0 collective-permute-start.5
  34.3 0.1 collective-permute-done.14.refs_2_.refs_17_
  34.4 1.6 %collective-permute-start.10 = (bf16[256,256]{1,0:T(8,128)(2,1)S(1)}, bf16[256,256]{1,0:T(8,128)(2,1)S(1)}, u32[]{:S(2)}, u32[]{:S(2)}) collective-permute-start(bf16[256,256]{1,0:T(8,128)(2,1)S(1)} %get-tuple-element.55), channel_id=1, source_target_pairs={{0,11},{1,10},{2,9},{3,8},{4,15},{5,14},{6,13},{7,12},{8,3},{9,2},... | collective-permute-start | bytes 393224 | tf_op jit(solution)/shard_map/ppermute | solution.py:293
  35.9 0.0 collective-permute-done.9.refs_10_
  36.0 2.5 %collective-permute-start.6 = (bf16[256,256]{1,0:T(8,128)(2,1)S(1)}, bf16[256,256]{1,0:T(8,128)(2,1)S(1)}, u32[]{:S(2)}, u32[]{:S(2)}) collective-permute-start(bf16[256,256]{1,0:T(8,128)(2,1)S(1)} %get-tuple-element.49), channel_id=1, source_target_pairs={{0,7},{1,6},{2,5},{3,4},{4,3},{5,2},{6,1},{7,0},{8,15},{9,14},{10,... | collective-permute-start | bytes 393224 | tf_op jit(solution)/shard_map/ppermute | solution.py:293
  39.1 0.0 collective-permute-done.12.refs_12_
  39.1 0.9 %collective-permute-start.15 = (bf16[256,128]{1,0:T(8,128)(2,1)S(1)}, bf16[256,128]{1,0:T(8,128)(2,1)S(1)}, u32[]{:S(2)}, u32[]{:S(2)}) collective-permute-start(bf16[256,128]{1,0:T(8,128)(2,1)S(1)} %get-tuple-element.64), channel_id=1, source_target_pairs={{0,13},{1,12},{2,15},{3,14},{4,9},{5,8},{6,11},{7,10},{8,5},{9,4},... | collective-permute-start | bytes 196616 | tf_op jit(solution)/shard_map/ppermute | solution.py:293
  39.9 0.0 collective-permute-done.4.refs_5_
  39.9 2.1 %collective-permute-start.16 = (bf16[256,128]{1,0:T(8,128)(2,1)S(1)}, bf16[256,128]{1,0:T(8,128)(2,1)S(1)}, u32[]{:S(2)}, u32[]{:S(2)}) collective-permute-start(bf16[256,128]{1,0:T(8,128)(2,1)S(1)} %get-tuple-element.66), channel_id=1, source_target_pairs={{0,14},{1,15},{2,12},{3,13},{4,10},{5,11},{6,8},{7,9},{8,6},{9,7},... | collective-permute-start | bytes 196616 | tf_op jit(solution)/shard_map/ppermute | solution.py:293
  42.0 0.0 collective-permute-done.5.refs_6_
  42.0 0.7 %collective-permute-start.17 = (bf16[256,128]{1,0:T(8,128)(2,1)S(1)}, bf16[256,128]{1,0:T(8,128)(2,1)S(1)}, u32[]{:S(2)}, u32[]{:S(2)}) collective-permute-start(bf16[256,128]{1,0:T(8,128)(2,1)S(1)} %get-tuple-element.68), channel_id=1, source_target_pairs={{0,15},{1,14},{2,13},{3,12},{4,11},{5,10},{6,9},{7,8},{8,7},{9,6},... | collective-permute-start | bytes 196616 | tf_op jit(solution)/shard_map/ppermute | solution.py:293
  42.7 0.0 collective-permute-done.10.refs_11_
  42.7 2.8 %collective-permute-done.6.refs_7_ = bf16[256,256]{1,0:T(8,128)(2,1)S(1)} collective-permute-done((bf16[256,256]{1,0:T(8,128)(2,1)S(1)}, bf16[256,256]{1,0:T(8,128)(2,1)S(1)}, u32[]{:S(2)}, u32[]{:S(2)}) %collective-permute-start.6) | collective-permute-done | bytes 131104 | tf_op jit(solution)/shard_map/ppermute | solution.py:293
  45.5 1.2 %shard_map.51.gram = f32[256,256]{1,0:T(8,128)S(1)} custom-call(s32[1,16]{1,0:T(1,128)S(1)} %bitcast.2, bf16[256,256]{1,0:T(8,128)(2,1)S(1)} %get-tuple-element.38.refs_0_, bf16[256,256]{1,0:T(8,128)(2,1)S(1)} %collective-permute-done.refs_1_, bf16[256,256]{1,0:T(8,128)(2,1)S(1)} %collective-permute-done.1.refs_2_, ...), custom_call_target="tpu_custom_call" | custom-call | flops 536870912 | bytes 2097152 | tf_op jit(solution)/shard_map/pallas_call | solution.py:295
  46.7 3.4 %shard_map.52 = (f32[128,128]{1,0:T(8,128)S(1)}, f32[128,128]{1,0:T(8,128)S(1)}) custom-call(s32[1,16]{1,0:T(1,128)S(1)} %bitcast.3, s32[1,1]{1,0:T(1,128)S(6)} %copy.5.size, f32[256,256]{1,0:T(8,128)S(1)} %shard_map.51.gram, bf16[256,128]{1,0:T(8,128)(2,1)S(1)} %collective-permute-done.11.refs_0_.refs_13_, ...), custom_call_target="tpu_custom_call" | custom-call | tf_op jit(solution)/shard_map/pallas_call | solution.py:304
  50.1 0.6 collective-permute-start.18
  50.7 0.0 collective-permute-done.15.refs_3_.refs_14_
  50.7 1.6 %collective-permute-done.16.refs_4_.refs_16_ = bf16[256,128]{1,0:T(8,128)(2,1)S(1)} collective-permute-done((bf16[256,128]{1,0:T(8,128)(2,1)S(1)}, bf16[256,128]{1,0:T(8,128)(2,1)S(1)}, u32[]{:S(2)}, u32[]{:S(2)}) %collective-permute-start.16) | collective-permute-done | bytes 65568 | tf_op jit(solution)/shard_map/ppermute | solution.py:293
  52.3 0.3 collective-permute-done.17.refs_5_.refs_18_
  52.7 4.2 %shard_map.53 = (f32[256,256]{1,0:T(8,128)S(1)}, f32[128,256]{1,0:T(8,128)S(1)}, f32[128,128]{1,0:T(8,128)S(1)}) custom-call(s32[1,16]{1,0:T(1,128)S(1)} %bitcast.4, s32[1,1]{1,0:T(1,128)S(6)} %copy.5.size, f32[256,256]{1,0:T(8,128)S(1)} %shard_map.51.gram, f32[128,128]{1,0:T(8,128)S(1)} %get-tuple-element.61.r_lead, ...), custom_call_target="tpu_custom_call" | custom-call | tf_op jit(solution)/shard_map/pallas_call | solution.py:318
  56.9 0.0 collective-permute-done.18.lead
  56.9 0.6 collective-permute-start.19
  57.5 3.2 %shard_map.54 = bf16[1,4096,256]{2,1,0:T(8,128)(2,1)} custom-call(s32[1,16]{1,0:T(1,128)S(1)} %bitcast.5, s32[1,1]{1,0:T(1,128)S(6)} %copy.5.size, f32[256,256]{1,0:T(8,128)S(1)} %get-tuple-element.69.factor.own, f32[128,128]{1,0:T(8,128)S(1)} %get-tuple-element.62.inverse_lead.lead, f32[128,128]{1,0:T(8,128)S(1)} %get-tuple-element.70.trail, ...), custom_call_target="tpu_custom_call" | custom-call | flops 1073741824 | bytes 4194304 | tf_op jit(solution)/shard_map/pallas_call | solution.py:328
  60.7 2.1 %collective-permute-done.19.rest = f32[128,256]{1,0:T(8,128)S(1)} collective-permute-done((f32[128,256]{1,0:T(8,128)S(1)}, f32[128,256]{1,0:T(8,128)S(1)}, u32[]{:S(2)}, u32[]{:S(2)}) %collective-permute-start.19) | collective-permute-done | bytes 131104 | tf_op jit(solution)/shard_map/ppermute | solution.py:315
  62.8 0.9 %shard_map.55 = f32[256,256]{1,0:T(8,128)} custom-call(f32[256,256]{1,0:T(8,128)S(1)} %get-tuple-element.69.factor.own, f32[128,128]{1,0:T(8,128)S(1)} %collective-permute-done.18.lead, f32[128,256]{1,0:T(8,128)S(1)} %collective-permute-done.19.rest), custom_call_target="tpu_custom_call" | custom-call | tf_op jit(solution)/shard_map/pallas_call | solution.py:347
  (2 shorter events, 0.0 us)
Async XLA Ops:
  0.6 1.6 %copy-start = (bf16[1,256,4096]{2,1,0:T(8,128)(2,1)S(1)}, bf16[1,256,4096]{2,1,0:T(8,128)(2,1)}, u32[]{:S(2)}) copy-start(bf16[1,256,4096]{2,1,0:T(8,128)(2,1)} %src.1) | copy-start | bytes 6291460
  2.2 43.2 %copy-start.1 = (s32[1,1,16]{2,1,0:T(1,128)S(1)}, s32[1,1,16]{2,1,0:T(1,128)}, u32[]{:S(2)}) copy-start(s32[1,1,16]{2,1,0:T(1,128)} %param.4) | copy-start | bytes 196
  2.7 4.3 %collective-permute-start = (bf16[256,256]{1,0:T(8,128)(2,1)S(1)}, bf16[256,256]{1,0:T(8,128)(2,1)S(1)}, u32[]{:S(2)}, u32[]{:S(2)}) collective-permute-start(bf16[256,256]{1,0:T(8,128)(2,1)S(1)} %get-tuple-element.39), channel_id=1, source_target_pairs={{0,1},{1,0},{2,3},{3,2},{4,5},{5,4},{6,7},{7,6},{8,9},{9,8},{10,11... | collective-permute-start | bytes 393224 | tf_op jit(solution)/shard_map/ppermute | solution.py:293
  2.8 13.0 %collective-permute-start.7 = (bf16[256,256]{1,0:T(8,128)(2,1)S(1)}, bf16[256,256]{1,0:T(8,128)(2,1)S(1)}, u32[]{:S(2)}, u32[]{:S(2)}) collective-permute-start(bf16[256,256]{1,0:T(8,128)(2,1)S(1)} %get-tuple-element.50), channel_id=1, source_target_pairs={{0,8},{1,9},{2,10},{3,11},{4,12},{5,13},{6,14},{7,15},{8,0},{9,1},... | collective-permute-start | bytes 393224 | tf_op jit(solution)/shard_map/ppermute | solution.py:293
  5.5 13.7 %collective-permute-start.1 = (bf16[256,256]{1,0:T(8,128)(2,1)S(1)}, bf16[256,256]{1,0:T(8,128)(2,1)S(1)}, u32[]{:S(2)}, u32[]{:S(2)}) collective-permute-start(bf16[256,256]{1,0:T(8,128)(2,1)S(1)} %get-tuple-element.40), channel_id=1, source_target_pairs={{0,2},{1,3},{2,0},{3,1},{4,6},{5,7},{6,4},{7,5},{8,10},{9,11},{10,... | collective-permute-start | bytes 393224 | tf_op jit(solution)/shard_map/ppermute | solution.py:293
  6.0 14.2 %collective-permute-start.2 = (bf16[256,256]{1,0:T(8,128)(2,1)S(1)}, bf16[256,256]{1,0:T(8,128)(2,1)S(1)}, u32[]{:S(2)}, u32[]{:S(2)}) collective-permute-start(bf16[256,256]{1,0:T(8,128)(2,1)S(1)} %get-tuple-element.41), channel_id=1, source_target_pairs={{0,3},{1,2},{2,1},{3,0},{4,7},{5,6},{6,5},{7,4},{8,11},{9,10},{10,... | collective-permute-start | bytes 393224 | tf_op jit(solution)/shard_map/ppermute | solution.py:293
  7.0 10.6 %collective-permute-start.11 = (bf16[256,128]{1,0:T(8,128)(2,1)S(1)}, bf16[256,128]{1,0:T(8,128)(2,1)S(1)}, u32[]{:S(2)}, u32[]{:S(2)}) collective-permute-start(bf16[256,128]{1,0:T(8,128)(2,1)S(1)} %get-tuple-element.57), channel_id=1, source_target_pairs={{0,13},{1,12},{2,15},{3,14},{4,9},{5,8},{6,11},{7,10},{8,5},{9,4},... | collective-permute-start | bytes 196616 | tf_op jit(solution)/shard_map/ppermute | solution.py:293
  7.0 14.1 %collective-permute-start.8 = (bf16[256,256]{1,0:T(8,128)(2,1)S(1)}, bf16[256,256]{1,0:T(8,128)(2,1)S(1)}, u32[]{:S(2)}, u32[]{:S(2)}) collective-permute-start(bf16[256,256]{1,0:T(8,128)(2,1)S(1)} %get-tuple-element.51), channel_id=1, source_target_pairs={{0,9},{1,8},{2,11},{3,10},{4,13},{5,12},{6,15},{7,14},{8,1},{9,0},... | collective-permute-start | bytes 393224 | tf_op jit(solution)/shard_map/ppermute | solution.py:293
  15.8 8.1 %collective-permute-start.3 = (bf16[256,256]{1,0:T(8,128)(2,1)S(1)}, bf16[256,256]{1,0:T(8,128)(2,1)S(1)}, u32[]{:S(2)}, u32[]{:S(2)}) collective-permute-start(bf16[256,256]{1,0:T(8,128)(2,1)S(1)} %get-tuple-element.43), channel_id=1, source_target_pairs={{0,4},{1,5},{2,6},{3,7},{4,0},{5,1},{6,2},{7,3},{8,12},{9,13},{10,... | collective-permute-start | bytes 393224 | tf_op jit(solution)/shard_map/ppermute | solution.py:293
  17.6 18.4 %collective-permute-start.9 = (bf16[256,256]{1,0:T(8,128)(2,1)S(1)}, bf16[256,256]{1,0:T(8,128)(2,1)S(1)}, u32[]{:S(2)}, u32[]{:S(2)}) collective-permute-start(bf16[256,256]{1,0:T(8,128)(2,1)S(1)} %get-tuple-element.53), channel_id=1, source_target_pairs={{0,10},{1,11},{2,8},{3,9},{4,14},{5,15},{6,12},{7,13},{8,2},{9,3},... | collective-permute-start | bytes 393224 | tf_op jit(solution)/shard_map/ppermute | solution.py:293
  19.1 15.1 %collective-permute-start.13 = (bf16[256,128]{1,0:T(8,128)(2,1)S(1)}, bf16[256,128]{1,0:T(8,128)(2,1)S(1)}, u32[]{:S(2)}, u32[]{:S(2)}) collective-permute-start(bf16[256,128]{1,0:T(8,128)(2,1)S(1)} %get-tuple-element.59), channel_id=1, source_target_pairs={{0,14},{1,15},{2,12},{3,13},{4,10},{5,11},{6,8},{7,9},{8,6},{9,7},... | collective-permute-start | bytes 196616 | tf_op jit(solution)/shard_map/ppermute | solution.py:293
  20.2 14.2 %collective-permute-start.14 = (bf16[256,128]{1,0:T(8,128)(2,1)S(1)}, bf16[256,128]{1,0:T(8,128)(2,1)S(1)}, u32[]{:S(2)}, u32[]{:S(2)}) collective-permute-start(bf16[256,128]{1,0:T(8,128)(2,1)S(1)} %get-tuple-element.60), channel_id=1, source_target_pairs={{0,15},{1,14},{2,13},{3,12},{4,11},{5,10},{6,9},{7,8},{8,7},{9,6},... | collective-permute-start | bytes 196616 | tf_op jit(solution)/shard_map/ppermute | solution.py:293
  21.1 17.9 %collective-permute-start.12 = (bf16[256,256]{1,0:T(8,128)(2,1)S(1)}, bf16[256,256]{1,0:T(8,128)(2,1)S(1)}, u32[]{:S(2)}, u32[]{:S(2)}) collective-permute-start(bf16[256,256]{1,0:T(8,128)(2,1)S(1)} %get-tuple-element.58), channel_id=1, source_target_pairs={{0,12},{1,13},{2,14},{3,15},{4,8},{5,9},{6,10},{7,11},{8,4},{9,5},... | collective-permute-start | bytes 393224 | tf_op jit(solution)/shard_map/ppermute | solution.py:293
  23.9 16.0 %collective-permute-start.4 = (bf16[256,256]{1,0:T(8,128)(2,1)S(1)}, bf16[256,256]{1,0:T(8,128)(2,1)S(1)}, u32[]{:S(2)}, u32[]{:S(2)}) collective-permute-start(bf16[256,256]{1,0:T(8,128)(2,1)S(1)} %get-tuple-element.45), channel_id=1, source_target_pairs={{0,5},{1,4},{2,7},{3,6},{4,1},{5,0},{6,3},{7,2},{8,13},{9,12},{10,... | collective-permute-start | bytes 393224 | tf_op jit(solution)/shard_map/ppermute | solution.py:293
  34.3 7.8 %collective-permute-start.5 = (bf16[256,256]{1,0:T(8,128)(2,1)S(1)}, bf16[256,256]{1,0:T(8,128)(2,1)S(1)}, u32[]{:S(2)}, u32[]{:S(2)}) collective-permute-start(bf16[256,256]{1,0:T(8,128)(2,1)S(1)} %get-tuple-element.47), channel_id=1, source_target_pairs={{0,6},{1,7},{2,4},{3,5},{4,2},{5,3},{6,0},{7,1},{8,14},{9,15},{10,... | collective-permute-start | bytes 393224 | tf_op jit(solution)/shard_map/ppermute | solution.py:293
  34.4 8.3 %collective-permute-start.10 = (bf16[256,256]{1,0:T(8,128)(2,1)S(1)}, bf16[256,256]{1,0:T(8,128)(2,1)S(1)}, u32[]{:S(2)}, u32[]{:S(2)}) collective-permute-start(bf16[256,256]{1,0:T(8,128)(2,1)S(1)} %get-tuple-element.55), channel_id=1, source_target_pairs={{0,11},{1,10},{2,9},{3,8},{4,15},{5,14},{6,13},{7,12},{8,3},{9,2},... | collective-permute-start | bytes 393224 | tf_op jit(solution)/shard_map/ppermute | solution.py:293
  36.0 9.5 %collective-permute-start.6 = (bf16[256,256]{1,0:T(8,128)(2,1)S(1)}, bf16[256,256]{1,0:T(8,128)(2,1)S(1)}, u32[]{:S(2)}, u32[]{:S(2)}) collective-permute-start(bf16[256,256]{1,0:T(8,128)(2,1)S(1)} %get-tuple-element.49), channel_id=1, source_target_pairs={{0,7},{1,6},{2,5},{3,4},{4,3},{5,2},{6,1},{7,0},{8,15},{9,14},{10,... | collective-permute-start | bytes 393224 | tf_op jit(solution)/shard_map/ppermute | solution.py:293
  39.1 11.6 %collective-permute-start.15 = (bf16[256,128]{1,0:T(8,128)(2,1)S(1)}, bf16[256,128]{1,0:T(8,128)(2,1)S(1)}, u32[]{:S(2)}, u32[]{:S(2)}) collective-permute-start(bf16[256,128]{1,0:T(8,128)(2,1)S(1)} %get-tuple-element.64), channel_id=1, source_target_pairs={{0,13},{1,12},{2,15},{3,14},{4,9},{5,8},{6,11},{7,10},{8,5},{9,4},... | collective-permute-start | bytes 196616 | tf_op jit(solution)/shard_map/ppermute | solution.py:293
  39.9 12.4 %collective-permute-start.16 = (bf16[256,128]{1,0:T(8,128)(2,1)S(1)}, bf16[256,128]{1,0:T(8,128)(2,1)S(1)}, u32[]{:S(2)}, u32[]{:S(2)}) collective-permute-start(bf16[256,128]{1,0:T(8,128)(2,1)S(1)} %get-tuple-element.66), channel_id=1, source_target_pairs={{0,14},{1,15},{2,12},{3,13},{4,10},{5,11},{6,8},{7,9},{8,6},{9,7},... | collective-permute-start | bytes 196616 | tf_op jit(solution)/shard_map/ppermute | solution.py:293
  42.0 10.6 %collective-permute-start.17 = (bf16[256,128]{1,0:T(8,128)(2,1)S(1)}, bf16[256,128]{1,0:T(8,128)(2,1)S(1)}, u32[]{:S(2)}, u32[]{:S(2)}) collective-permute-start(bf16[256,128]{1,0:T(8,128)(2,1)S(1)} %get-tuple-element.68), channel_id=1, source_target_pairs={{0,15},{1,14},{2,13},{3,12},{4,11},{5,10},{6,9},{7,8},{8,7},{9,6},... | collective-permute-start | bytes 196616 | tf_op jit(solution)/shard_map/ppermute | solution.py:293
  50.1 6.8 %collective-permute-start.18 = (f32[128,128]{1,0:T(8,128)S(1)}, f32[128,128]{1,0:T(8,128)S(1)}, u32[]{:S(2)}, u32[]{:S(2)}) collective-permute-start(f32[128,128]{1,0:T(8,128)S(1)} %get-tuple-element.61.r_lead), channel_id=1, source_target_pairs={{0,16},{16,0},{1,17},{17,1},{2,18},{18,2},{3,19},{19,3},{4,20},{20... | collective-permute-start | bytes 196616 | tf_op jit(solution)/shard_map/ppermute | solution.py:315
  56.9 5.8 %collective-permute-start.19 = (f32[128,256]{1,0:T(8,128)S(1)}, f32[128,256]{1,0:T(8,128)S(1)}, u32[]{:S(2)}, u32[]{:S(2)}) collective-permute-start(f32[128,256]{1,0:T(8,128)S(1)} %get-tuple-element.73), channel_id=1, source_target_pairs={{0,16},{16,0},{1,17},{17,1},{2,18},{18,2},{3,19},{19,3},{4,20},{20... | collective-permute-start | bytes 393224 | tf_op jit(solution)/shard_map/ppermute | solution.py:315

commit v9 on v8

--- a/solution.py
+++ b/solution.py
@@ -23,22 +23,12 @@
     return jnp.broadcast_to(x[:, c : c + 1], (SUB, LANES))
 
 
-def split_columns(wanted, src, *refs):
-    *outs, rows, arrived = refs
-    total = rows.shape[0]
-    parts = arrived.shape[0]
-    each = total // parts
-    width = rows.shape[1] // lax.axis_size("blk")
+def split_columns(wanted, src, *outs):
+    width = src.shape[2] // lax.axis_size("blk")
     me = lax.axis_index("blk")
-    cuts = [pl.ds(i * each, each) for i in range(parts)]
-    reads = [pltpu.make_async_copy(src.at[0, cut], rows.at[cut], arrived.at[i]) for i, cut in enumerate(cuts)]
-    for read in reads:
-        read.start()
-    for cut, read in zip(cuts, reads):
-        read.wait()
-        for (r, first, count), out in zip(wanted, outs):
-            at = pl.multiple_of((me ^ r) * width + first, LANES)
-            out[cut, :] = rows[cut, pl.ds(at, count)]
+    for (r, first, count), out in zip(wanted, outs):
+        at = pl.multiple_of((me ^ r) * width + first, LANES)
+        out[...] = src[0, :, pl.ds(at, count)]
 
 
 def outer(u, first, last):
@@ -262,7 +252,6 @@
     in_smem = pl.BlockSpec(memory_space=pltpu.SMEM)
     in_vmem = pl.BlockSpec(memory_space=pltpu.VMEM)
     in_hbm = pl.BlockSpec(memory_space=pltpu.MemorySpace.HBM)
-    pieces = 4
     far, near = range(parts // 2, parts), range(1, parts // 2)
     whole, late = far[:-LATE], far[-LATE:]
     h = width // 2
@@ -275,12 +264,8 @@
     blocks = pl.pallas_call(
         functools.partial(split_columns, wanted),
         out_shape=[b16((rows_here, count)) for _, _, count in wanted],
-        in_specs=[in_hbm],
+        in_specs=[in_vmem],
         out_specs=[in_vmem] * len(wanted),
-        scratch_shapes=[
-            pltpu.VMEM((rows_here, parts * width), jnp.bfloat16),
-            pltpu.SemaphoreType.DMA((pieces,)),
-        ],
         compiler_params=PARAMS,
     )(products)
     blocks = dict(zip(wanted, blocks))

time: 64.6 us -> 64.4 us (level)
  no operation moved by 1% of the time
where the time goes in v9:
time: 64.4 us; the launch traced here: 63.5 us
  starting transfers between devices  24.2 us (38%)
  waiting for transfers between devices  23.1 us (36%)
  Pallas kernels  13.3 us (21%)
  local copies, waits for them, and re-layouts  1.59 us (2%)
  between operations  1.37 us (2%)
    ppermute x18, starting transfers between devices, local(): lax.ppermute(block, 'blk', [(k, k ^ key[0]) for k in range(parts)])  23 us
    ppermute x18, waiting for transfers between devices, local(): lax.ppermute(block, 'blk', [(k, k ^ key[0]) for k in range(parts)])  21 us
    pallas_call x1, Pallas kernels, local(): pl.pallas_call(functools.partial(trailing_factor, late, rows), out_shape=...  4.25 us
    pallas_call x1, Pallas kernels, local(): pl.pallas_call(functools.partial(leading_factor, late, rows), out_shape=(...  3.42 us
    pallas_call x1, Pallas kernels, local(): pl.pallas_call(functools.partial(orthonormal_rows, rounds, rows), out_sha...  3.17 us
    ppermute x2, waiting for transfers between devices, onward(): return lax.ppermute(x, 'seg', [(i, (i + by) % sites) for i in range(sites)])  2.06 us
    unnamed x4, local copies, waits for them, and re-layouts  1.59 us
  transfers between devices with their start and end apart: 20, of which 8 were waited for; matrix products, arithmetic and copies ran while one was open for 0% of the time, Pallas kernels for 19%

profile of v9, /device:TPU:14, one launch (start us, length us, event | category | flops | bytes accessed | tf_op | source)
XLA Modules:
  0.0 63.5 jit_solution(8627518536582051961)
XLA Ops:
  0.6 0.0 copy-start
  0.6 1.6 %copy-done = bf16[1,256,4096]{2,1,0:T(8,128)(2,1)S(1)} copy-done((bf16[1,256,4096]{2,1,0:T(8,128)(2,1)S(1)}, bf16[1,256,4096]{2,1,0:T(8,128)(2,1)}, u32[]{:S(2)}) %copy-start) | copy-done | bytes 2097176
  2.2 0.3 shard_map.50
  2.6 0.1 collective-permute-start
  2.6 2.7 %collective-permute-start.7 = (bf16[256,256]{1,0:T(8,128)(2,1)S(1)}, bf16[256,256]{1,0:T(8,128)(2,1)S(1)}, u32[]{:S(2)}, u32[]{:S(2)}) collective-permute-start(bf16[256,256]{1,0:T(8,128)(2,1)S(1)} %get-tuple-element.50), channel_id=1, source_target_pairs={{0,8},{1,9},{2,10},{3,11},{4,12},{5,13},{6,14},{7,15},{8,0},{9,1},... | collective-permute-start | bytes 393224 | tf_op jit(solution)/shard_map/ppermute | solution.py:278
  5.3 0.5 collective-permute-start.1
  5.8 1.0 %collective-permute-start.2 = (bf16[256,256]{1,0:T(8,128)(2,1)S(1)}, bf16[256,256]{1,0:T(8,128)(2,1)S(1)}, u32[]{:S(2)}, u32[]{:S(2)}) collective-permute-start(bf16[256,256]{1,0:T(8,128)(2,1)S(1)} %get-tuple-element.41), channel_id=1, source_target_pairs={{0,3},{1,2},{2,1},{3,0},{4,7},{5,6},{6,5},{7,4},{8,11},{9,10},{10,... | collective-permute-start | bytes 393224 | tf_op jit(solution)/shard_map/ppermute | solution.py:278
  6.8 0.0 collective-permute-start.11
  6.8 0.0 collective-permute-done.refs_1_
  6.8 2.5 %collective-permute-start.8 = (bf16[256,256]{1,0:T(8,128)(2,1)S(1)}, bf16[256,256]{1,0:T(8,128)(2,1)S(1)}, u32[]{:S(2)}, u32[]{:S(2)}) collective-permute-start(bf16[256,256]{1,0:T(8,128)(2,1)S(1)} %get-tuple-element.51), channel_id=1, source_target_pairs={{0,9},{1,8},{2,11},{3,10},{4,13},{5,12},{6,15},{7,14},{8,1},{9,0},... | collective-permute-start | bytes 393224 | tf_op jit(solution)/shard_map/ppermute | solution.py:278
  9.3 6.3 %collective-permute-done.7.refs_8_ = bf16[256,256]{1,0:T(8,128)(2,1)S(1)} collective-permute-done((bf16[256,256]{1,0:T(8,128)(2,1)S(1)}, bf16[256,256]{1,0:T(8,128)(2,1)S(1)}, u32[]{:S(2)}, u32[]{:S(2)}) %collective-permute-start.7) | collective-permute-done | bytes 131104 | tf_op jit(solution)/shard_map/ppermute | solution.py:278
  15.6 1.8 %collective-permute-start.3 = (bf16[256,256]{1,0:T(8,128)(2,1)S(1)}, bf16[256,256]{1,0:T(8,128)(2,1)S(1)}, u32[]{:S(2)}, u32[]{:S(2)}) collective-permute-start(bf16[256,256]{1,0:T(8,128)(2,1)S(1)} %get-tuple-element.43), channel_id=1, source_target_pairs={{0,4},{1,5},{2,6},{3,7},{4,0},{5,1},{6,2},{7,3},{8,12},{9,13},{10,... | collective-permute-start | bytes 393224 | tf_op jit(solution)/shard_map/ppermute | solution.py:278
  17.4 0.0 collective-permute-done.11.refs_0_.refs_13_
  17.4 1.6 %collective-permute-start.9 = (bf16[256,256]{1,0:T(8,128)(2,1)S(1)}, bf16[256,256]{1,0:T(8,128)(2,1)S(1)}, u32[]{:S(2)}, u32[]{:S(2)}) collective-permute-start(bf16[256,256]{1,0:T(8,128)(2,1)S(1)} %get-tuple-element.53), channel_id=1, source_target_pairs={{0,10},{1,11},{2,8},{3,9},{4,14},{5,15},{6,12},{7,13},{8,2},{9,3},... | collective-permute-start | bytes 393224 | tf_op jit(solution)/shard_map/ppermute | solution.py:278
  18.9 0.0 collective-permute-done.1.refs_2_
  18.9 1.1 %collective-permute-start.13 = (bf16[256,128]{1,0:T(8,128)(2,1)S(1)}, bf16[256,128]{1,0:T(8,128)(2,1)S(1)}, u32[]{:S(2)}, u32[]{:S(2)}) collective-permute-start(bf16[256,128]{1,0:T(8,128)(2,1)S(1)} %get-tuple-element.59), channel_id=1, source_target_pairs={{0,14},{1,15},{2,12},{3,13},{4,10},{5,11},{6,8},{7,9},{8,6},{9,7},... | collective-permute-start | bytes 196616 | tf_op jit(solution)/shard_map/ppermute | solution.py:278
  20.0 0.0 collective-permute-done.2.refs_3_
  20.0 0.9 %collective-permute-start.14 = (bf16[256,128]{1,0:T(8,128)(2,1)S(1)}, bf16[256,128]{1,0:T(8,128)(2,1)S(1)}, u32[]{:S(2)}, u32[]{:S(2)}) collective-permute-start(bf16[256,128]{1,0:T(8,128)(2,1)S(1)} %get-tuple-element.60), channel_id=1, source_target_pairs={{0,15},{1,14},{2,13},{3,12},{4,11},{5,10},{6,9},{7,8},{8,7},{9,6},... | collective-permute-start | bytes 196616 | tf_op jit(solution)/shard_map/ppermute | solution.py:278
  20.9 0.0 collective-permute-done.8.refs_9_
  20.9 1.1 %collective-permute-start.12 = (bf16[256,256]{1,0:T(8,128)(2,1)S(1)}, bf16[256,256]{1,0:T(8,128)(2,1)S(1)}, u32[]{:S(2)}, u32[]{:S(2)}) collective-permute-start(bf16[256,256]{1,0:T(8,128)(2,1)S(1)} %get-tuple-element.58), channel_id=1, source_target_pairs={{0,12},{1,13},{2,14},{3,15},{4,8},{5,9},{6,10},{7,11},{8,4},{9,5},... | collective-permute-start | bytes 393224 | tf_op jit(solution)/shard_map/ppermute | solution.py:278
  22.0 1.7 %collective-permute-done.3.refs_4_ = bf16[256,256]{1,0:T(8,128)(2,1)S(1)} collective-permute-done((bf16[256,256]{1,0:T(8,128)(2,1)S(1)}, bf16[256,256]{1,0:T(8,128)(2,1)S(1)}, u32[]{:S(2)}, u32[]{:S(2)}) %collective-permute-start.3) | collective-permute-done | bytes 131104 | tf_op jit(solution)/shard_map/ppermute | solution.py:278
  23.7 2.2 %collective-permute-start.4 = (bf16[256,256]{1,0:T(8,128)(2,1)S(1)}, bf16[256,256]{1,0:T(8,128)(2,1)S(1)}, u32[]{:S(2)}, u32[]{:S(2)}) collective-permute-start(bf16[256,256]{1,0:T(8,128)(2,1)S(1)} %get-tuple-element.45), channel_id=1, source_target_pairs={{0,5},{1,4},{2,7},{3,6},{4,1},{5,0},{6,3},{7,2},{8,13},{9,12},{10,... | collective-permute-start | bytes 393224 | tf_op jit(solution)/shard_map/ppermute | solution.py:278
  25.9 8.2 %collective-permute-done.13.refs_1_.refs_15_ = bf16[256,128]{1,0:T(8,128)(2,1)S(1)} collective-permute-done((bf16[256,128]{1,0:T(8,128)(2,1)S(1)}, bf16[256,128]{1,0:T(8,128)(2,1)S(1)}, u32[]{:S(2)}, u32[]{:S(2)}) %collective-permute-start.13) | collective-permute-done | bytes 65568 | tf_op jit(solution)/shard_map/ppermute | solution.py:278
  34.1 0.0 collective-permute-start.5
  34.1 0.1 collective-permute-done.14.refs_2_.refs_17_
  34.2 1.6 %collective-permute-start.10 = (bf16[256,256]{1,0:T(8,128)(2,1)S(1)}, bf16[256,256]{1,0:T(8,128)(2,1)S(1)}, u32[]{:S(2)}, u32[]{:S(2)}) collective-permute-start(bf16[256,256]{1,0:T(8,128)(2,1)S(1)} %get-tuple-element.55), channel_id=1, source_target_pairs={{0,11},{1,10},{2,9},{3,8},{4,15},{5,14},{6,13},{7,12},{8,3},{9,2},... | collective-permute-start | bytes 393224 | tf_op jit(solution)/shard_map/ppermute | solution.py:278
  35.8 0.0 collective-permute-done.9.refs_10_
  35.8 2.5 %collective-permute-start.6 = (bf16[256,256]{1,0:T(8,128)(2,1)S(1)}, bf16[256,256]{1,0:T(8,128)(2,1)S(1)}, u32[]{:S(2)}, u32[]{:S(2)}) collective-permute-start(bf16[256,256]{1,0:T(8,128)(2,1)S(1)} %get-tuple-element.49), channel_id=1, source_target_pairs={{0,7},{1,6},{2,5},{3,4},{4,3},{5,2},{6,1},{7,0},{8,15},{9,14},{10,... | collective-permute-start | bytes 393224 | tf_op jit(solution)/shard_map/ppermute | solution.py:278
  38.9 0.0 collective-permute-done.12.refs_12_
  38.9 0.9 %collective-permute-start.15 = (bf16[256,128]{1,0:T(8,128)(2,1)S(1)}, bf16[256,128]{1,0:T(8,128)(2,1)S(1)}, u32[]{:S(2)}, u32[]{:S(2)}) collective-permute-start(bf16[256,128]{1,0:T(8,128)(2,1)S(1)} %get-tuple-element.64), channel_id=1, source_target_pairs={{0,13},{1,12},{2,15},{3,14},{4,9},{5,8},{6,11},{7,10},{8,5},{9,4},... | collective-permute-start | bytes 196616 | tf_op jit(solution)/shard_map/ppermute | solution.py:278
  39.7 0.0 collective-permute-done.4.refs_5_
  39.7 2.1 %collective-permute-start.16 = (bf16[256,128]{1,0:T(8,128)(2,1)S(1)}, bf16[256,128]{1,0:T(8,128)(2,1)S(1)}, u32[]{:S(2)}, u32[]{:S(2)}) collective-permute-start(bf16[256,128]{1,0:T(8,128)(2,1)S(1)} %get-tuple-element.66), channel_id=1, source_target_pairs={{0,14},{1,15},{2,12},{3,13},{4,10},{5,11},{6,8},{7,9},{8,6},{9,7},... | collective-permute-start | bytes 196616 | tf_op jit(solution)/shard_map/ppermute | solution.py:278
  41.8 0.0 collective-permute-done.5.refs_6_
  41.8 0.7 %collective-permute-start.17 = (bf16[256,128]{1,0:T(8,128)(2,1)S(1)}, bf16[256,128]{1,0:T(8,128)(2,1)S(1)}, u32[]{:S(2)}, u32[]{:S(2)}) collective-permute-start(bf16[256,128]{1,0:T(8,128)(2,1)S(1)} %get-tuple-element.68), channel_id=1, source_target_pairs={{0,15},{1,14},{2,13},{3,12},{4,11},{5,10},{6,9},{7,8},{8,7},{9,6},... | collective-permute-start | bytes 196616 | tf_op jit(solution)/shard_map/ppermute | solution.py:278
  42.5 0.0 collective-permute-done.10.refs_11_
  42.5 2.8 %collective-permute-done.6.refs_7_ = bf16[256,256]{1,0:T(8,128)(2,1)S(1)} collective-permute-done((bf16[256,256]{1,0:T(8,128)(2,1)S(1)}, bf16[256,256]{1,0:T(8,128)(2,1)S(1)}, u32[]{:S(2)}, u32[]{:S(2)}) %collective-permute-start.6) | collective-permute-done | bytes 131104 | tf_op jit(solution)/shard_map/ppermute | solution.py:278
  45.3 1.2 %shard_map.51.gram = f32[256,256]{1,0:T(8,128)S(1)} custom-call(s32[1,16]{1,0:T(1,128)S(1)} %bitcast.2, bf16[256,256]{1,0:T(8,128)(2,1)S(1)} %get-tuple-element.38.refs_0_, bf16[256,256]{1,0:T(8,128)(2,1)S(1)} %collective-permute-done.refs_1_, bf16[256,256]{1,0:T(8,128)(2,1)S(1)} %collective-permute-done.1.refs_2_, ...), custom_call_target="tpu_custom_call" | custom-call | flops 536870912 | bytes 2097152 | tf_op jit(solution)/shard_map/pallas_call | solution.py:280
  46.5 3.4 %shard_map.52 = (f32[128,128]{1,0:T(8,128)S(1)}, f32[128,128]{1,0:T(8,128)S(1)}) custom-call(s32[1,16]{1,0:T(1,128)S(1)} %bitcast.3, s32[1,1]{1,0:T(1,128)S(6)} %copy.5.size, f32[256,256]{1,0:T(8,128)S(1)} %shard_map.51.gram, bf16[256,128]{1,0:T(8,128)(2,1)S(1)} %collective-permute-done.11.refs_0_.refs_13_, ...), custom_call_target="tpu_custom_call" | custom-call | tf_op jit(solution)/shard_map/pallas_call | solution.py:289
  49.9 0.6 collective-permute-start.18
  50.5 0.0 collective-permute-done.15.refs_3_.refs_14_
  50.5 1.6 %collective-permute-done.16.refs_4_.refs_16_ = bf16[256,128]{1,0:T(8,128)(2,1)S(1)} collective-permute-done((bf16[256,128]{1,0:T(8,128)(2,1)S(1)}, bf16[256,128]{1,0:T(8,128)(2,1)S(1)}, u32[]{:S(2)}, u32[]{:S(2)}) %collective-permute-start.16) | collective-permute-done | bytes 65568 | tf_op jit(solution)/shard_map/ppermute | solution.py:278
  52.2 0.3 collective-permute-done.17.refs_5_.refs_18_
  52.5 4.2 %shard_map.53 = (f32[256,256]{1,0:T(8,128)S(1)}, f32[128,256]{1,0:T(8,128)S(1)}, f32[128,128]{1,0:T(8,128)S(1)}) custom-call(s32[1,16]{1,0:T(1,128)S(1)} %bitcast.4, s32[1,1]{1,0:T(1,128)S(6)} %copy.5.size, f32[256,256]{1,0:T(8,128)S(1)} %shard_map.51.gram, f32[128,128]{1,0:T(8,128)S(1)} %get-tuple-element.61.r_lead, ...), custom_call_target="tpu_custom_call" | custom-call | tf_op jit(solution)/shard_map/pallas_call | solution.py:303
  56.7 0.0 collective-permute-done.18.lead
  56.7 0.6 collective-permute-start.19
  57.3 3.2 %shard_map.54 = bf16[1,4096,256]{2,1,0:T(8,128)(2,1)} custom-call(s32[1,16]{1,0:T(1,128)S(1)} %bitcast.5, s32[1,1]{1,0:T(1,128)S(6)} %copy.5.size, f32[256,256]{1,0:T(8,128)S(1)} %get-tuple-element.69.factor.own, f32[128,128]{1,0:T(8,128)S(1)} %get-tuple-element.62.inverse_lead.lead, f32[128,128]{1,0:T(8,128)S(1)} %get-tuple-element.70.trail, ...), custom_call_target="tpu_custom_call" | custom-call | flops 1073741824 | bytes 4194304 | tf_op jit(solution)/shard_map/pallas_call | solution.py:313
  60.5 2.1 %collective-permute-done.19.rest = f32[128,256]{1,0:T(8,128)S(1)} collective-permute-done((f32[128,256]{1,0:T(8,128)S(1)}, f32[128,256]{1,0:T(8,128)S(1)}, u32[]{:S(2)}, u32[]{:S(2)}) %collective-permute-start.19) | collective-permute-done | bytes 131104 | tf_op jit(solution)/shard_map/ppermute | solution.py:300
  62.6 0.9 %shard_map.55 = f32[256,256]{1,0:T(8,128)} custom-call(f32[256,256]{1,0:T(8,128)S(1)} %get-tuple-element.69.factor.own, f32[128,128]{1,0:T(8,128)S(1)} %collective-permute-done.18.lead, f32[128,256]{1,0:T(8,128)S(1)} %collective-permute-done.19.rest), custom_call_target="tpu_custom_call" | custom-call | tf_op jit(solution)/shard_map/pallas_call | solution.py:332
  (2 shorter events, 0.0 us)
Async XLA Ops:
  0.6 1.6 %copy-start = (bf16[1,256,4096]{2,1,0:T(8,128)(2,1)S(1)}, bf16[1,256,4096]{2,1,0:T(8,128)(2,1)}, u32[]{:S(2)}) copy-start(bf16[1,256,4096]{2,1,0:T(8,128)(2,1)} %src.1) | copy-start | bytes 6291460
  2.2 43.1 %copy-start.1 = (s32[1,1,16]{2,1,0:T(1,128)S(1)}, s32[1,1,16]{2,1,0:T(1,128)}, u32[]{:S(2)}) copy-start(s32[1,1,16]{2,1,0:T(1,128)} %param.4) | copy-start | bytes 196
  2.6 4.3 %collective-permute-start = (bf16[256,256]{1,0:T(8,128)(2,1)S(1)}, bf16[256,256]{1,0:T(8,128)(2,1)S(1)}, u32[]{:S(2)}, u32[]{:S(2)}) collective-permute-start(bf16[256,256]{1,0:T(8,128)(2,1)S(1)} %get-tuple-element.39), channel_id=1, source_target_pairs={{0,1},{1,0},{2,3},{3,2},{4,5},{5,4},{6,7},{7,6},{8,9},{9,8},{10,11... | collective-permute-start | bytes 393224 | tf_op jit(solution)/shard_map/ppermute | solution.py:278
  2.6 13.0 %collective-permute-start.7 = (bf16[256,256]{1,0:T(8,128)(2,1)S(1)}, bf16[256,256]{1,0:T(8,128)(2,1)S(1)}, u32[]{:S(2)}, u32[]{:S(2)}) collective-permute-start(bf16[256,256]{1,0:T(8,128)(2,1)S(1)} %get-tuple-element.50), channel_id=1, source_target_pairs={{0,8},{1,9},{2,10},{3,11},{4,12},{5,13},{6,14},{7,15},{8,0},{9,1},... | collective-permute-start | bytes 393224 | tf_op jit(solution)/shard_map/ppermute | solution.py:278
  5.3 13.7 %collective-permute-start.1 = (bf16[256,256]{1,0:T(8,128)(2,1)S(1)}, bf16[256,256]{1,0:T(8,128)(2,1)S(1)}, u32[]{:S(2)}, u32[]{:S(2)}) collective-permute-start(bf16[256,256]{1,0:T(8,128)(2,1)S(1)} %get-tuple-element.40), channel_id=1, source_target_pairs={{0,2},{1,3},{2,0},{3,1},{4,6},{5,7},{6,4},{7,5},{8,10},{9,11},{10,... | collective-permute-start | bytes 393224 | tf_op jit(solution)/shard_map/ppermute | solution.py:278
  5.8 14.2 %collective-permute-start.2 = (bf16[256,256]{1,0:T(8,128)(2,1)S(1)}, bf16[256,256]{1,0:T(8,128)(2,1)S(1)}, u32[]{:S(2)}, u32[]{:S(2)}) collective-permute-start(bf16[256,256]{1,0:T(8,128)(2,1)S(1)} %get-tuple-element.41), channel_id=1, source_target_pairs={{0,3},{1,2},{2,1},{3,0},{4,7},{5,6},{6,5},{7,4},{8,11},{9,10},{10,... | collective-permute-start | bytes 393224 | tf_op jit(solution)/shard_map/ppermute | solution.py:278
  6.8 10.6 %collective-permute-start.11 = (bf16[256,128]{1,0:T(8,128)(2,1)S(1)}, bf16[256,128]{1,0:T(8,128)(2,1)S(1)}, u32[]{:S(2)}, u32[]{:S(2)}) collective-permute-start(bf16[256,128]{1,0:T(8,128)(2,1)S(1)} %get-tuple-element.57), channel_id=1, source_target_pairs={{0,13},{1,12},{2,15},{3,14},{4,9},{5,8},{6,11},{7,10},{8,5},{9,4},... | collective-permute-start | bytes 196616 | tf_op jit(solution)/shard_map/ppermute | solution.py:278
  6.8 14.1 %collective-permute-start.8 = (bf16[256,256]{1,0:T(8,128)(2,1)S(1)}, bf16[256,256]{1,0:T(8,128)(2,1)S(1)}, u32[]{:S(2)}, u32[]{:S(2)}) collective-permute-start(bf16[256,256]{1,0:T(8,128)(2,1)S(1)} %get-tuple-element.51), channel_id=1, source_target_pairs={{0,9},{1,8},{2,11},{3,10},{4,13},{5,12},{6,15},{7,14},{8,1},{9,0},... | collective-permute-start | bytes 393224 | tf_op jit(solution)/shard_map/ppermute | solution.py:278
  15.6 8.1 %collective-permute-start.3 = (bf16[256,256]{1,0:T(8,128)(2,1)S(1)}, bf16[256,256]{1,0:T(8,128)(2,1)S(1)}, u32[]{:S(2)}, u32[]{:S(2)}) collective-permute-start(bf16[256,256]{1,0:T(8,128)(2,1)S(1)} %get-tuple-element.43), channel_id=1, source_target_pairs={{0,4},{1,5},{2,6},{3,7},{4,0},{5,1},{6,2},{7,3},{8,12},{9,13},{10,... | collective-permute-start | bytes 393224 | tf_op jit(solution)/shard_map/ppermute | solution.py:278
  17.4 18.4 %collective-permute-start.9 = (bf16[256,256]{1,0:T(8,128)(2,1)S(1)}, bf16[256,256]{1,0:T(8,128)(2,1)S(1)}, u32[]{:S(2)}, u32[]{:S(2)}) collective-permute-start(bf16[256,256]{1,0:T(8,128)(2,1)S(1)} %get-tuple-element.53), channel_id=1, source_target_pairs={{0,10},{1,11},{2,8},{3,9},{4,14},{5,15},{6,12},{7,13},{8,2},{9,3},... | collective-permute-start | bytes 393224 | tf_op jit(solution)/shard_map/ppermute | solution.py:278
  18.9 15.1 %collective-permute-start.13 = (bf16[256,128]{1,0:T(8,128)(2,1)S(1)}, bf16[256,128]{1,0:T(8,128)(2,1)S(1)}, u32[]{:S(2)}, u32[]{:S(2)}) collective-permute-start(bf16[256,128]{1,0:T(8,128)(2,1)S(1)} %get-tuple-element.59), channel_id=1, source_target_pairs={{0,14},{1,15},{2,12},{3,13},{4,10},{5,11},{6,8},{7,9},{8,6},{9,7},... | collective-permute-start | bytes 196616 | tf_op jit(solution)/shard_map/ppermute | solution.py:278
  20.0 14.2 %collective-permute-start.14 = (bf16[256,128]{1,0:T(8,128)(2,1)S(1)}, bf16[256,128]{1,0:T(8,128)(2,1)S(1)}, u32[]{:S(2)}, u32[]{:S(2)}) collective-permute-start(bf16[256,128]{1,0:T(8,128)(2,1)S(1)} %get-tuple-element.60), channel_id=1, source_target_pairs={{0,15},{1,14},{2,13},{3,12},{4,11},{5,10},{6,9},{7,8},{8,7},{9,6},... | collective-permute-start | bytes 196616 | tf_op jit(solution)/shard_map/ppermute | solution.py:278
  20.9 17.9 %collective-permute-start.12 = (bf16[256,256]{1,0:T(8,128)(2,1)S(1)}, bf16[256,256]{1,0:T(8,128)(2,1)S(1)}, u32[]{:S(2)}, u32[]{:S(2)}) collective-permute-start(bf16[256,256]{1,0:T(8,128)(2,1)S(1)} %get-tuple-element.58), channel_id=1, source_target_pairs={{0,12},{1,13},{2,14},{3,15},{4,8},{5,9},{6,10},{7,11},{8,4},{9,5},... | collective-permute-start | bytes 393224 | tf_op jit(solution)/shard_map/ppermute | solution.py:278
  23.7 16.0 %collective-permute-start.4 = (bf16[256,256]{1,0:T(8,128)(2,1)S(1)}, bf16[256,256]{1,0:T(8,128)(2,1)S(1)}, u32[]{:S(2)}, u32[]{:S(2)}) collective-permute-start(bf16[256,256]{1,0:T(8,128)(2,1)S(1)} %get-tuple-element.45), channel_id=1, source_target_pairs={{0,5},{1,4},{2,7},{3,6},{4,1},{5,0},{6,3},{7,2},{8,13},{9,12},{10,... | collective-permute-start | bytes 393224 | tf_op jit(solution)/shard_map/ppermute | solution.py:278
  34.1 7.8 %collective-permute-start.5 = (bf16[256,256]{1,0:T(8,128)(2,1)S(1)}, bf16[256,256]{1,0:T(8,128)(2,1)S(1)}, u32[]{:S(2)}, u32[]{:S(2)}) collective-permute-start(bf16[256,256]{1,0:T(8,128)(2,1)S(1)} %get-tuple-element.47), channel_id=1, source_target_pairs={{0,6},{1,7},{2,4},{3,5},{4,2},{5,3},{6,0},{7,1},{8,14},{9,15},{10,... | collective-permute-start | bytes 393224 | tf_op jit(solution)/shard_map/ppermute | solution.py:278
  34.2 8.3 %collective-permute-start.10 = (bf16[256,256]{1,0:T(8,128)(2,1)S(1)}, bf16[256,256]{1,0:T(8,128)(2,1)S(1)}, u32[]{:S(2)}, u32[]{:S(2)}) collective-permute-start(bf16[256,256]{1,0:T(8,128)(2,1)S(1)} %get-tuple-element.55), channel_id=1, source_target_pairs={{0,11},{1,10},{2,9},{3,8},{4,15},{5,14},{6,13},{7,12},{8,3},{9,2},... | collective-permute-start | bytes 393224 | tf_op jit(solution)/shard_map/ppermute | solution.py:278
  35.8 9.5 %collective-permute-start.6 = (bf16[256,256]{1,0:T(8,128)(2,1)S(1)}, bf16[256,256]{1,0:T(8,128)(2,1)S(1)}, u32[]{:S(2)}, u32[]{:S(2)}) collective-permute-start(bf16[256,256]{1,0:T(8,128)(2,1)S(1)} %get-tuple-element.49), channel_id=1, source_target_pairs={{0,7},{1,6},{2,5},{3,4},{4,3},{5,2},{6,1},{7,0},{8,15},{9,14},{10,... | collective-permute-start | bytes 393224 | tf_op jit(solution)/shard_map/ppermute | solution.py:278
  38.9 11.6 %collective-permute-start.15 = (bf16[256,128]{1,0:T(8,128)(2,1)S(1)}, bf16[256,128]{1,0:T(8,128)(2,1)S(1)}, u32[]{:S(2)}, u32[]{:S(2)}) collective-permute-start(bf16[256,128]{1,0:T(8,128)(2,1)S(1)} %get-tuple-element.64), channel_id=1, source_target_pairs={{0,13},{1,12},{2,15},{3,14},{4,9},{5,8},{6,11},{7,10},{8,5},{9,4},... | collective-permute-start | bytes 196616 | tf_op jit(solution)/shard_map/ppermute | solution.py:278
  39.7 12.4 %collective-permute-start.16 = (bf16[256,128]{1,0:T(8,128)(2,1)S(1)}, bf16[256,128]{1,0:T(8,128)(2,1)S(1)}, u32[]{:S(2)}, u32[]{:S(2)}) collective-permute-start(bf16[256,128]{1,0:T(8,128)(2,1)S(1)} %get-tuple-element.66), channel_id=1, source_target_pairs={{0,14},{1,15},{2,12},{3,13},{4,10},{5,11},{6,8},{7,9},{8,6},{9,7},... | collective-permute-start | bytes 196616 | tf_op jit(solution)/shard_map/ppermute | solution.py:278
  41.8 10.6 %collective-permute-start.17 = (bf16[256,128]{1,0:T(8,128)(2,1)S(1)}, bf16[256,128]{1,0:T(8,128)(2,1)S(1)}, u32[]{:S(2)}, u32[]{:S(2)}) collective-permute-start(bf16[256,128]{1,0:T(8,128)(2,1)S(1)} %get-tuple-element.68), channel_id=1, source_target_pairs={{0,15},{1,14},{2,13},{3,12},{4,11},{5,10},{6,9},{7,8},{8,7},{9,6},... | collective-permute-start | bytes 196616 | tf_op jit(solution)/shard_map/ppermute | solution.py:278
  49.9 6.8 %collective-permute-start.18 = (f32[128,128]{1,0:T(8,128)S(1)}, f32[128,128]{1,0:T(8,128)S(1)}, u32[]{:S(2)}, u32[]{:S(2)}) collective-permute-start(f32[128,128]{1,0:T(8,128)S(1)} %get-tuple-element.61.r_lead), channel_id=1, source_target_pairs={{0,16},{16,0},{1,17},{17,1},{2,18},{18,2},{3,19},{19,3},{4,20},{20... | collective-permute-start | bytes 196616 | tf_op jit(solution)/shard_map/ppermute | solution.py:300
  56.7 5.8 %collective-permute-start.19 = (f32[128,256]{1,0:T(8,128)S(1)}, f32[128,256]{1,0:T(8,128)S(1)}, u32[]{:S(2)}, u32[]{:S(2)}) collective-permute-start(f32[128,256]{1,0:T(8,128)S(1)} %get-tuple-element.73), channel_id=1, source_target_pairs={{0,16},{16,0},{1,17},{17,1},{2,18},{18,2},{3,19},{19,3},{4,20},{20... | collective-permute-start | bytes 393224 | tf_op jit(solution)/shard_map/ppermute | solution.py:300

commit v10 on v9

--- a/solution.py
+++ b/solution.py
@@ -144,10 +144,11 @@
 
 
 def leading_factor(rounds, rows, compat, size, gram, *refs):
-    *blocks, r_out, inverse_out, w = refs
+    *blocks, r_out, lower_out, inverse_out, w = refs
     h = r_out.shape[0]
     g = gram[:h, :h] + gram_of(rounds, rows, compat, blocks)
     factor_block(shifted(g, size, 0, 0), r_out, inverse_out, w)
+    lower_out[...] = r_out[...].T
 
 
 def thrice(x, y):
@@ -158,7 +159,7 @@
     return jnp.dot(left, jnp.concatenate([y_high, y_low, y_high], axis=0), preferred_element_type=jnp.float32)
 
 
-def trailing_factor(rounds, rows, compat, size, gram, r_lead, inverse_lead, *refs):
+def trailing_factor(rounds, rows, compat, size, gram, r_lead, lower, inverse_lead, *refs):
     *blocks, r_out, rest_out, inverse_out, w = refs
     first, second = blocks[: len(rounds)], blocks[len(rounds) :]
     h = r_lead.shape[0]
@@ -172,7 +173,7 @@
         precision=HIGHEST,
         preferred_element_type=jnp.float32,
     )
-    right = right + dot(inverse_lead[...], cross - down_t(r_lead[...], right))
+    right = right + dot(inverse_lead[...], cross - dot(lower[...], right, precision=HIGHEST))
     factor_block(own - down_t(right, right), rest_out.at[:, h:], inverse_out, w)
     rest_out[:, :h] = right
     r_out[:h, :h] = r_lead[...]
@@ -286,11 +287,11 @@
         compiler_params=PARAMS,
     )(compat[0], *[got[r, 0, width] for r in early])
     firsts, seconds = [got[key] for key in first], [got[key] for key in second]
-    lead_r, lead = pl.pallas_call(
+    lead_r, lower, lead = pl.pallas_call(
         functools.partial(leading_factor, late, rows),
-        out_shape=(f32((h, h)), f32((h, h))),
+        out_shape=[f32((h, h))] * 3,
         in_specs=[in_smem, in_smem] + [in_vmem] * (1 + LATE),
-        out_specs=[in_vmem] * 2,
+        out_specs=[in_vmem] * 3,
         scratch_shapes=[pltpu.VMEM((h, 2 * h), jnp.float32)],
         compiler_params=PARAMS,
     )(compat[0], sizes, gram, *firsts)
@@ -303,11 +304,11 @@
     factor, rest, trail = pl.pallas_call(
         functools.partial(trailing_factor, late, rows),
         out_shape=(f32((width, width)), f32((h, width)), f32((h, h))),
-        in_specs=[in_smem, in_smem] + [in_vmem] * (3 + 2 * LATE),
+        in_specs=[in_smem, in_smem] + [in_vmem] * (4 + 2 * LATE),
         out_specs=[in_vmem] * 3,
         scratch_shapes=[pltpu.VMEM((h, 2 * h), jnp.float32)],
         compiler_params=PARAMS,
-    )(compat[0], sizes, gram, lead_r, lead, *firsts, *seconds)
+    )(compat[0], sizes, gram, lead_r, lower, lead, *firsts, *seconds)
     rounds = [(r, 1) for r in early] + [(r, 2) for r in late]
     views = [got[r, 0, width] for r in early] + [x for pair in zip(firsts, seconds) for x in pair]
     ortho = pl.pallas_call(

time: 64.4 us -> 64.5 us (level)
  no operation moved by 1% of the time
where the time goes in v10:
time: 64.5 us; the launch traced here: 63.5 us
  starting transfers between devices  24.2 us (38%)
  waiting for transfers between devices  23 us (36%)
  Pallas kernels  13.4 us (21%)
  local copies, waits for them, and re-layouts  1.59 us (2%)
  between operations  1.37 us (2%)
    ppermute x18, starting transfers between devices, local(): lax.ppermute(block, 'blk', [(k, k ^ key[0]) for k in range(parts)])  23 us
    ppermute x18, waiting for transfers between devices, local(): lax.ppermute(block, 'blk', [(k, k ^ key[0]) for k in range(parts)])  20.9 us
    pallas_call x1, Pallas kernels, local(): pl.pallas_call(functools.partial(trailing_factor, late, rows), out_shape=...  4.23 us
    pallas_call x1, Pallas kernels, local(): pl.pallas_call(functools.partial(leading_factor, late, rows), out_shape=[...  3.5 us
    pallas_call x1, Pallas kernels, local(): pl.pallas_call(functools.partial(orthonormal_rows, rounds, rows), out_sha...  3.17 us
    ppermute x2, waiting for transfers between devices, onward(): return lax.ppermute(x, 'seg', [(i, (i + by) % sites) for i in range(sites)])  2.06 us
    unnamed x4, local copies, waits for them, and re-layouts  1.59 us
  transfers between devices with their start and end apart: 20, of which 8 were waited for; matrix products, arithmetic and copies ran while one was open for 0% of the time, Pallas kernels for 19%

profile of v10, /device:TPU:14, one launch (start us, length us, event | category | flops | bytes accessed | tf_op | source)
XLA Modules:
  0.0 63.5 jit_solution(10495205945996778951)
XLA Ops:
  0.6 0.0 copy-start
  0.6 1.6 %copy-done = bf16[1,256,4096]{2,1,0:T(8,128)(2,1)S(1)} copy-done((bf16[1,256,4096]{2,1,0:T(8,128)(2,1)S(1)}, bf16[1,256,4096]{2,1,0:T(8,128)(2,1)}, u32[]{:S(2)}) %copy-start) | copy-done | bytes 2097176
  2.2 0.3 shard_map.50
  2.6 0.1 collective-permute-start
  2.6 2.7 %collective-permute-start.7 = (bf16[256,256]{1,0:T(8,128)(2,1)S(1)}, bf16[256,256]{1,0:T(8,128)(2,1)S(1)}, u32[]{:S(2)}, u32[]{:S(2)}) collective-permute-start(bf16[256,256]{1,0:T(8,128)(2,1)S(1)} %get-tuple-element.51), channel_id=1, source_target_pairs={{0,8},{1,9},{2,10},{3,11},{4,12},{5,13},{6,14},{7,15},{8,0},{9,1},... | collective-permute-start | bytes 393224 | tf_op jit(solution)/shard_map/ppermute | solution.py:279
  5.3 0.5 collective-permute-start.1
  5.8 1.0 %collective-permute-start.2 = (bf16[256,256]{1,0:T(8,128)(2,1)S(1)}, bf16[256,256]{1,0:T(8,128)(2,1)S(1)}, u32[]{:S(2)}, u32[]{:S(2)}) collective-permute-start(bf16[256,256]{1,0:T(8,128)(2,1)S(1)} %get-tuple-element.42), channel_id=1, source_target_pairs={{0,3},{1,2},{2,1},{3,0},{4,7},{5,6},{6,5},{7,4},{8,11},{9,10},{10,... | collective-permute-start | bytes 393224 | tf_op jit(solution)/shard_map/ppermute | solution.py:279
  6.8 0.0 collective-permute-start.11
  6.8 0.0 collective-permute-done.refs_1_
  6.8 2.5 %collective-permute-start.8 = (bf16[256,256]{1,0:T(8,128)(2,1)S(1)}, bf16[256,256]{1,0:T(8,128)(2,1)S(1)}, u32[]{:S(2)}, u32[]{:S(2)}) collective-permute-start(bf16[256,256]{1,0:T(8,128)(2,1)S(1)} %get-tuple-element.52), channel_id=1, source_target_pairs={{0,9},{1,8},{2,11},{3,10},{4,13},{5,12},{6,15},{7,14},{8,1},{9,0},... | collective-permute-start | bytes 393224 | tf_op jit(solution)/shard_map/ppermute | solution.py:279
  9.3 6.3 %collective-permute-done.7.refs_8_ = bf16[256,256]{1,0:T(8,128)(2,1)S(1)} collective-permute-done((bf16[256,256]{1,0:T(8,128)(2,1)S(1)}, bf16[256,256]{1,0:T(8,128)(2,1)S(1)}, u32[]{:S(2)}, u32[]{:S(2)}) %collective-permute-start.7) | collective-permute-done | bytes 131104 | tf_op jit(solution)/shard_map/ppermute | solution.py:279
  15.6 1.8 %collective-permute-start.3 = (bf16[256,256]{1,0:T(8,128)(2,1)S(1)}, bf16[256,256]{1,0:T(8,128)(2,1)S(1)}, u32[]{:S(2)}, u32[]{:S(2)}) collective-permute-start(bf16[256,256]{1,0:T(8,128)(2,1)S(1)} %get-tuple-element.44), channel_id=1, source_target_pairs={{0,4},{1,5},{2,6},{3,7},{4,0},{5,1},{6,2},{7,3},{8,12},{9,13},{10,... | collective-permute-start | bytes 393224 | tf_op jit(solution)/shard_map/ppermute | solution.py:279
  17.4 0.0 collective-permute-done.11.refs_0_.refs_13_
  17.4 1.6 %collective-permute-start.9 = (bf16[256,256]{1,0:T(8,128)(2,1)S(1)}, bf16[256,256]{1,0:T(8,128)(2,1)S(1)}, u32[]{:S(2)}, u32[]{:S(2)}) collective-permute-start(bf16[256,256]{1,0:T(8,128)(2,1)S(1)} %get-tuple-element.54), channel_id=1, source_target_pairs={{0,10},{1,11},{2,8},{3,9},{4,14},{5,15},{6,12},{7,13},{8,2},{9,3},... | collective-permute-start | bytes 393224 | tf_op jit(solution)/shard_map/ppermute | solution.py:279
  18.9 0.0 collective-permute-done.1.refs_2_
  18.9 1.1 %collective-permute-start.13 = (bf16[256,128]{1,0:T(8,128)(2,1)S(1)}, bf16[256,128]{1,0:T(8,128)(2,1)S(1)}, u32[]{:S(2)}, u32[]{:S(2)}) collective-permute-start(bf16[256,128]{1,0:T(8,128)(2,1)S(1)} %get-tuple-element.60), channel_id=1, source_target_pairs={{0,14},{1,15},{2,12},{3,13},{4,10},{5,11},{6,8},{7,9},{8,6},{9,7},... | collective-permute-start | bytes 196616 | tf_op jit(solution)/shard_map/ppermute | solution.py:279
  20.0 0.0 collective-permute-done.2.refs_3_
  20.0 0.9 %collective-permute-start.14 = (bf16[256,128]{1,0:T(8,128)(2,1)S(1)}, bf16[256,128]{1,0:T(8,128)(2,1)S(1)}, u32[]{:S(2)}, u32[]{:S(2)}) collective-permute-start(bf16[256,128]{1,0:T(8,128)(2,1)S(1)} %get-tuple-element.61), channel_id=1, source_target_pairs={{0,15},{1,14},{2,13},{3,12},{4,11},{5,10},{6,9},{7,8},{8,7},{9,6},... | collective-permute-start | bytes 196616 | tf_op jit(solution)/shard_map/ppermute | solution.py:279
  20.9 0.0 collective-permute-done.8.refs_9_
  20.9 1.1 %collective-permute-start.12 = (bf16[256,256]{1,0:T(8,128)(2,1)S(1)}, bf16[256,256]{1,0:T(8,128)(2,1)S(1)}, u32[]{:S(2)}, u32[]{:S(2)}) collective-permute-start(bf16[256,256]{1,0:T(8,128)(2,1)S(1)} %get-tuple-element.59), channel_id=1, source_target_pairs={{0,12},{1,13},{2,14},{3,15},{4,8},{5,9},{6,10},{7,11},{8,4},{9,5},... | collective-permute-start | bytes 393224 | tf_op jit(solution)/shard_map/ppermute | solution.py:279
  22.0 1.7 %collective-permute-done.3.refs_4_ = bf16[256,256]{1,0:T(8,128)(2,1)S(1)} collective-permute-done((bf16[256,256]{1,0:T(8,128)(2,1)S(1)}, bf16[256,256]{1,0:T(8,128)(2,1)S(1)}, u32[]{:S(2)}, u32[]{:S(2)}) %collective-permute-start.3) | collective-permute-done | bytes 131104 | tf_op jit(solution)/shard_map/ppermute | solution.py:279
  23.7 2.2 %collective-permute-start.4 = (bf16[256,256]{1,0:T(8,128)(2,1)S(1)}, bf16[256,256]{1,0:T(8,128)(2,1)S(1)}, u32[]{:S(2)}, u32[]{:S(2)}) collective-permute-start(bf16[256,256]{1,0:T(8,128)(2,1)S(1)} %get-tuple-element.46), channel_id=1, source_target_pairs={{0,5},{1,4},{2,7},{3,6},{4,1},{5,0},{6,3},{7,2},{8,13},{9,12},{10,... | collective-permute-start | bytes 393224 | tf_op jit(solution)/shard_map/ppermute | solution.py:279
  25.9 8.2 %collective-permute-done.13.refs_1_.refs_15_ = bf16[256,128]{1,0:T(8,128)(2,1)S(1)} collective-permute-done((bf16[256,128]{1,0:T(8,128)(2,1)S(1)}, bf16[256,128]{1,0:T(8,128)(2,1)S(1)}, u32[]{:S(2)}, u32[]{:S(2)}) %collective-permute-start.13) | collective-permute-done | bytes 65568 | tf_op jit(solution)/shard_map/ppermute | solution.py:279
  34.1 0.0 collective-permute-start.5
  34.1 0.1 collective-permute-done.14.refs_2_.refs_17_
  34.2 1.6 %collective-permute-start.10 = (bf16[256,256]{1,0:T(8,128)(2,1)S(1)}, bf16[256,256]{1,0:T(8,128)(2,1)S(1)}, u32[]{:S(2)}, u32[]{:S(2)}) collective-permute-start(bf16[256,256]{1,0:T(8,128)(2,1)S(1)} %get-tuple-element.56), channel_id=1, source_target_pairs={{0,11},{1,10},{2,9},{3,8},{4,15},{5,14},{6,13},{7,12},{8,3},{9,2},... | collective-permute-start | bytes 393224 | tf_op jit(solution)/shard_map/ppermute | solution.py:279
  35.8 0.0 collective-permute-done.9.refs_10_
  35.8 2.5 %collective-permute-start.6 = (bf16[256,256]{1,0:T(8,128)(2,1)S(1)}, bf16[256,256]{1,0:T(8,128)(2,1)S(1)}, u32[]{:S(2)}, u32[]{:S(2)}) collective-permute-start(bf16[256,256]{1,0:T(8,128)(2,1)S(1)} %get-tuple-element.50), channel_id=1, source_target_pairs={{0,7},{1,6},{2,5},{3,4},{4,3},{5,2},{6,1},{7,0},{8,15},{9,14},{10,... | collective-permute-start | bytes 393224 | tf_op jit(solution)/shard_map/ppermute | solution.py:279
  38.9 0.0 collective-permute-done.12.refs_12_
  38.9 0.9 %collective-permute-start.15 = (bf16[256,128]{1,0:T(8,128)(2,1)S(1)}, bf16[256,128]{1,0:T(8,128)(2,1)S(1)}, u32[]{:S(2)}, u32[]{:S(2)}) collective-permute-start(bf16[256,128]{1,0:T(8,128)(2,1)S(1)} %get-tuple-element.66), channel_id=1, source_target_pairs={{0,13},{1,12},{2,15},{3,14},{4,9},{5,8},{6,11},{7,10},{8,5},{9,4},... | collective-permute-start | bytes 196616 | tf_op jit(solution)/shard_map/ppermute | solution.py:279
  39.7 0.0 collective-permute-done.4.refs_5_
  39.7 2.1 %collective-permute-start.16 = (bf16[256,128]{1,0:T(8,128)(2,1)S(1)}, bf16[256,128]{1,0:T(8,128)(2,1)S(1)}, u32[]{:S(2)}, u32[]{:S(2)}) collective-permute-start(bf16[256,128]{1,0:T(8,128)(2,1)S(1)} %get-tuple-element.68), channel_id=1, source_target_pairs={{0,14},{1,15},{2,12},{3,13},{4,10},{5,11},{6,8},{7,9},{8,6},{9,7},... | collective-permute-start | bytes 196616 | tf_op jit(solution)/shard_map/ppermute | solution.py:279
  41.8 0.0 collective-permute-done.5.refs_6_
  41.8 0.7 %collective-permute-start.17 = (bf16[256,128]{1,0:T(8,128)(2,1)S(1)}, bf16[256,128]{1,0:T(8,128)(2,1)S(1)}, u32[]{:S(2)}, u32[]{:S(2)}) collective-permute-start(bf16[256,128]{1,0:T(8,128)(2,1)S(1)} %get-tuple-element.70), channel_id=1, source_target_pairs={{0,15},{1,14},{2,13},{3,12},{4,11},{5,10},{6,9},{7,8},{8,7},{9,6},... | collective-permute-start | bytes 196616 | tf_op jit(solution)/shard_map/ppermute | solution.py:279
  42.5 0.0 collective-permute-done.10.refs_11_
  42.5 2.8 %collective-permute-done.6.refs_7_ = bf16[256,256]{1,0:T(8,128)(2,1)S(1)} collective-permute-done((bf16[256,256]{1,0:T(8,128)(2,1)S(1)}, bf16[256,256]{1,0:T(8,128)(2,1)S(1)}, u32[]{:S(2)}, u32[]{:S(2)}) %collective-permute-start.6) | collective-permute-done | bytes 131104 | tf_op jit(solution)/shard_map/ppermute | solution.py:279
  45.3 1.2 %shard_map.51.gram = f32[256,256]{1,0:T(8,128)S(1)} custom-call(s32[1,16]{1,0:T(1,128)S(1)} %bitcast.2, bf16[256,256]{1,0:T(8,128)(2,1)S(1)} %get-tuple-element.39.refs_0_, bf16[256,256]{1,0:T(8,128)(2,1)S(1)} %collective-permute-done.refs_1_, bf16[256,256]{1,0:T(8,128)(2,1)S(1)} %collective-permute-done.1.refs_2_, ...), custom_call_target="tpu_custom_call" | custom-call | flops 536870912 | bytes 2097152 | tf_op jit(solution)/shard_map/pallas_call | solution.py:281
  46.5 3.5 %shard_map.52 = (f32[128,128]{1,0:T(8,128)S(1)}, f32[128,128]{1,0:T(8,128)S(1)}, f32[128,128]{1,0:T(8,128)S(1)}) custom-call(s32[1,16]{1,0:T(1,128)S(1)} %bitcast.3, s32[1,1]{1,0:T(1,128)S(6)} %copy.5.size, f32[256,256]{1,0:T(8,128)S(1)} %shard_map.51.gram, bf16[256,128]{1,0:T(8,128)(2,1)S(1)} %collective-permute-done.11.refs_0_.refs_13_, ...), custom_call_target="tpu_custom_call" | custom-call | tf_op jit(solution)/shard_map/pallas_call | solution.py:290
  50.0 0.6 collective-permute-start.18
  50.6 0.0 collective-permute-done.15.refs_3_.refs_14_
  50.6 1.6 %collective-permute-done.16.refs_4_.refs_16_ = bf16[256,128]{1,0:T(8,128)(2,1)S(1)} collective-permute-done((bf16[256,128]{1,0:T(8,128)(2,1)S(1)}, bf16[256,128]{1,0:T(8,128)(2,1)S(1)}, u32[]{:S(2)}, u32[]{:S(2)}) %collective-permute-start.16) | collective-permute-done | bytes 65568 | tf_op jit(solution)/shard_map/ppermute | solution.py:279
  52.2 0.3 collective-permute-done.17.refs_5_.refs_18_
  52.5 4.2 %shard_map.53 = (f32[256,256]{1,0:T(8,128)S(1)}, f32[128,256]{1,0:T(8,128)S(1)}, f32[128,128]{1,0:T(8,128)S(1)}) custom-call(s32[1,16]{1,0:T(1,128)S(1)} %bitcast.4, s32[1,1]{1,0:T(1,128)S(6)} %copy.5.size, f32[256,256]{1,0:T(8,128)S(1)} %shard_map.51.gram, f32[128,128]{1,0:T(8,128)S(1)} %get-tuple-element.62.r_lead, ...), custom_call_target="tpu_custom_call" | custom-call | tf_op jit(solution)/shard_map/pallas_call | solution.py:304
  56.7 0.0 collective-permute-done.18.lead
  56.7 0.6 collective-permute-start.19
  57.3 3.2 %shard_map.54 = bf16[1,4096,256]{2,1,0:T(8,128)(2,1)} custom-call(s32[1,16]{1,0:T(1,128)S(1)} %bitcast.5, s32[1,1]{1,0:T(1,128)S(6)} %copy.5.size, f32[256,256]{1,0:T(8,128)S(1)} %get-tuple-element.71.factor.own, f32[128,128]{1,0:T(8,128)S(1)} %get-tuple-element.64.inverse_lead.lead, f32[128,128]{1,0:T(8,128)S(1)} %get-tuple-element.72.trail, ...), custom_call_target="tpu_custom_call" | custom-call | flops 1073741824 | bytes 4194304 | tf_op jit(solution)/shard_map/pallas_call | solution.py:314
  60.5 2.1 %collective-permute-done.19.rest = f32[128,256]{1,0:T(8,128)S(1)} collective-permute-done((f32[128,256]{1,0:T(8,128)S(1)}, f32[128,256]{1,0:T(8,128)S(1)}, u32[]{:S(2)}, u32[]{:S(2)}) %collective-permute-start.19) | collective-permute-done | bytes 131104 | tf_op jit(solution)/shard_map/ppermute | solution.py:301
  62.5 0.9 %shard_map.55 = f32[256,256]{1,0:T(8,128)} custom-call(f32[256,256]{1,0:T(8,128)S(1)} %get-tuple-element.71.factor.own, f32[128,128]{1,0:T(8,128)S(1)} %collective-permute-done.18.lead, f32[128,256]{1,0:T(8,128)S(1)} %collective-permute-done.19.rest), custom_call_target="tpu_custom_call" | custom-call | tf_op jit(solution)/shard_map/pallas_call | solution.py:333
  (2 shorter events, 0.0 us)
Async XLA Ops:
  0.6 1.6 %copy-start = (bf16[1,256,4096]{2,1,0:T(8,128)(2,1)S(1)}, bf16[1,256,4096]{2,1,0:T(8,128)(2,1)}, u32[]{:S(2)}) copy-start(bf16[1,256,4096]{2,1,0:T(8,128)(2,1)} %src.1) | copy-start | bytes 6291460
  2.2 43.1 %copy-start.1 = (s32[1,1,16]{2,1,0:T(1,128)S(1)}, s32[1,1,16]{2,1,0:T(1,128)}, u32[]{:S(2)}) copy-start(s32[1,1,16]{2,1,0:T(1,128)} %param.4) | copy-start | bytes 196
  2.6 4.3 %collective-permute-start = (bf16[256,256]{1,0:T(8,128)(2,1)S(1)}, bf16[256,256]{1,0:T(8,128)(2,1)S(1)}, u32[]{:S(2)}, u32[]{:S(2)}) collective-permute-start(bf16[256,256]{1,0:T(8,128)(2,1)S(1)} %get-tuple-element.40), channel_id=1, source_target_pairs={{0,1},{1,0},{2,3},{3,2},{4,5},{5,4},{6,7},{7,6},{8,9},{9,8},{10,11... | collective-permute-start | bytes 393224 | tf_op jit(solution)/shard_map/ppermute | solution.py:279
  2.6 13.0 %collective-permute-start.7 = (bf16[256,256]{1,0:T(8,128)(2,1)S(1)}, bf16[256,256]{1,0:T(8,128)(2,1)S(1)}, u32[]{:S(2)}, u32[]{:S(2)}) collective-permute-start(bf16[256,256]{1,0:T(8,128)(2,1)S(1)} %get-tuple-element.51), channel_id=1, source_target_pairs={{0,8},{1,9},{2,10},{3,11},{4,12},{5,13},{6,14},{7,15},{8,0},{9,1},... | collective-permute-start | bytes 393224 | tf_op jit(solution)/shard_map/ppermute | solution.py:279
  5.3 13.7 %collective-permute-start.1 = (bf16[256,256]{1,0:T(8,128)(2,1)S(1)}, bf16[256,256]{1,0:T(8,128)(2,1)S(1)}, u32[]{:S(2)}, u32[]{:S(2)}) collective-permute-start(bf16[256,256]{1,0:T(8,128)(2,1)S(1)} %get-tuple-element.41), channel_id=1, source_target_pairs={{0,2},{1,3},{2,0},{3,1},{4,6},{5,7},{6,4},{7,5},{8,10},{9,11},{10,... | collective-permute-start | bytes 393224 | tf_op jit(solution)/shard_map/ppermute | solution.py:279
  5.8 14.2 %collective-permute-start.2 = (bf16[256,256]{1,0:T(8,128)(2,1)S(1)}, bf16[256,256]{1,0:T(8,128)(2,1)S(1)}, u32[]{:S(2)}, u32[]{:S(2)}) collective-permute-start(bf16[256,256]{1,0:T(8,128)(2,1)S(1)} %get-tuple-element.42), channel_id=1, source_target_pairs={{0,3},{1,2},{2,1},{3,0},{4,7},{5,6},{6,5},{7,4},{8,11},{9,10},{10,... | collective-permute-start | bytes 393224 | tf_op jit(solution)/shard_map/ppermute | solution.py:279
  6.8 10.6 %collective-permute-start.11 = (bf16[256,128]{1,0:T(8,128)(2,1)S(1)}, bf16[256,128]{1,0:T(8,128)(2,1)S(1)}, u32[]{:S(2)}, u32[]{:S(2)}) collective-permute-start(bf16[256,128]{1,0:T(8,128)(2,1)S(1)} %get-tuple-element.58), channel_id=1, source_target_pairs={{0,13},{1,12},{2,15},{3,14},{4,9},{5,8},{6,11},{7,10},{8,5},{9,4},... | collective-permute-start | bytes 196616 | tf_op jit(solution)/shard_map/ppermute | solution.py:279
  6.8 14.1 %collective-permute-start.8 = (bf16[256,256]{1,0:T(8,128)(2,1)S(1)}, bf16[256,256]{1,0:T(8,128)(2,1)S(1)}, u32[]{:S(2)}, u32[]{:S(2)}) collective-permute-start(bf16[256,256]{1,0:T(8,128)(2,1)S(1)} %get-tuple-element.52), channel_id=1, source_target_pairs={{0,9},{1,8},{2,11},{3,10},{4,13},{5,12},{6,15},{7,14},{8,1},{9,0},... | collective-permute-start | bytes 393224 | tf_op jit(solution)/shard_map/ppermute | solution.py:279
  15.6 8.1 %collective-permute-start.3 = (bf16[256,256]{1,0:T(8,128)(2,1)S(1)}, bf16[256,256]{1,0:T(8,128)(2,1)S(1)}, u32[]{:S(2)}, u32[]{:S(2)}) collective-permute-start(bf16[256,256]{1,0:T(8,128)(2,1)S(1)} %get-tuple-element.44), channel_id=1, source_target_pairs={{0,4},{1,5},{2,6},{3,7},{4,0},{5,1},{6,2},{7,3},{8,12},{9,13},{10,... | collective-permute-start | bytes 393224 | tf_op jit(solution)/shard_map/ppermute | solution.py:279
  17.4 18.4 %collective-permute-start.9 = (bf16[256,256]{1,0:T(8,128)(2,1)S(1)}, bf16[256,256]{1,0:T(8,128)(2,1)S(1)}, u32[]{:S(2)}, u32[]{:S(2)}) collective-permute-start(bf16[256,256]{1,0:T(8,128)(2,1)S(1)} %get-tuple-element.54), channel_id=1, source_target_pairs={{0,10},{1,11},{2,8},{3,9},{4,14},{5,15},{6,12},{7,13},{8,2},{9,3},... | collective-permute-start | bytes 393224 | tf_op jit(solution)/shard_map/ppermute | solution.py:279
  18.9 15.1 %collective-permute-start.13 = (bf16[256,128]{1,0:T(8,128)(2,1)S(1)}, bf16[256,128]{1,0:T(8,128)(2,1)S(1)}, u32[]{:S(2)}, u32[]{:S(2)}) collective-permute-start(bf16[256,128]{1,0:T(8,128)(2,1)S(1)} %get-tuple-element.60), channel_id=1, source_target_pairs={{0,14},{1,15},{2,12},{3,13},{4,10},{5,11},{6,8},{7,9},{8,6},{9,7},... | collective-permute-start | bytes 196616 | tf_op jit(solution)/shard_map/ppermute | solution.py:279
  20.0 14.2 %collective-permute-start.14 = (bf16[256,128]{1,0:T(8,128)(2,1)S(1)}, bf16[256,128]{1,0:T(8,128)(2,1)S(1)}, u32[]{:S(2)}, u32[]{:S(2)}) collective-permute-start(bf16[256,128]{1,0:T(8,128)(2,1)S(1)} %get-tuple-element.61), channel_id=1, source_target_pairs={{0,15},{1,14},{2,13},{3,12},{4,11},{5,10},{6,9},{7,8},{8,7},{9,6},... | collective-permute-start | bytes 196616 | tf_op jit(solution)/shard_map/ppermute | solution.py:279
  20.9 17.9 %collective-permute-start.12 = (bf16[256,256]{1,0:T(8,128)(2,1)S(1)}, bf16[256,256]{1,0:T(8,128)(2,1)S(1)}, u32[]{:S(2)}, u32[]{:S(2)}) collective-permute-start(bf16[256,256]{1,0:T(8,128)(2,1)S(1)} %get-tuple-element.59), channel_id=1, source_target_pairs={{0,12},{1,13},{2,14},{3,15},{4,8},{5,9},{6,10},{7,11},{8,4},{9,5},... | collective-permute-start | bytes 393224 | tf_op jit(solution)/shard_map/ppermute | solution.py:279
  23.7 16.0 %collective-permute-start.4 = (bf16[256,256]{1,0:T(8,128)(2,1)S(1)}, bf16[256,256]{1,0:T(8,128)(2,1)S(1)}, u32[]{:S(2)}, u32[]{:S(2)}) collective-permute-start(bf16[256,256]{1,0:T(8,128)(2,1)S(1)} %get-tuple-element.46), channel_id=1, source_target_pairs={{0,5},{1,4},{2,7},{3,6},{4,1},{5,0},{6,3},{7,2},{8,13},{9,12},{10,... | collective-permute-start | bytes 393224 | tf_op jit(solution)/shard_map/ppermute | solution.py:279
  34.1 7.8 %collective-permute-start.5 = (bf16[256,256]{1,0:T(8,128)(2,1)S(1)}, bf16[256,256]{1,0:T(8,128)(2,1)S(1)}, u32[]{:S(2)}, u32[]{:S(2)}) collective-permute-start(bf16[256,256]{1,0:T(8,128)(2,1)S(1)} %get-tuple-element.48), channel_id=1, source_target_pairs={{0,6},{1,7},{2,4},{3,5},{4,2},{5,3},{6,0},{7,1},{8,14},{9,15},{10,... | collective-permute-start | bytes 393224 | tf_op jit(solution)/shard_map/ppermute | solution.py:279
  34.2 8.3 %collective-permute-start.10 = (bf16[256,256]{1,0:T(8,128)(2,1)S(1)}, bf16[256,256]{1,0:T(8,128)(2,1)S(1)}, u32[]{:S(2)}, u32[]{:S(2)}) collective-permute-start(bf16[256,256]{1,0:T(8,128)(2,1)S(1)} %get-tuple-element.56), channel_id=1, source_target_pairs={{0,11},{1,10},{2,9},{3,8},{4,15},{5,14},{6,13},{7,12},{8,3},{9,2},... | collective-permute-start | bytes 393224 | tf_op jit(solution)/shard_map/ppermute | solution.py:279
  35.8 9.5 %collective-permute-start.6 = (bf16[256,256]{1,0:T(8,128)(2,1)S(1)}, bf16[256,256]{1,0:T(8,128)(2,1)S(1)}, u32[]{:S(2)}, u32[]{:S(2)}) collective-permute-start(bf16[256,256]{1,0:T(8,128)(2,1)S(1)} %get-tuple-element.50), channel_id=1, source_target_pairs={{0,7},{1,6},{2,5},{3,4},{4,3},{5,2},{6,1},{7,0},{8,15},{9,14},{10,... | collective-permute-start | bytes 393224 | tf_op jit(solution)/shard_map/ppermute | solution.py:279
  38.9 11.7 %collective-permute-start.15 = (bf16[256,128]{1,0:T(8,128)(2,1)S(1)}, bf16[256,128]{1,0:T(8,128)(2,1)S(1)}, u32[]{:S(2)}, u32[]{:S(2)}) collective-permute-start(bf16[256,128]{1,0:T(8,128)(2,1)S(1)} %get-tuple-element.66), channel_id=1, source_target_pairs={{0,13},{1,12},{2,15},{3,14},{4,9},{5,8},{6,11},{7,10},{8,5},{9,4},... | collective-permute-start | bytes 196616 | tf_op jit(solution)/shard_map/ppermute | solution.py:279
  39.7 12.4 %collective-permute-start.16 = (bf16[256,128]{1,0:T(8,128)(2,1)S(1)}, bf16[256,128]{1,0:T(8,128)(2,1)S(1)}, u32[]{:S(2)}, u32[]{:S(2)}) collective-permute-start(bf16[256,128]{1,0:T(8,128)(2,1)S(1)} %get-tuple-element.68), channel_id=1, source_target_pairs={{0,14},{1,15},{2,12},{3,13},{4,10},{5,11},{6,8},{7,9},{8,6},{9,7},... | collective-permute-start | bytes 196616 | tf_op jit(solution)/shard_map/ppermute | solution.py:279
  41.8 10.6 %collective-permute-start.17 = (bf16[256,128]{1,0:T(8,128)(2,1)S(1)}, bf16[256,128]{1,0:T(8,128)(2,1)S(1)}, u32[]{:S(2)}, u32[]{:S(2)}) collective-permute-start(bf16[256,128]{1,0:T(8,128)(2,1)S(1)} %get-tuple-element.70), channel_id=1, source_target_pairs={{0,15},{1,14},{2,13},{3,12},{4,11},{5,10},{6,9},{7,8},{8,7},{9,6},... | collective-permute-start | bytes 196616 | tf_op jit(solution)/shard_map/ppermute | solution.py:279
  50.0 6.7 %collective-permute-start.18 = (f32[128,128]{1,0:T(8,128)S(1)}, f32[128,128]{1,0:T(8,128)S(1)}, u32[]{:S(2)}, u32[]{:S(2)}) collective-permute-start(f32[128,128]{1,0:T(8,128)S(1)} %get-tuple-element.62.r_lead), channel_id=1, source_target_pairs={{0,16},{16,0},{1,17},{17,1},{2,18},{18,2},{3,19},{19,3},{4,20},{20... | collective-permute-start | bytes 196616 | tf_op jit(solution)/shard_map/ppermute | solution.py:301
  56.7 5.8 %collective-permute-start.19 = (f32[128,256]{1,0:T(8,128)S(1)}, f32[128,256]{1,0:T(8,128)S(1)}, u32[]{:S(2)}, u32[]{:S(2)}) collective-permute-start(f32[128,256]{1,0:T(8,128)S(1)} %get-tuple-element.75), channel_id=1, source_target_pairs={{0,16},{16,0},{1,17},{17,1},{2,18},{18,2},{3,19},{19,3},{4,20},{20... | collective-permute-start | bytes 393224 | tf_op jit(solution)/shard_map/ppermute | solution.py:301
